TPU v7x, 32 devices: a whole 2x2x4 slice. The times are simulated.
32 devices in a mesh: seq: 8 (over y, x, core), fsdp: 4 (over z).
Axes of the slice: x: 2, y: 2, z: 4, core: 2. Of those that a mesh axis runs over, the one named last changes fastest.
Arguments:
- tokens: bfloat16 [4, 8192, 1024], P('fsdp', 'seq'), may hold values from -6 to 6
- segment_ids: int32 [4, 8192], P('fsdp', 'seq'), may hold values from 0 to 2, as said below
- in_weight: bfloat16 [1024, 4384], P(('seq', 'fsdp')), may hold values from -0.1875 to 0.1875
- out_weight: bfloat16 [2048, 1024], P(('seq', 'fsdp')), may hold values from -0.125 to 0.125
- conv_weight: bfloat16 [4, 2304], P(None, ('seq', 'fsdp')), may hold values from -3 to 3
- conv_bias: bfloat16 [2304], P(('seq', 'fsdp')), may hold values from -0.5 to 0.5
- norm_gain: bfloat16 [1024], P(('seq', 'fsdp')), may hold values from 0.5 to 1.5
- gate_gain: bfloat16 [2048], P(('seq', 'fsdp')), may hold values from 0.5 to 1.5
- log_rate: float32 [32], replicated, may hold values from -11 to -1
- skip_gain: float32 [32], replicated, may hold values from 0.5 to 1.5
- step_bias: float32 [32], replicated, may hold values from -4 to -1
- cotangent: bfloat16 [4, 8192, 1024], P('fsdp', 'seq'), may hold values from -6 to 6
Outputs:
- block_out: bfloat16 [4, 8192, 1024], P('fsdp', 'seq')
- grad_tokens: float32 [4, 8192, 1024], P('fsdp', 'seq')
- grad_in_weight: float32 [1024, 4384], P(('seq', 'fsdp'))
- grad_out_weight: float32 [2048, 1024], P(('seq', 'fsdp'))
- grad_conv_weight: float32 [4, 2304], P(None, ('seq', 'fsdp'))
- grad_conv_bias: float32 [2304], P(('seq', 'fsdp'))
- grad_norm_gain: float32 [1024], P(('seq', 'fsdp'))
- grad_gate_gain: float32 [2048], P(('seq', 'fsdp'))
- grad_log_rate: float32 [32], replicated
- grad_skip_gain: float32 [32], replicated
- grad_step_bias: float32 [32], replicated
Inputs may be any that keep to these rules, and one draw needn't show every extreme that they name: `segment_ids`: in each row the number rises by one at exactly two positions, one inside the first block of 1024 positions and one inside the last, at an offset from 1 to 1021 within its block.
All inputs are finite; a program needn't handle non-finite values.
Results may differ from a plain program's by a relative error of at most 0.0082.
Values may be sent and summed in bfloat16 or wider, within the bound.
No kernel may reach another device: no remote copies, remote signals or barrier semaphores. Data moves between devices by JAX's collectives and lax.ppermute only.
A program may use at most 320 MiB of HBM per device.

v0:
```python
import jax
import jax.numpy as jnp
from jax import lax
from jax.sharding import PartitionSpec as P

HEADS = 32
HEADDIM = 64
STATE = 128
GROUP = 256


HIGH = lax.Precision.HIGHEST


def from_behind(block, axis, distance):
    devices = range(lax.axis_size(axis))
    route = [(i - distance, i) for i in devices if i - distance in devices]
    return lax.ppermute(block, axis, route)


def entering_2(x, axis, join, neutral):
    place = lax.axis_index(axis)
    gathered = jax.tree.map(
        lambda a, kind: lax.all_gather(a.astype(kind), axis), x, (jnp.bfloat16, jnp.bfloat16)
    )
    state = jax.tree.map(lambda a, e: jnp.zeros_like(a) + jnp.asarray(e, a.dtype), x, neutral)

    def one(step, state):
        return join(
            state,
            jax.tree.map(
                lambda a, own: lax.dynamic_index_in_dim(a, step, 0, False).astype(own.dtype),
                gathered,
                x,
            ),
        )

    return lax.fori_loop(0, place, one, state)


def prefix(x, axis, combine, identity):
    count, here = (lax.axis_size(axis), lax.axis_index(axis))
    everything = jax.tree.map(
        lambda part, kind: lax.all_gather(part.astype(kind), axis),
        x,
        jax.tree.map(lambda a: jnp.bfloat16 if a.dtype == jnp.float32 else a.dtype, x),
    )
    start = jax.tree.map(
        lambda part, zero: jnp.broadcast_to(jnp.asarray(zero, part.dtype), part.shape), x, identity
    )

    def step(k, before):
        at = count - 1 - k
        reached = at > here
        new = combine(
            before, jax.tree.map(lambda part, own: part[at].astype(own.dtype), everything, x)
        )
        return jax.tree.map(lambda a, b: jnp.where(reached, a, b), new, before)

    return lax.fori_loop(0, count, step, start)


def norm_scale(value, gain):
    return value * lax.rsqrt(jnp.mean(value * value, axis=-1, keepdims=True) + 1e-05) * gain


def link_states(earlier, later):
    return (later[0] * earlier[0], later[0][:, None, None] * earlier[1] + later[1])


def conv_local(conv_ext, label_ext, labels, conv_weight, conv_bias):
    kernel_len = conv_weight.shape[0]
    row_count = labels.shape[0]
    summed = conv_bias[None, :] + jnp.zeros((row_count, conv_ext.shape[1]), jnp.float32)
    for offset in range(kernel_len):
        keep_mask = (label_ext[offset : offset + row_count] == labels).astype(jnp.float32)
        summed = (
            summed
            + conv_weight[offset][None, :]
            * conv_ext[offset : offset + row_count]
            * keep_mask[:, None]
        )
    return jax.nn.silu(summed)


def prepare(conv_ext, raw_step, conv_weight, conv_bias, log_rate, step_bias, label_ext, labels):
    row_count = labels.shape[0]
    mixed = conv_local(conv_ext, label_ext, labels, conv_weight, conv_bias)
    inner_width = HEADS * HEADDIM
    values = mixed[:, :inner_width].reshape(row_count, HEADS, HEADDIM)
    keys_in = mixed[:, inner_width : inner_width + STATE]
    queries = mixed[:, inner_width + STATE :]
    step_size = jax.nn.softplus(raw_step + step_bias)
    decay_log = -jnp.exp(log_rate) * step_size
    return (values, keys_in, queries, step_size, decay_log)


def advance(memory, item):
    carry_factor, block_state = item
    return (carry_factor[:, None, None] * memory + block_state, memory)


def local_scan(values, keys_in, queries, step_size, decay_log, labels):
    row_count = labels.shape[0]
    blocks_count = row_count // GROUP
    block_values = values.reshape(blocks_count, GROUP, HEADS, HEADDIM)
    block_keys = keys_in.reshape(blocks_count, GROUP, STATE)
    block_queries = queries.reshape(blocks_count, GROUP, STATE)
    block_decay = decay_log.reshape(blocks_count, GROUP, HEADS).transpose(0, 2, 1)
    block_step = step_size.reshape(blocks_count, GROUP, HEADS).transpose(0, 2, 1)
    block_labels = labels.reshape(blocks_count, GROUP)
    running = jnp.cumsum(block_decay, axis=2)
    places = jnp.arange(GROUP)
    allowed = (places[:, None] >= places[None, :])[None] & (
        block_labels[:, :, None] == block_labels[:, None, :]
    )
    allowed_heads = allowed[:, None]
    differ = running[:, :, :, None] - running[:, :, None, :]
    factor = jnp.exp(jnp.where(allowed_heads, differ, 0.0)) * allowed_heads.astype(jnp.float32)
    scores = jnp.einsum("btn,bsn->bts", block_queries, block_keys, precision=HIGH)
    mixing = factor * scores[:, None] * block_step[:, :, None, :]
    output = jnp.einsum("bhts,bshp->bthp", mixing, block_values, precision=HIGH)
    previous_last = jnp.concatenate([block_labels[:1, 0], block_labels[:-1, -1]], axis=0)
    summed = running[:, :, -1]
    tail_same = (block_labels == block_labels[:, -1:]).astype(jnp.float32)
    weight_tail = jnp.exp(summed[:, :, None] - running) * tail_same[:, None, :] * block_step
    block_state = jnp.einsum(
        "bhs,bshp,bsn->bhpn", weight_tail, block_values, block_keys, precision=HIGH
    )
    carried = jnp.exp(summed) * (block_labels[:, -1] == previous_last).astype(jnp.float32)[:, None]
    final, states_in = lax.scan(
        advance, jnp.zeros((HEADS, HEADDIM, STATE), jnp.float32), (carried, block_state)
    )
    enter_block = (
        jnp.exp(running) * (block_labels == previous_last[:, None]).astype(jnp.float32)[:, None, :]
    )
    output = output + jnp.einsum(
        "bht,btn,bhpn->bthp", enter_block, block_queries, states_in, precision=HIGH
    )
    through = jnp.exp(jnp.sum(decay_log, axis=0)) * (labels[-1] == labels[0]).astype(jnp.float32)
    entering = (
        jnp.exp(jnp.cumsum(decay_log, axis=0)) * (labels == labels[0]).astype(jnp.float32)[:, None]
    )
    return (output.reshape(row_count, HEADS, HEADDIM), final, through, entering)


def finish(local_out, entering, queries, incoming, skip_gain, values):
    result = local_out + entering[:, :, None] * jnp.einsum(
        "tn,hpn->thp", queries, incoming, precision=HIGH
    )
    result = result + skip_gain[:, None] * values
    return result.reshape(result.shape[0], HEADS * HEADDIM)


def gate_norm(mixed_out, gate_part, gate_gain):
    return norm_scale(mixed_out * jax.nn.silu(gate_part), gate_gain)


def on_device(
    tokens,
    segment_ids,
    in_weight,
    out_weight,
    conv_weight,
    conv_bias,
    norm_gain,
    gate_gain,
    log_rate,
    skip_gain,
    step_bias,
    cotangent,
):
    in_full, out_full, conv_full, bias_full, norm_full, gate_full = (
        lax.all_gather(in_weight, ("seq", "fsdp"), axis=0, tiled=True),
        lax.all_gather(out_weight, ("seq", "fsdp"), axis=0, tiled=True),
        lax.all_gather(conv_weight, ("seq", "fsdp"), axis=1, tiled=True),
        lax.all_gather(conv_bias, ("seq", "fsdp"), axis=0, tiled=True),
        lax.all_gather(norm_gain, ("seq", "fsdp"), axis=0, tiled=True),
        lax.all_gather(gate_gain, ("seq", "fsdp"), axis=0, tiled=True),
    )
    inputs = tokens[0].astype(jnp.float32)
    labels = segment_ids[0]
    row_count = labels.shape[0]
    kernel_len = conv_full.shape[0]
    inner_width = out_full.shape[0]
    channels = conv_full.shape[1]
    hidden_low = norm_scale(inputs, norm_full.astype(jnp.float32)).astype(jnp.bfloat16)
    projected = jnp.dot(hidden_low, in_full, preferred_element_type=jnp.float32).astype(
        jnp.bfloat16
    )
    gate_part = projected[:, :inner_width].astype(jnp.float32)
    conv_in = projected[:, inner_width : inner_width + channels]
    raw_step = projected[:, inner_width + channels :].astype(jnp.float32)
    edge_rows = from_behind(conv_in[row_count - kernel_len + 1 :], "seq", 1)
    conv_ext = jnp.concatenate([edge_rows, conv_in], axis=0).astype(jnp.float32)
    label_ext = jnp.concatenate(
        [jnp.zeros((kernel_len - 1,), jnp.int32) + labels[0], labels], axis=0
    )
    values, keys_in, queries, step_size, decay_log = prepare(
        conv_ext,
        raw_step,
        conv_full.astype(jnp.float32),
        bias_full.astype(jnp.float32),
        log_rate,
        step_bias,
        label_ext,
        labels,
    )
    local_out, local_state, through, entering = local_scan(
        values, keys_in, queries, step_size, decay_log, labels
    )
    carried_in = entering_2(
        (through, local_state),
        "seq",
        link_states,
        (jnp.ones_like(through), jnp.zeros_like(local_state)),
    )
    incoming = carried_in[1]
    mixed_out = finish(local_out, entering, queries, incoming, skip_gain, values)
    normed_low = gate_norm(mixed_out, gate_part, gate_full.astype(jnp.float32)).astype(jnp.bfloat16)
    block_out = (inputs + jnp.dot(normed_low, out_full, preferred_element_type=jnp.float32)).astype(
        jnp.bfloat16
    )
    in_back, out_back, conv_back, bias_back, norm_back, gate_back = (
        lax.all_gather(in_weight, ("seq", "fsdp"), axis=0, tiled=True),
        lax.all_gather(out_weight, ("seq", "fsdp"), axis=0, tiled=True),
        lax.all_gather(conv_weight, ("seq", "fsdp"), axis=1, tiled=True),
        lax.all_gather(conv_bias, ("seq", "fsdp"), axis=0, tiled=True),
        lax.all_gather(norm_gain, ("seq", "fsdp"), axis=0, tiled=True),
        lax.all_gather(gate_gain, ("seq", "fsdp"), axis=0, tiled=True),
    )
    upstream = cotangent[0]
    grad_out_w = jnp.einsum("td,te->de", normed_low, upstream, preferred_element_type=jnp.float32)
    grad_normed = jnp.einsum("te,de->td", upstream, out_back, preferred_element_type=jnp.float32)
    ignored, pull_gate = jax.vjp(gate_norm, mixed_out, gate_part, gate_back.astype(jnp.float32))
    grad_mixed, grad_gate_part, grad_gate_gain = pull_gate(grad_normed)
    grad_heads = grad_mixed.reshape(row_count, HEADS, HEADDIM)
    local_adjoint = jnp.einsum("th,thp,tn->hpn", entering, grad_heads, queries, precision=HIGH)
    carried_back = prefix(
        (through, local_adjoint),
        "seq",
        link_states,
        (jnp.ones_like(through), jnp.zeros_like(local_adjoint)),
    )

    def core(
        conv_ext, raw_step, conv_values, bias_values, log_rate, skip_gain, step_bias, incoming
    ):
        values, keys_in, queries, step_size, decay_log = prepare(
            conv_ext, raw_step, conv_values, bias_values, log_rate, step_bias, label_ext, labels
        )
        local_out, local_state, through, entering = local_scan(
            values, keys_in, queries, step_size, decay_log, labels
        )
        result = finish(local_out, entering, queries, incoming, skip_gain, values)
        return (result, through[:, None, None] * incoming + local_state)

    ignored, pull_core = jax.vjp(
        core,
        conv_ext,
        raw_step,
        conv_back.astype(jnp.float32),
        bias_back.astype(jnp.float32),
        log_rate,
        skip_gain,
        step_bias,
        incoming,
    )
    (
        grad_ext,
        grad_raw_step,
        grad_conv_w,
        grad_conv_b,
        grad_log_rate,
        grad_skip,
        grad_step_bias,
        unused,
    ) = pull_core((grad_mixed, carried_back[1]))
    edge_grad = from_behind(grad_ext[: kernel_len - 1], "seq", -1)
    grad_conv_in = grad_ext[kernel_len - 1 :] + jnp.pad(
        edge_grad, ((row_count - kernel_len + 1, 0), (0, 0))
    )
    grad_projected = jnp.concatenate([grad_gate_part, grad_conv_in, grad_raw_step], axis=1).astype(
        jnp.bfloat16
    )
    grad_hidden = jnp.einsum(
        "tk,dk->td", grad_projected, in_back, preferred_element_type=jnp.float32
    )
    ignored, pull_norm = jax.vjp(norm_scale, inputs, norm_back.astype(jnp.float32))
    grad_inputs, grad_norm_gain = pull_norm(grad_hidden)
    grad_tokens = upstream.astype(jnp.float32) + grad_inputs
    grad_in_w = jnp.einsum(
        "td,tk->dk", hidden_low, grad_projected, preferred_element_type=jnp.float32
    )
    shards = (
        lax.psum_scatter(grad_in_w, ("seq", "fsdp"), scatter_dimension=0, tiled=True),
        lax.psum_scatter(grad_out_w, ("seq", "fsdp"), scatter_dimension=0, tiled=True),
        lax.psum_scatter(grad_conv_w, ("seq", "fsdp"), scatter_dimension=1, tiled=True),
        lax.psum_scatter(grad_conv_b, ("seq", "fsdp"), scatter_dimension=0, tiled=True),
        lax.psum_scatter(grad_norm_gain, ("seq", "fsdp"), scatter_dimension=0, tiled=True),
        lax.psum_scatter(grad_gate_gain, ("seq", "fsdp"), scatter_dimension=0, tiled=True),
    )
    in_shard, out_shard, conv_shard, bias_shard, norm_shard, gate_shard = shards
    head_sums = lax.psum((grad_log_rate, grad_skip, grad_step_bias), ("seq", "fsdp"))
    return (
        block_out[None],
        grad_tokens[None],
        in_shard,
        out_shard,
        conv_shard,
        bias_shard,
        norm_shard,
        gate_shard,
        head_sums[0],
        head_sums[1],
        head_sums[2],
    )


def solution(mesh):
    return jax.shard_map(
        on_device,
        mesh=mesh,
        in_specs=(
            P("fsdp", "seq", None),
            P("fsdp", "seq"),
            P(("seq", "fsdp"), None),
            P(("seq", "fsdp"), None),
            P(None, ("seq", "fsdp")),
            P(("seq", "fsdp")),
            P(("seq", "fsdp")),
            P(("seq", "fsdp")),
            P(),
            P(),
            P(),
            P("fsdp", "seq", None),
        ),
        out_specs=(
            P("fsdp", "seq", None),
            P("fsdp", "seq", None),
            P(("seq", "fsdp"), None),
            P(("seq", "fsdp"), None),
            P(None, ("seq", "fsdp")),
            P(("seq", "fsdp")),
            P(("seq", "fsdp")),
            P(("seq", "fsdp")),
            P(),
            P(),
            P(),
        ),
        check_vma=False,
    )
```

profile of v0, /device:TPU:0, one launch (start us, length us, event | category | flops | bytes accessed | tf_op | source)
XLA Modules:
  0.0 1249.8 jit_solution(18191845233786007264)
XLA Ops:
  13.0 42.9 %all-reduce.23 = (bf16[1024]{0:T(1024)(128)(2,1)S(1)}, bf16[2304]{0:T(1024)(128)(2,1)S(1)}, bf16[2048]{0:T(1024)(128)(2,1)S(1)}) all-reduce(bf16[1024]{0:T(1024)(128)(2,1)S(1)} %dynamic-update-slice.1, bf16[2304]{0:T(1024)(128)(2,1)S(1)} %dynamic-update-slice, ...), channel_id=1, replica_groups=mesh['seq'=8,'fsdp'=4] {'seq','fsdp'}, use_global_device_ids=true, to_apply=%add.15 | all-reduce | flops 5376 | bytes 21504
  55.9 66.9 %all-gather.3 = bf16[32,72,4]{1,2,0:T(4,128)(2,1)S(1)} all-gather(bf16[1,72,4]{1,2,0:T(4,128)(2,1)} %bitcast.372), channel_id=1, replica_groups=mesh['seq'=8,'fsdp'=4] {'seq','fsdp'}, dimensions={0}, use_global_device_ids=true | all-gather | bytes 19008 | tf_op jit(solution)/shard_map/all_gather | solution.py:176
  130.4 16.3 %convolution_convert_fusion = bf16[1024,4384]{0,1:T(8,128)(2,1)} fusion(bf16[1024,4384]{1,0:T(8,128)(2,1)} %all-gather.9.cloned.1.call-done, bf16[1,1024,1024]{2,1,0:T(8,128)(2,1)} %param.22, f32[1024]{0:T(1024)S(1)} %convert_element_type.173, f32[1024]{0:T(1024)S(1)} %fusion.139), kind=kOutput, calls=%fused_computation.52 | convolution fusion | flops 9202597888 | bytes 20062208 | tf_op jit(solution)/shard_map/dot_general | solution.py:188
  164.8 11.1 fusion.31
  183.4 10.8 reshape_reshape.3
  194.2 13.3 %fusion.54 = f32[4,32,64,128]{3,2,1,0:T(8,128)} fusion(f32[4,256,128,1]{2,1,3,0:T(8,128)S(1)} %copy.294, f32[4,256,32,64]{1,0,3,2:T(4,128)} %reshape_reshape.3, f32[4,256,32]{1,2,0:T(8,128)S(1)} %get-tuple-element.563), kind=kOutput, calls=%fused_computation.109 | convolution fusion | flops 3223322624 | bytes 13238272 | tf_op jit(solution)/shard_map/bhs,bshp,bsn->bhpn/dot_general | solution.py:127
  236.9 12.0 all-reduce.16
  262.9 42.2 %fusion.45 = f32[4,32,8,8,256]{4,3,2,1,0:T(8,128)S(1)} fusion(f32[4,256,32,64]{1,3,2,0:T(8,128)S(1)} %fusion.157, f32[4,256,32]{1,2,0:T(8,128)S(1)} %get-tuple-element.562, f32[4,32,256]{2,1,0:T(8,128)S(1)} %bitcast.365, f32[4,256,256]{2,1,0:T(8,128)S(1)} %fusion.156, f32[4,256,256]{2,1,0:T(8,128)S(1)} %copy-done.25, f32[4,32,256]{2,1,0:T(8,128)S(1)} %copy-done.31, ...), kind=kOutput, calls=%fused_computation.85 | convolution fusion | flops 6488588288 | bytes 27918336 | tf_op jit(solution)/shard_map/bhts,bshp->bthp/dot_general | solution.py:122
  311.9 12.2 while.77
  324.1 10.8 convolution_bitcast_fusion
  335.0 14.6 %multiply_add_fusion.2 = (f32[1024,32,64]{0,2,1:T(8,128)S(1)}, f32[1024,32,64]{0,2,1:T(8,128)}) fusion(f32[1024,32,64]{0,2,1:T(8,128)} %bitcast.336, f32[1024,32,64]{0,2,1:T(8,128)} %bitcast.337, f32[32]{0:T(128)S(1)} %copy-done.85, f32[1024,32]{0,1:T(8,128)S(1)} %fusion.120, f32[32,64,128]{2,1,0:T(8,128)S(1)} %get-tuple-element.392, ...), kind=kOutput, calls=%fused_computation.100 | convolution fusion | flops 3229614080 | bytes 35258496 | tf_op jit(solution)/shard_map/tn,hpn->thp/dot_general | solution.py:148
  358.5 12.0 multiply_reduce_fusion.9
  370.5 13.1 %multiply_reduce_fusion.8 = (f32[2048]{0:T(1024)}, f32[1024,2048]{0,1:T(8,128)}, bf16[1024,2048]{0,1:T(8,128)(2,1)}) fusion(f32[1024,2304]{0,1:T(8,128)} %copy-done.1, bf16[1024,4384]{0,1:T(8,128)(2,1)} %convolution_convert_fusion, f32[1024,2048]{0,1:T(8,128)S(1)} %copy-done.8, f32[1024]{0:T(1024)S(1)} %multiply_multiply_fusion.5, f32[1024]{0:T(1024)S(1)} %fusion.140, ...), kind=kLoop, calls=%fused_computation.93 | loop fusion | flops 44038144 | bytes 50356224 | tf_op jit(solution)/shard_map/transpose(jvp())/reduce_sum | solution.py:151
  412.2 40.0 %reduce-window.34 = f32[32,8,128]{2,1,0:T(8,128)S(1)} reduce-window(f32[32,8,128]{2,1,0:T(8,128)S(1)} %bitcast.360, f32[]{:T(128)} %constant.178.clone.1), window={size=1x1x128 pad=0_0x0_0x0_127}, to_apply=%region_22.23 | reduce-window | flops 4161536 | bytes 262148 | tf_op jit(solution)/shard_map/reduce-window.4
  452.5 17.7 %fusion.104 = f32[4,256,128]{2,1,0:T(8,128)S(1)} fusion(f32[4,32,64,128]{3,2,1,0:T(8,128)} %get-tuple-element.863, f32[4,256,32,64]{1,0,3,2:T(4,128)} %reshape.378, f32[4,256,32]{1,2,0:T(8,128)S(1)} %get-tuple-element.562), kind=kOutput, calls=%fused_computation.151 | convolution fusion | flops 3223322624 | bytes 13238272 | tf_op jit(solution)/shard_map/transpose(jvp(bht,btn,bhpn->bthp))/dot_general | solution.py:137
  470.2 64.5 %fusion.13 = (f32[4,32,256]{2,1,0:T(8,128)}, f32[4,32,256]{2,1,0:T(8,128)}, f32[4,32,256]{2,1,0:T(8,128)}, f32[4,256,256]{2,1,0:T(8,128)S(1)}) fusion(f32[4,32,256]{2,1,0:T(8,128)} %bitcast.363, f32[4,256,256]{2,1,0:T(8,128)S(1)} %copy-done.28, f32[4,256,256]{2,1,0:T(8,128)S(1)} %copy-done.26, f32[4,32,256]{2,1,0:T(8,128)} %copy-done.30, ...), kind=kOutput, calls=%fused_computation.30 | convolution fusion | flops 6567919616 | bytes 20840448 | tf_op jit(solution)/shard_map/transpose(jvp(bhts,bshp->bthp))/dot_general | solution.py:122
  545.1 13.3 %fusion.41 = f32[4,32,64,128]{3,2,1,0:T(8,128)} fusion(f32[4,256,128,1]{2,1,3,0:T(8,128)S(1)} %copy.295, f32[4,256,32,64]{1,0,3,2:T(4,128)} %reshape.378, f32[4,256,32]{1,2,0:T(8,128)S(1)} %get-tuple-element.562), kind=kOutput, calls=%fused_computation.78 | convolution fusion | flops 3223322624 | bytes 13238272 | tf_op jit(solution)/shard_map/transpose(jvp(bht,btn,bhpn->bthp))/dot_general | solution.py:137
  558.4 14.6 %multiply_reduce_fusion.6 = f32[4,32,256]{2,0,1:T(4,128)S(1)} fusion(f32[4,32,256,64]{2,3,1,0:T(8,128)} %convolution_bitcast_fusion, f32[4,256,32,64]{1,0,3,2:T(4,128)} %reshape.378), kind=kLoop, calls=%fused_computation.91 | loop fusion | flops 4161536 | bytes 16908288
  584.5 16.3 %while.78 = (s32[]{:T(128)}, f32[32,64,128]{2,1,0:T(8,128)S(1)}, s32[]{:T(128)}, bf16[8,32]{1,0:T(8,128)(2,1)}, bf16[8,32,64,128]{3,2,1,0:T(8,128)(2,1)}, /*index=5*/s32[]{:T(128)}, s32[]{:T(128)}, s32[]{:T(128)}, s32[]{:T(128)}) while((s32[]{:T(128)}, f32[32,64,128]{2,1,0:T(8,128)S(1)}, s32[]{:T(128)}, ...), condition=%wide.region_16.17_spmd.clone, body=%wide.region_15.16_spmd.clone.sunk | while | flops 1310760 | bytes 2621935 | solution.py:60
  603.4 15.1 %while.75 = (s32[]{:T(128)}, f32[32,64,128]{2,1,0:T(8,128)S(1)}, f32[4,32]{1,0:T(4,128)S(1)}, f32[4,32,64,128]{3,2,1,0:T(8,128)}, f32[4,32,64,128]{3,2,1,0:T(8,1...) while((s32[]{:T(128)}, f32[32,64,128]{2,1,0:T(8,128)S(1)}, ...), condition=%wide.region_19.20_spmd, body=%wide.region_17.19_spmd.sunk | while | flops 1048547 | bytes 6292361 | solution.py:131
  618.6 14.9 %multiply_reduce_fusion.7 = (f32[4,32,256]{2,1,0:T(8,128)S(1)}, f32[4,256,32,64]{1,3,2,0:T(8,128)}) fusion(f32[4,32,256,64]{2,0,3,1:T(4,128)} %bitcast.333, f32[4,256,128,1]{2,1,3,0:T(8,128)} %copy-done.16, f32[4,32,64,128]{3,2,1,0:T(8,128)} %get-tuple-element.396), kind=kOutput, calls=%fused_computation.92 | convolution fusion | flops 3225387008 | bytes 21626880 | tf_op jit(solution)/shard_map/transpose(jvp(bhs,bshp,bsn->bhpn))/dot_general | solution.py:127
  645.4 34.8 %bitcast_add_fusion.3 = f32[4,256,32,64]{1,3,2,0:T(8,128)} fusion(f32[4,256,32,64]{1,3,2,0:T(8,128)} %get-tuple-element.578, f32[4,256,32]{1,2,0:T(8,128)S(1)} %copy-done.24, f32[4,32,256]{2,1,0:T(8,128)} %bitcast.364, f32[4,256,256]{2,1,0:T(8,128)} %copy-done.27, f32[4,256,256]{2,1,0:T(8,128)} %get-tuple-element.565, f32[4,32,256]{2,1,0:T(8,128)S(1)} %copy-done.32, ...), kind=kOutput, calls=%fused_computation.74 | convolution fusion | flops 6488588288 | bytes 27918336 | tf_op jit(solution)/shard_map/transpose(jvp(bhts,bshp->bthp))/dot_general | solution.py:122
  680.2 14.0 %copy.280 = f32[4,256,32,64]{1,0,3,2:T(4,128)} copy(f32[4,256,32,64]{1,3,2,0:T(8,128)} %bitcast_add_fusion.3) | data formatting | bytes 16777216 | tf_op jit(solution)/shard_map/transpose(jvp(bhts,bshp->bthp))/add_any | solution.py:122
  703.3 13.9 %fusion.101 = f32[4,256,128]{2,1,0:T(8,128)S(1)} fusion(f32[4,32,64,128]{3,2,1,0:T(8,128)S(1)} %copy-done.7, f32[4,256,32,64]{1,0,3,2:T(4,128)S(1)} %bitcast.335, f32[4,256,32]{1,2,0:T(8,128)S(1)} %copy-done.24), kind=kOutput, calls=%fused_computation.150 | convolution fusion | flops 3223322624 | bytes 13238272 | tf_op jit(solution)/shard_map/transpose(jvp(bhs,bshp,bsn->bhpn))/dot_general | solution.py:127
  729.7 28.6 %multiply_reduce_fusion.5 = (f32[2304]{0:T(1024)S(1)}, f32[2304]{0:T(1024)}, f32[2304]{0:T(1024)}, f32[2304]{0:T(1024)}, f32[2304]{0:T(1024)}, /*index=5*/f32[1024,2304]{0,1:T(8,128)}) fusion(f32[1027,2304]{0,1:T(8,128)} %copy-done, f32[1024]{0:T(1024)S(1)} %copy-done.52, f32[1024]{0:T(1024)S(1)} %copy-done.54, f32[1024]{0:T(1024)S(1)} %copy-done.56, ...), kind=kLoop, calls=%fused_computation.60 | loop fusion | flops 54252288 | bytes 66118656 | tf_op jit(solution)/shard_map/transpose(jvp())/reduce_sum | solution.py:79
  758.3 11.0 broadcast_multiply_fusion
  782.5 19.7 %pad_add_fusion = f32[1027,2304]{0,1:T(8,128)} fusion(f32[1024,2304]{0,1:T(8,128)} %copy-done.3, f32[1024,2304]{0,1:T(8,128)} %get-tuple-element.554, f32[1024,2304]{0,1:T(8,128)} %get-tuple-element.555, f32[1024,2304]{0,1:T(8,128)} %copy-done.2), kind=kLoop, calls=%fused_computation.51 | loop fusion | flops 7098624 | bytes 47213568 | tf_op jit(solution)/shard_map/transpose(jvp())/add_any | solution.py:80
  814.1 18.1 %fusion.88 = f32[1024,4384]{1,0:T(8,128)} fusion(bf16[1024,32]{0,1:T(8,128)(2,1)S(1)} %copy-done.57, bf16[1024,2304]{0,1:T(8,128)(2,1)} %fusion.30, bf16[1024,2048]{0,1:T(8,128)(2,1)} %get-tuple-element.551, bf16[1,1024,1024]{2,1,0:T(8,128)(2,1)S(1)} %copy-done.9, f32[1024]{0:T(1024)S(1)} %copy-done.72, f32[1024]{0:T(1024)S(1)} %copy-done.74), kind=kOutput, calls=%fused_computation.138 | convolution fusion | flops 9225043968 | bytes 29040640 | tf_op jit(solution)/shard_map/td,tk->dk/dot_general | solution.py:292
  833.2 10.7 fusion.90
  844.2 16.9 %fusion.67 = (f32[1024]{0:T(1024)S(1)}, f32[1024]{0:T(1024)S(1)}, f32[1024,1024]{1,0:T(8,128)}) fusion(bf16[1,1024,1024]{2,1,0:T(8,128)(2,1)S(1)} %copy-done.9, f32[1024]{0:T(1024)S(1)} %copy-done.74, f32[1024]{0:T(1024)S(1)} %copy-done.72, bf16[1024,4384]{1,0:T(8,128)(2,1)} %all-gather.9.cloned.1.call-done, bf16[1024,32]{0,1:T(8,128)(2,1)S(1)} %copy-done.57, ...), kind=kOutput, calls=%fused_computation.125 | convolution fusion | flops 9228187648 | bytes 24264704 | tf_op jit(solution)/shard_map/tk,dk->td/dot_general | solution.py:286
  861.0 57.1 %all-reduce.22 = (f32[4,2304]{1,0:T(4,128)S(1)}, f32[2304]{0:T(1024)S(1)}, f32[1024]{0:T(1024)S(1)}, f32[2048]{0:T(1024)S(1)}, f32[32]{0:T(128)}, /*index=5*/f32[32]{0:T(128)}, f32[32]{0:T(128)}) all-reduce(f32[4,2304]{1,0:T(4,128)S(1)} %pad_add_fusion.2, ...), channel_id=7, replica_groups=mesh['seq'=8,'fsdp'=4] {'seq','fsdp'}, use_global_device_ids=true, to_apply=%region_37.38.clone | all-reduce | flops 14688 | bytes 117504
  925.3 317.2 %reduce-scatter.4.cloned.1.call-done = f32[32,4384]{1,0:T(8,128)} async-done(((f32[1024,4384]{1,0:T(8,128)}), f32[32,4384]{1,0:T(8,128)}) %reduce-scatter.4.cloned.1.call-update) | async-done | bytes 561168 | tf_op jit(solution)/shard_map/reduce_scatter | solution.py:296
  (415 shorter events, 268.2 us)
Async XLA Ops:
  7.2 123.2 %all-gather.9.cloned.1.call-start = ((), (), s32[]{:S(2)}) async-start(), calls=%async_computation.2 | async-start | bytes 9461760 | tf_op jit(solution)/shard_map/all_gather | solution.py:174
  7.9 327.0 %all-gather.13.cloned.1.call-start = ((), (), s32[]{:S(2)}) async-start(), calls=%async_computation.6 | async-start | bytes 4718592 | tf_op jit(solution)/shard_map/all_gather | solution.py:24
  55.9 90.8 %copy-start.71 = (f32[1024]{0:T(1024)}, f32[1024]{0:T(1024)S(1)}, u32[]{:S(2)}) copy-start(f32[1024]{0:T(1024)S(1)} %convert_element_type.173) | copy-start | bytes 12292
  125.2 39.6 %copy-start.37 = (f32[2304]{0:T(1024)}, f32[2304]{0:T(1024)S(1)}, u32[]{:S(2)}) copy-start(f32[2304]{0:T(1024)S(1)} %get-tuple-element.468) | copy-start | bytes 27652
  125.2 39.6 %copy-start.39 = (f32[2304]{0:T(1024)}, f32[2304]{0:T(1024)S(1)}, u32[]{:S(2)}) copy-start(f32[2304]{0:T(1024)S(1)} %get-tuple-element.469) | copy-start | bytes 27652
  125.2 39.6 %copy-start.41 = (f32[2304]{0:T(1024)}, f32[2304]{0:T(1024)S(1)}, u32[]{:S(2)}) copy-start(f32[2304]{0:T(1024)S(1)} %get-tuple-element.470) | copy-start | bytes 27652
  125.2 39.6 %copy-start.43 = (f32[2304]{0:T(1024)}, f32[2304]{0:T(1024)S(1)}, u32[]{:S(2)}) copy-start(f32[2304]{0:T(1024)S(1)} %get-tuple-element.471) | copy-start | bytes 27652
  126.6 27.8 %copy-start.79 = (f32[4]{0:T(128)}, f32[4]{0:T(128)S(1)}, u32[]{:S(2)}) copy-start(f32[4]{0:T(128)S(1)} %fusion.141) | copy-start | bytes 52
  128.8 25.5 %copy-start.62 = (f32[4,256]{1,0:T(4,128)}, f32[4,256]{1,0:T(4,128)S(1)}, u32[]{:S(2)}) copy-start(f32[4,256]{1,0:T(4,128)S(1)} %get-tuple-element.572) | copy-start | bytes 12292
  130.4 34.4 %copy-start.51 = (f32[1024]{0:T(1024)}, f32[1024]{0:T(1024)S(1)}, u32[]{:S(2)}) copy-start(f32[1024]{0:T(1024)S(1)} %get-tuple-element.567) | copy-start | bytes 12292
  130.4 34.5 %copy-start.53 = (f32[1024]{0:T(1024)}, f32[1024]{0:T(1024)S(1)}, u32[]{:S(2)}) copy-start(f32[1024]{0:T(1024)S(1)} %get-tuple-element.568) | copy-start | bytes 12292
  130.4 34.5 %copy-start.55 = (f32[1024]{0:T(1024)}, f32[1024]{0:T(1024)S(1)}, u32[]{:S(2)}) copy-start(f32[1024]{0:T(1024)S(1)} %get-tuple-element.569) | copy-start | bytes 12292
  148.3 11.2 collective-permute-start
  150.7 75.7 %copy-start.19 = (f32[1024,32]{0,1:T(8,128)}, f32[1024,32]{0,1:T(8,128)S(1)}, u32[]{:S(2)}) copy-start(f32[1024,32]{0,1:T(8,128)S(1)} %get-tuple-element.559) | copy-start | bytes 393220
  150.7 85.9 %copy-start.86 = (f32[32]{0:T(128)}, f32[32]{0:T(128)S(1)}, u32[]{:S(2)}) copy-start(f32[32]{0:T(128)S(1)} %get-tuple-element.545) | copy-start | bytes 388
  154.4 39.8 %copy-start.23 = (f32[4,256,32]{1,2,0:T(8,128)}, f32[4,256,32]{1,2,0:T(8,128)S(1)}, u32[]{:S(2)}) copy-start(f32[4,256,32]{1,2,0:T(8,128)S(1)} %get-tuple-element.563) | copy-start | bytes 393220
  220.9 137.5 %all-gather.11.cloned.1.call-start = ((), (), s32[]{:S(2)}) async-start(), calls=%async_computation.3 | async-start | bytes 4325376 | tf_op jit(solution)/shard_map/all_gather | solution.py:175
  221.7 361.7 %all-gather.15.cloned.1.call-start = ((), (), s32[]{:S(2)}) async-start(), calls=%async_computation.7 | async-start | bytes 4718592 | tf_op jit(solution)/shard_map/all_gather | solution.py:44
  225.0 145.5 %copy-start.68 = (f32[2048]{0:T(1024)}, f32[2048]{0:T(1024)S(1)}, u32[]{:S(2)}) copy-start(f32[2048]{0:T(1024)S(1)} %convert_element_type.190) | copy-start | bytes 24580
  251.6 53.5 %copy-start.10 = (f32[4,256,128]{2,1,0:T(8,128)}, f32[4,256,128]{2,1,0:T(8,128)S(1)}, u32[]{:S(2)}) copy-start(f32[4,256,128]{2,1,0:T(8,128)S(1)} %copy.253) | copy-start | bytes 1572868
  404.0 521.3 %reduce-scatter.6.cloned.1.call-start = ((), (), s32[]{:S(2)}) async-start(), calls=%async_computation.5 | async-start | bytes 8650752 | tf_op jit(solution)/shard_map/reduce_scatter | solution.py:297
  412.1 58.0 %copy-start.26 = (f32[4,256,256]{2,1,0:T(8,128)S(1)}, f32[4,256,256]{2,1,0:T(8,128)}, u32[]{:S(2)}) copy-start(f32[4,256,256]{2,1,0:T(8,128)} %get-tuple-element.565) | copy-start | bytes 3145732
  470.2 64.5 %copy-start.13 = (f32[4,256,128]{2,1,0:T(8,128)S(1)}, f32[4,256,128]{2,1,0:T(8,128)}, u32[]{:S(2)}) copy-start(f32[4,256,128]{2,1,0:T(8,128)} %copy-done.12) | copy-start | bytes 1572868
  583.3 659.2 %reduce-scatter.4.cloned.1.call-start = ((), (), s32[]{:S(2)}) async-start(), calls=%async_computation.4 | async-start | bytes 18923520 | tf_op jit(solution)/shard_map/reduce_scatter | solution.py:296
  618.6 26.8 %copy-start.24 = (f32[4,256,32]{1,2,0:T(8,128)S(1)}, f32[4,256,32]{1,2,0:T(8,128)}, u32[]{:S(2)}) copy-start(f32[4,256,32]{1,2,0:T(8,128)} %copy-done.23) | copy-start | bytes 393220
  618.6 26.8 %copy-start.32 = (f32[4,32,256]{2,1,0:T(8,128)S(1)}, f32[4,32,256]{2,1,0:T(8,128)}, u32[]{:S(2)}) copy-start(f32[4,32,256]{2,1,0:T(8,128)} %copy-done.30) | copy-start | bytes 393220
  729.7 28.6 %copy-start.38 = (f32[2304]{0:T(1024)S(1)}, f32[2304]{0:T(1024)}, u32[]{:S(2)}) copy-start(f32[2304]{0:T(1024)} %copy-done.37) | copy-start | bytes 27652
  729.7 28.6 %copy-start.40 = (f32[2304]{0:T(1024)S(1)}, f32[2304]{0:T(1024)}, u32[]{:S(2)}) copy-start(f32[2304]{0:T(1024)} %copy-done.39) | copy-start | bytes 27652
  729.7 28.6 %copy-start.42 = (f32[2304]{0:T(1024)S(1)}, f32[2304]{0:T(1024)}, u32[]{:S(2)}) copy-start(f32[2304]{0:T(1024)} %copy-done.41) | copy-start | bytes 27652
  729.7 28.6 %copy-start.44 = (f32[2304]{0:T(1024)S(1)}, f32[2304]{0:T(1024)}, u32[]{:S(2)}) copy-start(f32[2304]{0:T(1024)} %copy-done.43) | copy-start | bytes 27652
  780.8 23.7 %collective-permute-start.1 = (f32[3,2304]{1,0:T(4,128)S(1)}, f32[3,2304]{1,0:T(4,128)}, u32[]{:S(2)}, u32[]{:S(2)}) collective-permute-start(f32[3,2304]{1,0:T(4,128)S(1)} %copy.281), channel_id=1, source_target_pairs={{4,0},{8,4},{12,8},{16,12},{20,16},{24,20},{28,24},{5,1},{9,5},{13... | collective-permute-start | bytes 82952 | tf_op jit(solution)/shard_map/ppermute | solution.py:18
  844.2 76.3 %copy-start.65 = (f32[1024]{0:T(1024)S(1)}, f32[1024]{0:T(1024)}, u32[]{:S(2)}) copy-start(f32[1024]{0:T(1024)} %copy-done.64) | copy-start | bytes 12292
  (71 other events, 841.1 us)
Sparse Core Ops, SparseCore 0:
  10.8 83.9 all-gather.8
  221.1 35.6 all-gather.12
  259.7 62.0 all-gather.10
  404.2 47.2 all-gather.14
  583.5 196.3 reduce-scatter.5
  832.5 410.0 reduce-scatter.3
where the time goes:
time: 1260 us; the launch traced here: 1250 us
  matrix products  356 us (28%)
  waiting for transfers between devices  319 us (25%)
  other arithmetic  268 us (21%)
  blocking collectives  179 us (14%)
  local copies, waits for them, and re-layouts  108 us (9%)
  between operations  18.1 us (1%)
    reduce_scatter x1, waiting for transfers between devices, on_device(): lax.psum_scatter(grad_in_w, ('seq', 'fsdp'), scatter_dimension=0, tiled=T...  317 us
    dot_general x3, matrix products, local_scan(): output = jnp.einsum('bhts,bshp->bthp', mixing, block_values, precision=HIGH)  142 us
    unnamed x3, blocking collectives  112 us
    another operation x11, other arithmetic  70.8 us
    all_gather x1, blocking collectives, on_device(): lax.all_gather(conv_weight, ('seq', 'fsdp'), axis=1, tiled=True)  66.9 us
    dot_general x4, matrix products, local_scan(): jnp.einsum('bht,btn,bhpn->bthp', enter_block, block_queries, states_in, p...  50.7 us
    dot_general x3, matrix products, local_scan(): jnp.einsum('bhs,bshp,bsn->bhpn', weight_tail, block_values, block_keys, p...  42.2 us
    reduce_sum x1, other arithmetic, conv_local(): conv_weight[offset][None, :] * conv_ext[offset:offset + row_count]  28.6 us
  transfers between devices with their start and end apart: 8, of which 1 were waited for; matrix products, arithmetic and copies ran while one was open for 48% of the time, Pallas kernels for 0%

commit v1 on v0

v1 whole, which is shorter than its diff:
```python
import functools

import jax
import jax.numpy as jnp
import numpy as np
from jax import lax
from jax.experimental import pallas as pl
from jax.experimental.pallas import tpu as pltpu
from jax.sharding import Mesh
from jax.sharding import PartitionSpec as P

HEADS = 32
HEADDIM = 64
STATE = 128
CHUNK = 128
LANES = 128
DI = HEADS * HEADDIM
CHANNELS = DI + 2 * STATE
WIDE = 512
NEG = -1e30
LOG2E = 1.4426950408889634
ALL = ("pair", "core", "fsdp")
BF = jnp.bfloat16
F32 = jnp.float32
NT = (((1,), (1,)), ((), ()))
TN = (((0,), (0,)), ((), ()))
NN = (((1,), (0,)), ((), ()))
PARAMS = pltpu.CompilerParams(
    dimension_semantics=("arbitrary",), vmem_limit_bytes=56 * 1024 * 1024
)


def mm(a, b, dims=NN):
    return lax.dot_general(a, b, dims, preferred_element_type=F32)


def pieces(x, count):
    out = []
    for _ in range(count):
        part = x.astype(BF)
        out.append(part)
        x = x - part.astype(F32)
    return out


def spread(x, expand):
    hi, lo = pieces(x, 2)
    return mm(hi, expand) + mm(lo, expand)


def head_sum(x, expand):
    hi, lo = pieces(x, 2)
    return mm(hi, expand, NT) + mm(lo, expand, NT)


def cumulate(tri, x):
    a, b, c = pieces(x, 3)
    return mm(tri, a) + mm(tri, b) + mm(tri, c)


def mm3(a, b, dims=NN):
    a_hi, a_lo = pieces(a, 2)
    b_hi, b_lo = pieces(b, 2)
    return mm(a_hi, b_hi, dims) + (mm(a_lo, b_hi, dims) + mm(a_hi, b_lo, dims))


def sigmoid(x):
    return 1.0 / (1.0 + jnp.exp(-x))


def iota2(shape, dim):
    return lax.broadcasted_iota(jnp.int32, shape, dim)


def rows8(x):
    return jnp.sum(x.reshape(x.shape[0] // 8, 8, x.shape[1]), axis=0)


def prep_kernel(
    x_ref, raw_ref, info_ref, halo_ref, w_ref, b_ref, rate_ref, sbias_ref, e_ref,
    z_ref, v_ref, k_ref, q_ref, rc_ref, rs_ref, pack_ref,
    state, thru, carry, pad,
):
    step = pl.program_id(0)

    @pl.when(step == 0)
    def _():
        carry[...] = halo_ref[...]
        state[...] = jnp.zeros_like(state)
        thru[...] = jnp.ones_like(thru)
        pad[...] = jnp.zeros_like(pad)

    info = info_ref[...]
    age = jnp.broadcast_to(info[:, 1:2], (CHUNK, LANES))
    masks = [(age >= d).astype(F32) for d in (1.0, 2.0, 3.0)]
    for tile in range(CHANNELS // LANES):
        sl = slice(tile * LANES, (tile + 1) * LANES)
        x = x_ref[:, sl].astype(F32)
        ext = jnp.concatenate([carry[:, sl], x], axis=0)
        z = b_ref[:, sl] + w_ref[3:4, sl] * x
        for d in (1, 2, 3):
            z = z + w_ref[3 - d : 4 - d, sl] * (ext[8 - d : 8 - d + CHUNK] * masks[d - 1])
        carry[:, sl] = x[CHUNK - 8 :]
        z_ref[:, sl] = z.astype(BF)
        value = z * sigmoid(z)
        if tile < DI // LANES:
            v_ref[:, sl] = value.astype(BF)
        elif tile == DI // LANES:
            k_ref[...] = value
        else:
            q_ref[...] = value

    raw = raw_ref[...].astype(F32) + sbias_ref[...]
    size = jnp.maximum(raw, 0.0) + jnp.log1p(jnp.exp(-jnp.abs(raw)))
    decay = -jnp.exp(rate_ref[...]) * size * LOG2E
    tri = (iota2((CHUNK, CHUNK), 0) >= iota2((CHUNK, CHUNK), 1)).astype(BF)
    running = cumulate(tri, decay)
    shifted = running - jnp.log2(jnp.maximum(size, 1e-37))
    rc_ref[...] = running
    pad[:, :HEADS] = shifted
    rs_ref[...] = pad[...].T[:HEADS]
    total = running[CHUNK - 1 :]
    weight = jnp.exp2(total - shifted) * info[:, 3:4]
    carried = jnp.exp2(running[CHUNK - 8 :]) * info[CHUNK - 8 :, 2:3]
    keys = k_ref[...].astype(BF)
    for g in range(DI // WIDE):
        sl = slice(g * WIDE, (g + 1) * WIDE)
        scaled = (spread(weight, e_ref[:, sl]) * v_ref[:, sl].astype(F32)).astype(BF)
        factor = spread(carried, e_ref[:, sl])[7:8]
        state[:, sl] = factor * state[:, sl] + mm(keys, scaled, TN)
        thru[:, sl] = factor * thru[:, sl]

    @pl.when(step == pl.num_programs(0) - 1)
    def _():
        pack_ref[:STATE] = state[...]
        hi, lo = pieces(thru[...], 2)
        row = iota2((16, DI), 0)
        pack_ref[STATE:] = jnp.where(
            row == 0, hi.astype(F32), jnp.where(row == 1, lo.astype(F32), 0.0)
        )


def shared(q_ref, k_ref, lc_ref, lr_ref):
    scores = mm3(q_ref[...], k_ref[...], NT)
    ok = (iota2((CHUNK, CHUNK), 0) >= iota2((CHUNK, CHUNK), 1)) & (
        lc_ref[:, 0:1] == lr_ref[0, 0:1, :]
    )
    bias = jnp.where(ok, 0.0, NEG)
    low_half = iota2((CHUNK, LANES), 1) < HEADDIM
    return scores, bias, low_half


def two_heads(v, low_half):
    zero = jnp.zeros_like(v)
    return jnp.concatenate([jnp.where(low_half, v, zero), jnp.where(low_half, zero, v)], axis=0)


def intra_kernel(q_ref, k_ref, v_ref, rc_ref, rs_ref, lc_ref, lr_ref, y_ref):
    scores, bias, low_half = shared(q_ref, k_ref, lc_ref, lr_ref)
    for pair in range(HEADS // 2):
        sl = slice(pair * LANES, (pair + 1) * LANES)
        mixing = []
        for h in (2 * pair, 2 * pair + 1):
            differ = (rc_ref[:, h : h + 1] - rs_ref[h : h + 1, :]) + bias
            mixing.append((jnp.exp2(differ) * scores).astype(BF))
        y_ref[:, sl] = mm(jnp.concatenate(mixing, axis=1), two_heads(v_ref[:, sl], low_half))


def gate_kernel(
    y_ref, q_ref, k_ref, v_ref, rc_ref, rs_ref, info_ref, gate_ref, dn_ref, sin_ref,
    skip_ref, gain_ref, e_ref,
    n_ref, dy_ref, dy_lo_ref, dgate_ref, u_ref, dq_ref, sc_ref, pack_ref, sums_ref,
    state, adj, reach, scan, enter, sums, pad,
):
    step = pl.program_id(0)

    @pl.when(step == 0)
    def _():
        state[...] = sin_ref[...]
        adj[...] = jnp.zeros_like(adj)
        reach[...] = jnp.ones_like(reach)
        sums[...] = jnp.zeros_like(sums)

    info = info_ref[...]
    running = rc_ref[...]
    pad[:HEADS] = rs_ref[...]
    shifted = pad[...].T[:, :HEADS]
    total = running[CHUNK - 1 :]
    weight = jnp.exp2(total - shifted) * info[:, 3:4]
    entering = jnp.exp2(running) * info[:, 2:3]
    queries, queries_lo = pieces(q_ref[...], 2)
    keys = k_ref[...].astype(BF)
    squares = jnp.zeros((CHUNK, LANES), F32)
    dots = jnp.zeros((CHUNK, LANES), F32)
    for g in range(DI // WIDE):
        sl = slice(g * WIDE, (g + 1) * WIDE)
        low_state, rest = pieces(state[:, sl], 2)
        sc_ref[:, sl] = low_state
        ent = spread(entering, e_ref[:, sl])
        enter[:, sl] = ent
        y = y_ref[:, sl] + ent * (
            mm(queries, low_state) + (mm(queries_lo, low_state) + mm(queries, rest))
        )
        scan[:, sl] = y
        gate = gate_ref[:, sl].astype(F32)
        gated = (y + skip_ref[:, sl] * v_ref[:, sl].astype(F32)) * (gate * sigmoid(gate))
        square = gated * gated
        dot = dn_ref[:, sl] * gain_ref[:, sl] * gated
        for t in range(WIDE // LANES):
            part = slice(t * LANES, (t + 1) * LANES)
            squares = squares + square[:, part]
            dots = dots + dot[:, part]
    inv = lax.rsqrt(jnp.sum(squares, axis=1, keepdims=True) * (1.0 / DI) + 1e-05)
    coef = inv * inv * inv * jnp.sum(dots, axis=1, keepdims=True) * (1.0 / DI)
    head_dots = jnp.zeros((CHUNK, HEADS), F32)
    dq = jnp.zeros((CHUNK, STATE), F32)
    for g in range(DI // WIDE):
        sl = slice(g * WIDE, (g + 1) * WIDE)
        y = scan[:, sl]
        v = v_ref[:, sl].astype(F32)
        gate = gate_ref[:, sl].astype(F32)
        sig = sigmoid(gate)
        silu = gate * sig
        mixed = y + skip_ref[:, sl] * v
        gated = mixed * silu
        gain = gain_ref[:, sl]
        dn = dn_ref[:, sl]
        unit = gated * inv
        n_ref[:, sl] = (unit * gain).astype(BF)
        sums[0:8, sl] += rows8(dn * unit)
        dg = dn * gain * inv - gated * coef
        dgate_ref[:, sl] = (dg * mixed * (sig + silu * (1.0 - sig))).astype(BF)
        dy = dg * silu
        sums[8:16, sl] += rows8(dy * v)
        low, rest = pieces(dy, 2)
        dy_ref[:, sl] = low
        dy_lo_ref[:, sl] = rest
        head_dots = head_dots + head_sum(low.astype(F32) * y, e_ref[:, sl])
        ent = enter[:, sl]
        dy_in, dy_in_lo = pieces(ent * dy, 2)
        state_hi, state_lo = pieces(state[:, sl], 2)
        dq = dq + (
            mm(dy_in, state_hi, NT) + (mm(dy_in_lo, state_hi, NT) + mm(dy_in, state_lo, NT))
        )
        adj[:, sl] += reach[:, sl] * mm(queries, dy_in, TN)
        factor = ent[CHUNK - 1 :]
        scaled = (spread(weight, e_ref[:, sl]) * v).astype(BF)
        state[:, sl] = factor * state[:, sl] + mm(keys, scaled, TN)
        reach[:, sl] = factor * reach[:, sl]
    u_ref[...] = head_dots
    dq_ref[...] = dq

    @pl.when(step == pl.num_programs(0) - 1)
    def _():
        pack_ref[:STATE] = adj[...].astype(BF)
        hi, lo = pieces(reach[...], 2)
        row = iota2((16, DI), 0)
        pack_ref[STATE:] = jnp.where(
            row == 0, hi.astype(F32), jnp.where(row == 1, lo.astype(F32), 0.0)
        ).astype(BF)
        sums_ref[...] = sums[...]


def intra_back_kernel(
    q_ref, k_ref, v_ref, dy_ref, dy_lo_ref, rc_ref, rs_ref, lc_ref, lr_ref, e_ref, dqin_ref,
    dv_ref, uv_ref, dq_ref, dk_ref,
):
    scores, bias, low_half = shared(q_ref, k_ref, lc_ref, lr_ref)
    dscores = jnp.zeros((CHUNK, CHUNK), F32)
    head_dots = jnp.zeros((CHUNK, HEADS), F32)
    for pair in range(HEADS // 2):
        sl = slice(pair * LANES, (pair + 1) * LANES)
        v = v_ref[:, sl]
        dy = dy_ref[:, sl]
        vv = two_heads(v, low_half)
        dmix = mm(
            jnp.concatenate([dy, dy_lo_ref[:, sl]], axis=1),
            jnp.concatenate([vv, vv], axis=1),
            NT,
        )
        mixing = []
        for i in range(2):
            h = 2 * pair + i
            differ = (rc_ref[:, h : h + 1] - rs_ref[h : h + 1, :]) + bias
            factor = jnp.exp2(differ)
            dscores = dscores + dmix[:, i * CHUNK : (i + 1) * CHUNK] * factor
            mixing.append((factor * scores).astype(BF))
        both = mm(jnp.concatenate(mixing, axis=1), dy, TN)
        dv = jnp.where(low_half, both[:CHUNK], both[CHUNK:])
        dv_ref[:, sl] = dv.astype(BF)
        head_dots = head_dots + head_sum(v.astype(F32) * dv, e_ref[:, sl])
    uv_ref[...] = head_dots
    dq_ref[...] = dqin_ref[...] + mm3(dscores, k_ref[...])
    dk_ref[...] = mm(dscores.astype(BF), q_ref[...].astype(BF), TN)


def back_kernel(
    x_ref, raw_ref, z_ref, v_ref, k_ref, q_ref, rc_ref, rs_ref, info_ref, dy_ref, dv_ref,
    uv_ref, u_ref, dq_ref, dk_ref, sc_ref, ain_ref, halo_ref, w_ref, rate_ref, sbias_ref,
    skip_ref, e_ref,
    dx_ref, dhalo_ref, csum_ref, hsum_ref,
    adj, nextz, nextage, csum, hsum, pad, dmix,
):
    step = pl.program_id(0)

    @pl.when(step == 0)
    def _():
        adj[...] = ain_ref[...]
        nextz[...] = jnp.zeros_like(nextz)
        nextage[...] = jnp.zeros_like(nextage)
        csum[...] = jnp.zeros_like(csum)
        hsum[...] = jnp.zeros_like(hsum)

    info = info_ref[...]
    running = rc_ref[...]
    pad[:HEADS] = rs_ref[...]
    shifted = pad[...].T[:, :HEADS]
    total = running[CHUNK - 1 :]
    weight = jnp.exp2(total - shifted) * info[:, 3:4]
    entering = jnp.exp2(running) * info[:, 2:3]
    queries = q_ref[...].astype(BF)
    keys = k_ref[...].astype(BF)
    dq = dq_ref[...]
    dk = dk_ref[...]
    later = jnp.zeros((CHUNK, HEADS), F32)
    through = jnp.zeros((8, HEADS), F32)
    for g in range(DI // WIDE):
        sl = slice(g * WIDE, (g + 1) * WIDE)
        e = e_ref[:, sl]
        v = v_ref[:, sl].astype(F32)
        dy = dy_ref[:, sl].astype(F32)
        ent = spread(entering, e)
        wide = spread(weight, e)
        dy_in = (ent * dy).astype(BF)
        scaled = (wide * v).astype(BF)
        adjoint = adj[:, sl]
        low_adj = adjoint.astype(BF)
        states = sc_ref[:, sl]
        dv = wide * mm(keys, low_adj)
        later = later + head_sum(v * dv, e)
        dk = dk + mm(scaled, low_adj, NT)
        factor = ent[CHUNK - 1 :]
        through = through + head_sum(rows8(adjoint * states.astype(F32)) * factor, e)
        adj[:, sl] = factor * adjoint + mm(queries, dy_in, TN)
        dmix[:, sl] = dv_ref[:, sl].astype(F32) + dv + skip_ref[:, sl] * dy
    dmix[:, DI : DI + STATE] = dk
    dmix[:, DI + STATE :] = dq

    age = jnp.broadcast_to(info[:, 1:2], (CHUNK, LANES))
    masks = [(age >= d).astype(F32) for d in (1.0, 2.0, 3.0)]
    ages = nextage[...]
    next_masks = [(ages >= d).astype(F32) for d in (1.0, 2.0, 3.0)]
    for tile in range(CHANNELS // LANES):
        sl = slice(tile * LANES, (tile + 1) * LANES)
        z = z_ref[:, sl].astype(F32)
        sig = sigmoid(z)
        dz = dmix[:, sl] * (sig + z * sig * (1.0 - sig))
        x = x_ref[:, sl].astype(F32)
        after = nextz[:, sl]
        dx = w_ref[3:4, sl] * dz
        csum[32:40, sl] += rows8(dz)
        csum[24:32, sl] += rows8(x * dz)
        for d in (1, 2, 3):
            ext = jnp.concatenate([dz * masks[d - 1], after * next_masks[d - 1]], axis=0)
            moved = ext[d : d + CHUNK]
            dx = dx + w_ref[3 - d : 4 - d, sl] * moved
            csum[8 * (3 - d) : 8 * (4 - d), sl] += rows8(x * moved)
        dx_ref[:, sl] = dx.astype(BF)
        nextz[:, sl] = dz[:8]

        @pl.when(step == pl.num_programs(0) - 1)
        def _():
            halo = halo_ref[:, sl]
            acc = jnp.zeros((8, LANES), F32)
            for d in (1, 2, 3):
                ext = jnp.concatenate(
                    [jnp.zeros((8, LANES), F32), dz[:8] * masks[d - 1][:8]], axis=0
                )
                moved = ext[d : d + 8]
                acc = acc + w_ref[3 - d : 4 - d, sl] * moved
                csum[8 * (3 - d) : 8 * (4 - d), sl] += halo * moved
            dhalo_ref[:, sl] = acc
    nextage[...] = age[:8]

    row = iota2((CHUNK, CHUNK), 0)
    col = iota2((CHUNK, CHUNK), 1)
    ddecay = (
        cumulate((col >= row).astype(BF), u_ref[...] - uv_ref[...])
        + cumulate((col < row).astype(BF), later)
        + jnp.sum(through, axis=0, keepdims=True)
    )
    raw = raw_ref[...].astype(F32) + sbias_ref[...]
    sig = sigmoid(raw)
    size = jnp.maximum(raw, 0.0) + jnp.log1p(jnp.exp(-jnp.abs(raw)))
    rate = -jnp.exp(rate_ref[...])
    ratio = jnp.where(raw < -15.0, 1.0, sig / jnp.maximum(size, 1e-37))
    draw = (uv_ref[...] + later) * ratio + ddecay * rate * sig
    dx_ref[:, CHANNELS:] = draw.astype(BF)
    hsum[0:8] += rows8(ddecay * rate * size)
    hsum[8:16] += rows8(draw)

    @pl.when(step == pl.num_programs(0) - 1)
    def _():
        csum_ref[...] = csum[...]
        hsum_ref[...] = hsum[...]


def whole(shape):
    return pl.BlockSpec(shape, lambda c: (0,) * len(shape))


def rows(width, count=None, per=CHUNK):
    if count is None:
        return pl.BlockSpec((per, width), lambda c: (c, 0))
    return pl.BlockSpec((per, width), lambda c: (count - 1 - c, 0))


def shape(dims, kind):
    return jax.ShapeDtypeStruct(dims, kind)


def cost(flops, moved):
    return pl.CostEstimate(flops=flops, bytes_accessed=moved, transcendentals=0)


def vm(dims, kind=F32):
    return pltpu.VMEM(dims, kind)


def pack(state, thru, kind):
    hi, lo = pieces(thru, 2)
    return jnp.concatenate([state.astype(kind), hi.astype(kind), lo.astype(kind)], axis=0)


def unpack(packed):
    packed = packed.astype(F32)
    return packed[:STATE], packed[STATE : STATE + 1] + packed[STATE + 1 : STATE + 2]


def carry_states(packed, pairs, backward):
    packed = packed[: STATE + 2]
    core = lax.axis_index("core")
    place = lax.axis_index("pair")
    half = packed.shape[1] // 2
    swap = [(0, 1), (1, 0)]
    left, right = packed[:, :half], packed[:, half:]
    mine = jnp.where(core == 0, left, right)
    theirs = lax.ppermute(jnp.where(core == 0, right, left), "core", swap)
    leads = (core == 1) if backward else (core == 0)
    first, first_thru = unpack(jnp.where(leads, mine, theirs))
    second, second_thru = unpack(jnp.where(leads, theirs, mine))
    total, total_thru = second + second_thru * first, second_thru * first_thru
    before, before_thru = jnp.zeros_like(total), jnp.ones_like(total_thru)
    distance = 1
    while distance < pairs:
        route = [(i, i ^ distance) for i in range(pairs)]
        other, other_thru = unpack(
            lax.ppermute(pack(total, total_thru, packed.dtype), "pair", route)
        )
        upper = (place & distance) != 0
        follows = jnp.logical_not(upper) if backward else upper
        before = jnp.where(follows, before + before_thru * other, before)
        before_thru = jnp.where(follows, before_thru * other_thru, before_thru)
        total = jnp.where(
            follows, total + total_thru * other, other + other_thru * total
        )
        total_thru = total_thru * other_thru
        distance *= 2
    after = first + first_thru * before
    keep = jnp.where(leads, before, after)
    other = lax.ppermute(
        jnp.where(leads, after, before).astype(packed.dtype), "core", swap
    ).astype(F32)
    return jnp.where(
        core == 0,
        jnp.concatenate([keep, other], axis=1),
        jnp.concatenate([other, keep], axis=1),
    )


def shift(block, count, by):
    moved = [(i, i + by) for i in range(count) if 0 <= i + by < count]
    return lax.ppermute(block, ("pair", "core"), moved)


def swap(block, axis, mask):
    count = lax.axis_size(axis)
    return lax.ppermute(block, axis, [(i, i ^ mask) for i in range(count)])


def bit_orders(pairs):
    bits = list(range(pairs.bit_length() - 1))
    cut = len(bits) // 2
    return bits, bits[cut:] + bits[:cut]


def part_ids(pairs, fsdp):
    out = []
    for part, order in enumerate(bit_orders(pairs)):
        ids = [(0, k) for k in range(part * fsdp // 2, (part + 1) * fsdp // 2)]
        for b in order:
            ids = ids + [(mask ^ (1 << b), k) for mask, k in ids]
        out.append(ids)
    return out


def shard_of(place_ref, fsdp, mask, flip, k):
    return ((place_ref[0] ^ mask) * 2 + (place_ref[1] ^ flip)) * fsdp + (place_ref[2] ^ k)


def place_rows(place, pieces_in, r, fsdp, total):
    jobs = [
        (i, at, mask, flip, k)
        for i, (_, flip, ids) in enumerate(pieces_in)
        for at, (mask, k) in enumerate(ids)
    ]

    def body(place_ref, *refs):
        dst, sem = refs[-2], refs[-1]
        copies = []
        for j, (i, at, mask, flip, k) in enumerate(jobs):
            row = pl.multiple_of(shard_of(place_ref, fsdp, mask, flip, k) * r, r)
            copies.append(
                pltpu.make_async_copy(
                    refs[i].at[pl.ds(at * r, r)], dst.at[pl.ds(row, r)], sem.at[j]
                )
            )
            copies[-1].start()
        for copy in copies:
            copy.wait()

    arrays = [a for a, _, _ in pieces_in]
    cols = arrays[0].shape[1]
    return pl.pallas_call(
        body,
        name="place_rows",
        in_specs=[pl.BlockSpec(memory_space=pltpu.SMEM)]
        + [pl.BlockSpec(memory_space=pl.ANY)] * len(arrays),
        out_specs=pl.BlockSpec(memory_space=pl.ANY),
        out_shape=jax.ShapeDtypeStruct((total, cols), arrays[0].dtype),
        scratch_shapes=[pltpu.SemaphoreType.DMA((len(jobs),))],
        cost_estimate=pl.CostEstimate(
            flops=0, bytes_accessed=4 * total * cols, transcendentals=0
        ),
    )(place, *arrays)


def pick_rows(place, whole_rows, r, pairs, fsdp):
    order = [i for ids in part_ids(pairs, fsdp) for i in ids]
    half = len(order) * r
    cols = whole_rows.shape[1]

    def body(place_ref, src, keep, give, sem):
        copies = []
        for flip, dst in ((1, give), (0, keep)):
            for at, (mask, k) in enumerate(order):
                row = pl.multiple_of(shard_of(place_ref, fsdp, mask, flip, k) * r, r)
                copies.append(
                    pltpu.make_async_copy(
                        src.at[pl.ds(row, r)], dst.at[pl.ds(at * r, r)], sem.at[len(copies)]
                    )
                )
                copies[-1].start()
        for copy in copies:
            copy.wait()

    return pl.pallas_call(
        body,
        name="pick_rows",
        in_specs=[
            pl.BlockSpec(memory_space=pltpu.SMEM), pl.BlockSpec(memory_space=pl.ANY),
        ],
        out_specs=[pl.BlockSpec(memory_space=pl.ANY)] * 2,
        out_shape=[jax.ShapeDtypeStruct((half, cols), whole_rows.dtype)] * 2,
        scratch_shapes=[pltpu.SemaphoreType.DMA((2 * len(order),))],
        cost_estimate=pl.CostEstimate(
            flops=0, bytes_accessed=8 * half * cols, transcendentals=0
        ),
    )(place, whole_rows)


def gather_rows(w, place, pairs):
    r, fsdp = w.shape[0], lax.axis_size("fsdp")
    if r % 16:
        return lax.all_gather(w, ALL, axis=0, tiled=True)
    line = [w] + [swap(w, "fsdp", k) for k in range(1, fsdp)]
    held = []
    for part, order in enumerate(bit_orders(pairs)):
        ks = range(part * fsdp // 2, (part + 1) * fsdp // 2)
        block = jnp.concatenate([line[k] for k in ks], axis=0)
        ids = [(0, k) for k in ks]
        held.append((block, 0, ids))
        for b in order:
            got = swap(block, "pair", 1 << b)
            got_ids = [(mask ^ (1 << b), k) for mask, k in ids]
            held.append((got, 0, got_ids))
            block = jnp.concatenate([block, got], axis=0)
            ids = ids + got_ids
    held = held + [(swap(a, "core", 1), 1, ids) for a, _, ids in held]
    return place_rows(place, held, r, fsdp, 2 * pairs * fsdp * r)


def reduce_rows(g, place, pairs):
    fsdp = lax.axis_size("fsdp")
    r = g.shape[0] // (2 * pairs * fsdp)
    if r % 16:
        return lax.psum_scatter(g.astype(F32), ALL, scatter_dimension=0, tiled=True)
    keep, give = pick_rows(place, g, r, pairs, fsdp)
    summed = keep.astype(F32) + swap(give, "core", 1).astype(F32)
    half = summed.shape[0] // 2
    ends = []
    for part, order in enumerate(bit_orders(pairs)):
        block = summed[part * half : (part + 1) * half]
        for b in reversed(order):
            cut = block.shape[0] // 2
            got = swap(block[cut:].astype(BF), "pair", 1 << b)
            block = block[:cut] + got.astype(F32)
        ends.append(block)
    total = ends[0][:r]
    for k in range(1, fsdp):
        at = (k % (fsdp // 2)) * r
        block = ends[k // (fsdp // 2)][at : at + r]
        total = total + swap(block.astype(BF), "fsdp", k).astype(F32)
    return total


def links(pairs, fsdp):
    out = [("fsdp", 1 << b) for b in range(fsdp.bit_length() - 1)]
    out.append(("core", 1))
    return out + [("pair", 1 << b) for b in range(pairs.bit_length() - 1)]


def gather_small(vec, place_index, pairs, fsdp):
    block = vec[None]
    for axis, mask in links(pairs, fsdp):
        block = jnp.concatenate([block, swap(block, axis, mask)], axis=0)
    count = block.shape[0]
    index = jnp.arange(count)
    pick = (index[:, None] == (index[None] ^ place_index)).astype(BF)
    return jnp.dot(pick, block, preferred_element_type=F32)


def sum_small(block, pairs, fsdp):
    for axis, mask in links(pairs, fsdp):
        block = block + swap(block, axis, mask)
    return block


def hidden_of(tokens, gain):
    x = tokens.astype(F32)
    return (x * lax.rsqrt(jnp.mean(x * x, axis=-1, keepdims=True) + 1e-05) * gain).astype(BF)


def on_device(
    pairs, tokens, segment_ids, in_weight, out_weight, conv_weight, conv_bias, norm_gain,
    gate_gain, log_rate, skip_gain, step_bias, cotangent,
):
    tokens, labels, upstream = tokens[0], segment_ids[0], cotangent[0]
    count, model = tokens.shape
    chunks = count // CHUNK
    taps = conv_weight.shape[0]
    own = (conv_weight.size, conv_bias.size, norm_gain.size, gate_gain.size)
    fsdp = lax.axis_size("fsdp")
    place = jnp.stack([lax.axis_index(a) for a in ALL])
    device = (place[0] * 2 + place[1]) * fsdp + place[2]
    small = jnp.concatenate([conv_weight.reshape(-1), conv_bias, norm_gain, gate_gain])
    small = gather_small(small, device, pairs, fsdp)
    conv_full = (
        small[:, : own[0]].reshape(-1, taps, own[0] // taps).transpose(1, 0, 2)
        .reshape(taps, CHANNELS).astype(F32)
    )
    at = own[0]
    bias_full = small[:, at : at + own[1]].reshape(1, CHANNELS).astype(F32)
    at += own[1]
    norm_full = small[:, at : at + own[2]].reshape(1, model).astype(F32)
    at += own[2]
    gate_full = small[:, at :].reshape(1, DI).astype(F32)
    w_mix = gather_rows(in_weight[:, DI:], place, pairs)
    w_gate = gather_rows(in_weight[:, :DI], place, pairs)
    w_out = gather_rows(out_weight, place, pairs)

    expand = jnp.asarray(np.repeat(np.eye(HEADS), HEADDIM, axis=1), BF)
    skip_wide = jnp.repeat(skip_gain, HEADDIM)[None]
    rate, sbias = log_rate[None], step_bias[None]
    before = jnp.concatenate([jnp.broadcast_to(labels[:1], (3,)), labels])
    age = sum((before[3 - d : 3 - d + count] == labels).astype(F32) for d in (1, 2, 3))
    by_chunk = labels.reshape(chunks, CHUNK)
    last = by_chunk[:, -1:]
    prior = jnp.concatenate([by_chunk[:1, :1], last[:-1]], axis=0)
    info = jnp.stack(
        [
            labels.astype(F32),
            age,
            (by_chunk == prior).astype(F32).reshape(-1),
            (by_chunk == last).astype(F32).reshape(-1),
        ]
        + [jnp.zeros((count,), F32)] * 4,
        axis=1,
    )
    label_rows = labels.astype(F32).reshape(chunks, 1, CHUNK)
    row_spec = pl.BlockSpec((1, 1, CHUNK), lambda c: (c, 0, 0))

    tail = shift(tokens[count - 8 :], 2 * pairs, 1)
    hidden = hidden_of(tokens, norm_full)
    halo_hidden = hidden_of(tail, norm_full)
    mix = jnp.dot(hidden, w_mix, preferred_element_type=F32).astype(BF)
    raw_step = mix[:, CHANNELS:]
    halo = jnp.dot(halo_hidden, w_mix[:, :CHANNELS], preferred_element_type=F32)
    halo = halo.astype(BF).astype(F32)

    z, v, k, q, rc, rs, packed = pl.pallas_call(
        prep_kernel,
        name="conv_states",
        grid=(chunks,),
        in_specs=[
            rows(CHANNELS), rows(HEADS), rows(8), whole((8, CHANNELS)), whole((taps, CHANNELS)),
            whole((1, CHANNELS)), whole((1, HEADS)), whole((1, HEADS)), whole((HEADS, DI)),
        ],
        out_specs=[
            rows(CHANNELS), rows(DI), rows(STATE), rows(STATE), rows(HEADS),
            rows(CHUNK, per=HEADS), whole((STATE + 16, DI)),
        ],
        out_shape=[
            shape((count, CHANNELS), BF), shape((count, DI), BF), shape((count, STATE), F32),
            shape((count, STATE), F32), shape((count, HEADS), F32),
            shape((chunks * HEADS, CHUNK), F32), shape((STATE + 16, DI), F32),
        ],
        scratch_shapes=[
            vm((STATE, DI)), vm((1, DI)), vm((8, CHANNELS)), vm((CHUNK, LANES)),
        ],
        compiler_params=PARAMS,
        cost_estimate=cost(10**9, 30 * 10**6),
    )(mix, raw_step, info, halo, conv_full, bias_full, rate, sbias, expand)

    incoming = carry_states(packed, pairs, False)

    y_local = pl.pallas_call(
        intra_kernel,
        name="intra",
        grid=(chunks,),
        in_specs=[
            rows(STATE), rows(STATE), rows(DI), rows(HEADS), rows(CHUNK, per=HEADS), rows(8),
            row_spec,
        ],
        out_specs=rows(DI),
        out_shape=shape((count, DI), F32),
        compiler_params=PARAMS,
        cost_estimate=cost(10**9, 30 * 10**6),
    )(q, k, v, rc, rs, info, label_rows)

    gate = jnp.dot(hidden, w_gate, preferred_element_type=F32).astype(BF)
    grad_normed = lax.dot_general(upstream, w_out, NT, preferred_element_type=F32)

    normed, dy, dy_lo, dgate, u, dq, states, packed_back, gate_sums = pl.pallas_call(
        gate_kernel,
        name="gate_norm",
        grid=(chunks,),
        in_specs=[
            rows(DI), rows(STATE), rows(STATE), rows(DI), rows(HEADS), rows(CHUNK, per=HEADS),
            rows(8), rows(DI), rows(DI), whole((STATE, DI)), whole((1, DI)), whole((1, DI)),
            whole((HEADS, DI)),
        ],
        out_specs=[
            rows(DI), rows(DI), rows(DI), rows(DI), rows(HEADS), rows(STATE), rows(DI),
            whole((STATE + 16, DI)), whole((16, DI)),
        ],
        out_shape=[
            shape((count, DI), BF), shape((count, DI), BF), shape((count, DI), BF),
            shape((count, DI), BF), shape((count, HEADS), F32), shape((count, STATE), F32),
            shape((chunks * STATE, DI), BF),
            shape((STATE + 16, DI), BF), shape((16, DI), F32),
        ],
        scratch_shapes=[
            vm((STATE, DI)), vm((STATE, DI)), vm((1, DI)), vm((CHUNK, DI)), vm((CHUNK, DI)),
            vm((16, DI)), vm((LANES, CHUNK)),
        ],
        compiler_params=PARAMS,
        cost_estimate=cost(10**9, 50 * 10**6),
    )(
        y_local, q, k, v, rc, rs, info, gate, grad_normed, incoming, skip_wide, gate_full,
        expand,
    )

    coming_back = carry_states(packed_back, pairs, True)

    grad_out_w = lax.dot_general(normed, upstream, TN, preferred_element_type=F32).astype(BF)
    out_shard = reduce_rows(grad_out_w, place, pairs)
    grad_gate_w = lax.dot_general(hidden, dgate, TN, preferred_element_type=F32).astype(BF)
    gate_shard = reduce_rows(grad_gate_w, place, pairs)
    block_out = (
        tokens.astype(F32) + jnp.dot(normed, w_out, preferred_element_type=F32)
    ).astype(BF)

    dv, uv, dq, dk = pl.pallas_call(
        intra_back_kernel,
        name="intra_back",
        grid=(chunks,),
        in_specs=[
            rows(STATE), rows(STATE), rows(DI), rows(DI), rows(DI), rows(HEADS),
            rows(CHUNK, per=HEADS), rows(8), row_spec, whole((HEADS, DI)), rows(STATE),
        ],
        out_specs=[rows(DI), rows(HEADS), rows(STATE), rows(STATE)],
        out_shape=[
            shape((count, DI), BF), shape((count, HEADS), F32), shape((count, STATE), F32),
            shape((count, STATE), F32),
        ],
        compiler_params=PARAMS,
        cost_estimate=cost(2 * 10**9, 40 * 10**6),
    )(q, k, v, dy, dy_lo, rc, rs, info, label_rows, expand, dq)

    back = functools.partial(rows, count=chunks)
    grad_mix, dhalo, conv_sums, head_sums = pl.pallas_call(
        back_kernel,
        name="states_conv_back",
        grid=(chunks,),
        in_specs=[
            back(CHANNELS), back(HEADS), back(CHANNELS), back(DI), back(STATE), back(STATE),
            back(HEADS), back(CHUNK, per=HEADS), back(8), back(DI), back(DI), back(HEADS),
            back(HEADS), back(STATE), back(STATE), back(DI), whole((STATE, DI)),
            whole((8, CHANNELS)), whole((taps, CHANNELS)), whole((1, HEADS)),
            whole((1, HEADS)), whole((1, DI)), whole((HEADS, DI)),
        ],
        out_specs=[
            back(CHANNELS + HEADS), whole((8, CHANNELS)), whole((40, CHANNELS)),
            whole((16, HEADS)),
        ],
        out_shape=[
            shape((count, CHANNELS + HEADS), BF), shape((8, CHANNELS), F32),
            shape((40, CHANNELS), F32), shape((16, HEADS), F32),
        ],
        scratch_shapes=[
            vm((STATE, DI)), vm((8, CHANNELS)), vm((8, LANES)), vm((40, CHANNELS)),
            vm((16, HEADS)), vm((LANES, CHUNK)), vm((CHUNK, CHANNELS)),
        ],
        compiler_params=PARAMS,
        cost_estimate=cost(2 * 10**9, 60 * 10**6),
    )(
        mix, raw_step, z, v, k, q, rc, rs, info, dy, dv, uv, u, dq, dk, states, coming_back,
        halo, conv_full, rate, sbias, skip_wide, expand,
    )

    edge = shift(dhalo, 2 * pairs, -1)
    edge = jnp.pad(edge, ((0, 0), (0, HEADS)))
    fixed = (grad_mix[count - 8 :].astype(F32) + edge).astype(BF)
    grad_mix = lax.dynamic_update_slice(grad_mix, fixed, (count - 8, 0))
    grad_mix_w = lax.dot_general(hidden, grad_mix, TN, preferred_element_type=F32).astype(BF)
    mix_shard = reduce_rows(grad_mix_w, place, pairs)
    grad_hidden = lax.dot_general(dgate, w_gate, NT, preferred_element_type=F32)
    grad_hidden = grad_hidden + lax.dot_general(grad_mix, w_mix, NT, preferred_element_type=F32)

    x = tokens.astype(F32)
    inv = lax.rsqrt(jnp.mean(x * x, axis=-1, keepdims=True) + 1e-05)
    unit = x * inv
    scaled = grad_hidden * norm_full
    mean = jnp.mean(scaled * unit, axis=-1, keepdims=True)
    grad_tokens = upstream.astype(F32) + inv * (scaled - unit * mean)
    grad_norm = jnp.sum(grad_hidden * unit, axis=0)

    conv_sums = conv_sums.reshape(taps + 1, 8, CHANNELS).sum(axis=1)
    gate_sums = gate_sums.reshape(2, 8, DI).sum(axis=1)
    head_sums = head_sums.reshape(2, 8, HEADS).sum(axis=1)
    grad_skip = gate_sums[1].reshape(HEADS, HEADDIM).sum(axis=1)
    devices = 2 * pairs * fsdp
    parts = jnp.concatenate(
        [
            conv_sums.reshape(taps + 1, devices, own[1]).transpose(1, 0, 2).reshape(devices, -1),
            grad_norm.reshape(devices, -1),
            gate_sums[0].reshape(devices, -1),
            jnp.broadcast_to(
                jnp.concatenate([head_sums[0], grad_skip, head_sums[1]])[None],
                (devices, 3 * HEADS),
            ),
        ],
        axis=1,
    )
    mine = lax.dynamic_slice(
        sum_small(parts, pairs, fsdp), (device, 0), (1, parts.shape[1])
    )[0]
    ends = np.cumsum([own[0], own[1], own[2], own[3], HEADS, HEADS, HEADS]).tolist()
    conv_shard, bias_shard, norm_shard, gain_shard, *heads = [
        mine[a:b] for a, b in zip([0] + ends[:-1], ends)
    ]
    conv_shard = conv_shard.reshape(taps, -1)
    in_shard = jnp.concatenate([gate_shard, mix_shard], axis=1)
    return (
        block_out[None],
        grad_tokens[None],
        in_shard,
        out_shard,
        conv_shard,
        bias_shard,
        norm_shard,
        gain_shard,
        heads[0],
        heads[1],
        heads[2],
    )


def solution(mesh):
    seq, fsdp = mesh.devices.shape
    fine = Mesh(mesh.devices.reshape(seq // 2, 2, fsdp), ALL)
    line = ("pair", "core")
    tokens, labels, mat = P("fsdp", line, None), P("fsdp", line), P(ALL, None)
    weights = (mat, mat, P(None, ALL), P(ALL), P(ALL), P(ALL), P(), P(), P())
    return jax.shard_map(
        functools.partial(on_device, seq // 2),
        mesh=fine,
        in_specs=(tokens, labels) + weights + (tokens,),
        out_specs=(tokens, tokens) + weights,
        check_vma=False,
    )
```

time: 1260 us -> 1340 us (1.063)
  Pallas kernels: 0 us -> 953 us
  matrix products: 356 us -> 75.8 us
  other arithmetic: 268 us -> 53.5 us
  waiting for transfers between devices: 319 us -> 116 us
  blocking collectives: 179 us -> 0 us
  starting transfers between devices: 2.82 us -> 80.8 us
  local copies, waits for them, and re-layouts: 108 us -> 54.5 us
  between operations: 18.1 us -> 2.08 us
    pallas_call x0 -> x11, Pallas kernels: none -> 953 us  [the longest x3 411 us: place_rows(): pl.pallas_call(body, name='place_rows', in_specs=[pl.BlockSpec(memory_spa...]
    reduce_scatter x2 -> x0, waiting for transfers between devices: 317 us -> none  [the longest x1 317 us: on_device(): lax.psum_scatter(grad_in_w, ('seq', 'fsdp'), scatter_dimension=0, tiled=T...]
    dot_general x22 -> x11, matrix products: 356 us -> 75.8 us  [the longest x1 9.88 us: on_device(): lax.dot_general(hidden, grad_mix, TN, preferred_element_type=F32).astype(BF)]
    ppermute x2 -> x83, waiting for transfers between devices: 0.01 us -> 116 us  [the longest x73 98.3 us: swap(): return lax.ppermute(block, axis, [(i, i ^ mask) for i in range(count)])]
    unnamed x3 -> x0, blocking collectives: 112 us -> none
    ppermute x2 -> x83, starting transfers between devices: 2.58 us -> 80.8 us  [the longest x73 75.3 us: swap(): return lax.ppermute(block, axis, [(i, i ^ mask) for i in range(count)])]
    reduce_sum x14 -> x6, other arithmetic: 72.6 us -> 4.15 us  [the longest x2 2.19 us: hidden_of(): jnp.mean(x * x, axis=-1, keepdims=True) + 1e-05]
    all_gather x1 -> x0, blocking collectives: 66.9 us -> none  [on_device(): lax.all_gather(conv_weight, ('seq', 'fsdp'), axis=1, tiled=True)]
  transfers between devices with their start and end apart: 8 -> 83, of which waited for: 1 -> 28; matrix products, arithmetic and copies ran while one was open for 48% -> 11% of each run, Pallas kernels for 0% -> 66%
where the time goes in v1:
time: 1340 us
  Pallas kernels  953 us (71%)
  waiting for transfers between devices  116 us (9%)
  starting transfers between devices  80.8 us (6%)
  matrix products  75.8 us (6%)
  local copies, waits for them, and re-layouts  54.5 us (4%)
  other arithmetic  53.5 us (4%)
    pallas_call x3, Pallas kernels, place_rows(): pl.pallas_call(body, name='place_rows', in_specs=[pl.BlockSpec(memory_spa...  411 us
    pallas_call x3, Pallas kernels, pick_rows(): pl.pallas_call(body, name='pick_rows', in_specs=[pl.BlockSpec(memory_spac...  411 us
    ppermute x73, waiting for transfers between devices, swap(): return lax.ppermute(block, axis, [(i, i ^ mask) for i in range(count)])  98.3 us
    ppermute x73, starting transfers between devices, swap(): return lax.ppermute(block, axis, [(i, i ^ mask) for i in range(count)])  75.3 us
    pallas_call x1, Pallas kernels, on_device(): pl.pallas_call(back_kernel, name='states_conv_back', grid=(chunks,), in_s...  37.5 us
    pallas_call x1, Pallas kernels, on_device(): pl.pallas_call(gate_kernel, name='gate_norm', grid=(chunks,), in_specs=[r...  33.1 us
    pallas_call x1, Pallas kernels, on_device(): pl.pallas_call(intra_back_kernel, name='intra_back', grid=(chunks,), in_s...  29.2 us
  transfers between devices with their start and end apart: 83, of which 28 were waited for; matrix products, arithmetic and copies ran while one was open for 11% of the time, Pallas kernels for 66%

profile of v1, /device:TPU:0, one launch (start us, length us, event | category | flops | bytes accessed | tf_op | source)
XLA Modules:
  0.0 1335.2 jit_solution(16064176827349653087)
XLA Ops:
  1.6 5.1 collective-permute-start.23
  38.9 11.7 collective-permute-done.8
  75.7 8.8 collective-permute-done.35
  102.1 152.9 %place_rows.3 = bf16[1024,2336]{1,0:T(8,128)(2,1)} custom-call(s32[3]{0:T(128)} %pad_add_fusion.place_ref, bf16[64,2336]{1,0:T(8,128)(2,1)} %copy-done.13, bf16[64,2336]{1,0:T(8,128)(2,1)} %copy-done.14, bf16[128,2336]{1,0:T(8,128)(2,1)} %copy.72.refs_2_, bf16[64,2336]{1,0:T(8,128)(2,1)} %constant_dynamic-update-slice_fusion.refs_3_, ...), custom_call_target="tpu_custom_call" | custom-call | bytes 9568256 | tf_op jit(solution)/shard_map/place_rows/pallas_call | solution.py:534
  255.1 8.8 convolution_convert_fusion.1.x_ref
  266.2 18.9 %conv_states.1 = (bf16[1024,2304]{1,0:T(8,128)(2,1)}, bf16[1024,2048]{1,0:T(8,128)(2,1)}, f32[1024,128]{1,0:T(8,128)}, f32[1024,128]{1,0:T(8,128)}, f32[1024,32]...) custom-call(bf16[1024,2336]{1,0:T(8,128)(2,1)} %copy-done, bf16[1024,32]{1,0:T(8,128)(2,1)} %slice.433.raw_ref, ...), custom_call_target="tpu_custom_call" | custom-call | flops 1000000000 | bytes 30000000 | tf_op jit(solution)/shard_map/conv_states/pallas_call | solution.py:711
  298.8 8.0 collective-permute-done.34.refs_2_
  310.4 6.8 collective-permute-done.21.refs_2_
  324.3 129.1 %place_rows.5 = bf16[2048,1024]{1,0:T(8,128)(2,1)} custom-call(s32[3]{0:T(128)} %pad_add_fusion.place_ref, bf16[128,1024]{1,0:T(8,128)(2,1)} %constant_dynamic-update-slice_fusion.4.refs_0_, bf16[128,1024]{1,0:T(8,128)(2,1)} %collective-permute-done.33.refs_1_, bf16[256,1024]{1,0:T(8,128)(2,1)} %copy-done.24, bf16[128,1024]{1,0:T(8,128)(2,1)} %copy-done.23, ...), custom_call_target="tpu_custom_call" | custom-call | bytes 8388608 | tf_op jit(solution)/shard_map/place_rows/pallas_call | solution.py:534
  453.4 129.1 %place_rows.4 = bf16[1024,2048]{1,0:T(8,128)(2,1)} custom-call(s32[3]{0:T(128)} %pad_add_fusion.place_ref, bf16[64,2048]{1,0:T(8,128)(2,1)} %pad_maximum_fusion.12.refs_0_, bf16[64,2048]{1,0:T(8,128)(2,1)} %copy-done.17, bf16[128,2048]{1,0:T(8,128)(2,1)} %collective-permute-done.21.refs_2_, bf16[64,2048]{1,0:T(8,128)(2,1)} %copy-done.22, ...), custom_call_target="tpu_custom_call" | custom-call | bytes 8388608 | tf_op jit(solution)/shard_map/place_rows/pallas_call | solution.py:534
  585.0 8.6 convolution_convert_fusion.4.gate_ref
  593.7 5.6 collective-permute-done.47
  600.6 6.7 convolution_bitcast_fusion.dn_ref
  607.4 11.8 intra.1.y_ref
  620.4 33.1 %gate_norm.1 = (bf16[1024,2048]{1,0:T(8,128)(2,1)}, bf16[1024,2048]{1,0:T(8,128)(2,1)}, bf16[1024,2048]{1,0:T(8,128)(2,1)}, bf16[1024,2048]{1,0:T(8,128)(2,1)}, ...) custom-call(f32[1024,2048]{1,0:T(8,128)} %intra.1.y_ref, ...), custom_call_target="tpu_custom_call" | custom-call | flops 1000000000 | bytes 50000000 | tf_op jit(solution)/shard_map/gate_norm/pallas_call | solution.py:754
  659.2 8.5 collective-permute-done.50
  669.3 9.3 fusion.21
  679.8 29.2 %intra_back.1 = (bf16[1024,2048]{1,0:T(8,128)(2,1)}, f32[1024,32]{1,0:T(8,128)}, f32[1024,128]{1,0:T(8,128)}, f32[1024,128]{1,0:T(8,128)}) custom-call(f32[1024,128]{1,0:T(8,128)} %get-tuple-element.41.q_ref, f32[1024,128]{1,0:T(8,128)} %get-tuple-element.42.k_ref, bf16[1024,2048]{1,0:T(8,128)(2,1)} %get-tuple-element.43.v_ref, ...), custom_call_target="tpu_custom_call" | custom-call | flops 2000000000 | bytes 40000000 | tf_op jit(solution)/shard_map/intra_back/pallas_call | solution.py:794
  710.3 37.5 %states_conv_back.1 = (bf16[1024,2336]{1,0:T(8,128)(2,1)}, f32[8,2304]{1,0:T(8,128)}, f32[40,2304]{1,0:T(8,128)}, f32[16,32]{1,0:T(8,128)}) custom-call(bf16[1024,2336]{1,0:T(8,128)(2,1)} %copy-done, bf16[1024,32]{1,0:T(8,128)(2,1)} %slice.433.raw_ref, bf16[1024,2304]{1,0:T(8,128)(2,1)} %get-tuple-element.49.z_ref, ...), custom_call_target="tpu_custom_call" | custom-call | flops 2000000000 | bytes 60000000 | tf_op jit(solution)/shard_map/states_conv_back/pallas_call | solution.py:812
  754.6 9.2 fusion.63
  763.8 6.7 fusion.12
  771.1 8.8 convolution_convert_fusion.3.src
  781.7 6.2 convolution_convert_fusion.2.src
  787.9 129.1 %pick_rows.3 = (bf16[512,2048]{1,0:T(8,128)(2,1)}, bf16[512,2048]{1,0:T(8,128)(2,1)}) custom-call(s32[3]{0:T(128)} %pad_add_fusion.place_ref, bf16[1024,2048]{1,0:T(8,128)(2,1)} %convolution_convert_fusion.3.src), custom_call_target="tpu_custom_call" | custom-call | bytes 8388608 | tf_op jit(solution)/shard_map/pick_rows/pallas_call | solution.py:567
  917.0 129.1 %pick_rows.5 = (bf16[1024,1024]{1,0:T(8,128)(2,1)}, bf16[1024,1024]{1,0:T(8,128)(2,1)}) custom-call(s32[3]{0:T(128)} %pad_add_fusion.place_ref, bf16[2048,1024]{1,0:T(8,128)(2,1)} %convolution_convert_fusion.2.src), custom_call_target="tpu_custom_call" | custom-call | bytes 8388608 | tf_op jit(solution)/shard_map/pick_rows/pallas_call | solution.py:567
  1049.5 9.9 convolution_convert_fusion
  1061.4 7.4 copy.87.src
  1068.7 152.9 %pick_rows.4 = (bf16[512,2336]{1,0:T(8,128)(2,1)}, bf16[512,2336]{1,0:T(8,128)(2,1)}) custom-call(s32[3]{0:T(128)} %pad_add_fusion.place_ref, bf16[1024,2336]{1,0:T(8,128)(2,1)} %copy.87.src), custom_call_target="tpu_custom_call" | custom-call | bytes 9568256 | tf_op jit(solution)/shard_map/pick_rows/pallas_call | solution.py:567
  1244.1 7.4 collective-permute-done.74
  1255.7 7.0 collective-permute-done.58
  1287.0 11.6 collective-permute-done.63
  1321.0 5.2 collective-permute-start.68
  (404 shorter events, 212.9 us)
Async XLA Ops:
  1.6 73.3 %collective-permute-start.23 = (bf16[32,2048]{1,0:T(8,128)(2,1)S(1)}, bf16[32,2048]{1,0:T(8,128)(2,1)S(1)}, u32[]{:S(2)}, u32[]{:S(2)}) collective-permute-start(bf16[32,2048]{1,0:T(8,128)(2,1)S(1)} %slice.351), channel_id=1, source_target_pairs={{0,3},{1,2},{2,1},{3,0},{4,7},{5,6},{6,5},{7,4},{8,11},{9,10},{10,... | collective-permute-start | bytes 393224 | tf_op jit(solution)/shard_map/ppermute | solution.py:488
  6.7 59.4 %collective-permute-start.22 = (bf16[32,2048]{1,0:T(8,128)(2,1)S(1)}, bf16[32,2048]{1,0:T(8,128)(2,1)S(1)}, u32[]{:S(2)}, u32[]{:S(2)}) collective-permute-start(bf16[32,2048]{1,0:T(8,128)(2,1)S(1)} %slice.351), channel_id=1, source_target_pairs={{0,2},{1,3},{2,0},{3,1},{4,6},{5,7},{6,4},{7,5},{8,10},{9,11},{10,... | collective-permute-start | bytes 393224 | tf_op jit(solution)/shard_map/ppermute | solution.py:488
  9.6 27.0 %collective-permute-start.18 = (bf16[8,1024]{1,0:T(8,128)(2,1)S(1)}, bf16[8,1024]{1,0:T(8,128)(2,1)S(1)}, u32[]{:S(2)}, u32[]{:S(2)}) collective-permute-start(bf16[8,1024]{1,0:T(8,128)(2,1)S(1)} %slice_bitcast_fusion), channel_id=1, source_target_pairs={{0,4},{4,8},{8,12},{12,16},{16,20},{20,24},{24,28},{1,5},{5,9},{9,... | collective-permute-start | bytes 49160 | tf_op jit(solution)/shard_map/ppermute | solution.py:483
  11.8 25.2 %collective-permute-start.5 = (bf16[32,2336]{1,0:T(8,128)(2,1)S(1)}, bf16[32,2336]{1,0:T(8,128)(2,1)S(1)}, u32[]{:S(2)}, u32[]{:S(2)}) collective-permute-start(bf16[32,2336]{1,0:T(8,128)(2,1)S(1)} %slice.337), channel_id=1, source_target_pairs={{0,1},{1,0},{2,3},{3,2},{4,5},{5,4},{6,7},{7,6},{8,9},{9,8},{10,11... | collective-permute-start | bytes 448520 | tf_op jit(solution)/shard_map/ppermute | solution.py:488
  37.1 26.7 %collective-permute-start.4 = (bf16[16,456]{1,0:T(8,128)(2,1)S(1)}, bf16[16,456]{1,0:T(8,128)(2,1)S(1)}, u32[]{:S(2)}, u32[]{:S(2)}) collective-permute-start(bf16[16,456]{1,0:T(8,128)(2,1)S(1)} %concatenate.107), channel_id=1, source_target_pairs={{0,16},{8,24},{16,0},{24,8},{1,17},{9,25},{17,1},{25,9},{2,18},{10... | collective-permute-start | bytes 43784 | tf_op jit(solution)/shard_map/ppermute | solution.py:488
  63.8 20.9 %collective-permute-start.19 = (bf16[32,2048]{1,0:T(8,128)(2,1)S(1)}, bf16[32,2048]{1,0:T(8,128)(2,1)}, u32[]{:S(2)}, u32[]{:S(2)}) collective-permute-start(bf16[32,2048]{1,0:T(8,128)(2,1)S(1)} %slice.351), channel_id=1, source_target_pairs={{0,1},{1,0},{2,3},{3,2},{4,5},{5,4},{6,7},{7,6},{8,9},{9,8},{10,11... | collective-permute-start | bytes 393224 | tf_op jit(solution)/shard_map/ppermute | solution.py:488
  75.7 20.2 %collective-permute-start.17 = (bf16[128,2336]{0,1:T(8,128)(2,1)S(1)}, bf16[128,2336]{0,1:T(8,128)(2,1)}, u32[]{:S(2)}, u32[]{:S(2)}) collective-permute-start(bf16[128,2336]{0,1:T(8,128)(2,1)S(1)} %collective-permute-done.11), channel_id=1, source_target_pairs={{0,4},{4,0},{1,5},{5,1},{2,6},{6,2},{3,7},{7,3},{8,12},{12,8},{9,1... | collective-permute-start | bytes 1794056 | tf_op jit(solution)/shard_map/ppermute | solution.py:488
  95.9 196.1 %collective-permute-start.39 = (bf16[128,1024]{1,0:T(8,128)(2,1)}, bf16[128,1024]{1,0:T(8,128)(2,1)}, u32[]{:S(2)}, u32[]{:S(2)}) collective-permute-start(bf16[128,1024]{1,0:T(8,128)(2,1)} %constant_dynamic-update-slice_fusion.4.refs_0_), channel_id=1, source_target_pairs={{0,4},{4,0},{1,5},{5,1},{2,6},{6,2},{3,7},{7,3},{8,12},{12,8},{9,1... | collective-permute-start | bytes 786440 | tf_op jit(solution)/shard_map/ppermute | solution.py:488
  98.1 191.3 %collective-permute-start.33 = (bf16[128,1024]{1,0:T(8,128)(2,1)}, bf16[128,1024]{1,0:T(8,128)(2,1)}, u32[]{:S(2)}, u32[]{:S(2)}) collective-permute-start(bf16[128,1024]{1,0:T(8,128)(2,1)} %constant_dynamic-update-slice_fusion.4.refs_0_), channel_id=1, source_target_pairs={{0,8},{8,0},{16,24},{24,16},{1,9},{9,1},{17,25},{25,17},{2,10},{10... | collective-permute-start | bytes 786440 | tf_op jit(solution)/shard_map/ppermute | solution.py:488
  99.1 187.4 %collective-permute-start.24 = (bf16[64,2048]{1,0:T(8,128)(2,1)}, bf16[64,2048]{1,0:T(8,128)(2,1)}, u32[]{:S(2)}, u32[]{:S(2)}) collective-permute-start(bf16[64,2048]{1,0:T(8,128)(2,1)} %copy-done.22), channel_id=1, source_target_pairs={{0,16},{8,24},{16,0},{24,8},{1,17},{9,25},{17,1},{25,9},{2,18},{10... | collective-permute-start | bytes 786440 | tf_op jit(solution)/shard_map/ppermute | solution.py:488
  100.6 187.2 %collective-permute-start.37 = (bf16[128,1024]{1,0:T(8,128)(2,1)}, bf16[128,1024]{1,0:T(8,128)(2,1)S(1)}, u32[]{:S(2)}, u32[]{:S(2)}) collective-permute-start(bf16[128,1024]{1,0:T(8,128)(2,1)} %copy-done.23), channel_id=1, source_target_pairs={{0,16},{8,24},{16,0},{24,8},{1,17},{9,25},{17,1},{25,9},{2,18},{10... | collective-permute-start | bytes 786440 | tf_op jit(solution)/shard_map/ppermute | solution.py:488
  101.1 189.3 %collective-permute-start.20 = (bf16[64,2048]{1,0:T(8,128)(2,1)}, bf16[64,2048]{1,0:T(8,128)(2,1)S(1)}, u32[]{:S(2)}, u32[]{:S(2)}) collective-permute-start(bf16[64,2048]{1,0:T(8,128)(2,1)} %pad_maximum_fusion.12.refs_0_), channel_id=1, source_target_pairs={{0,8},{8,0},{16,24},{24,16},{1,9},{9,1},{17,25},{25,17},{2,10},{10... | collective-permute-start | bytes 786440 | tf_op jit(solution)/shard_map/ppermute | solution.py:488
  294.7 22.5 %collective-permute-start.21 = (bf16[128,2048]{1,0:T(8,128)(2,1)S(1)}, bf16[128,2048]{1,0:T(8,128)(2,1)}, u32[]{:S(2)}, u32[]{:S(2)}) collective-permute-start(bf16[128,2048]{1,0:T(8,128)(2,1)S(1)} %pad_maximum_fusion.5), channel_id=1, source_target_pairs={{0,16},{8,24},{16,0},{24,8},{1,17},{9,25},{17,1},{25,9},{2,18},{10... | collective-permute-start | bytes 1572872 | tf_op jit(solution)/shard_map/ppermute | solution.py:488
  295.4 24.6 %collective-permute-start.25 = (bf16[128,2048]{1,0:T(8,128)(2,1)S(1)}, bf16[128,2048]{1,0:T(8,128)(2,1)}, u32[]{:S(2)}, u32[]{:S(2)}) collective-permute-start(bf16[128,2048]{1,0:T(8,128)(2,1)S(1)} %pad_maximum_fusion.6), channel_id=1, source_target_pairs={{0,8},{8,0},{16,24},{24,16},{1,9},{9,1},{17,25},{25,17},{2,10},{10... | collective-permute-start | bytes 1572872 | tf_op jit(solution)/shard_map/ppermute | solution.py:488
  309.6 273.0 %collective-permute-start.46 = (f32[130,1024]{1,0:T(8,128)}, f32[130,1024]{1,0:T(8,128)}, u32[]{:S(2)}, u32[]{:S(2)}) collective-permute-start(f32[130,1024]{1,0:T(8,128)} %pad_maximum_fusion.3), channel_id=1, source_target_pairs={{0,8},{8,0},{16,24},{24,16},{1,9},{9,1},{17,25},{25,17},{2,10},{10... | collective-permute-start | bytes 1597448 | tf_op jit(solution)/shard_map/ppermute | solution.py:458
  317.2 136.2 %collective-permute-start.28 = (bf16[128,2048]{1,0:T(8,128)(2,1)}, bf16[128,2048]{1,0:T(8,128)(2,1)}, u32[]{:S(2)}, u32[]{:S(2)}) collective-permute-start(bf16[128,2048]{1,0:T(8,128)(2,1)} %collective-permute-done.21.refs_2_), channel_id=1, source_target_pairs={{0,4},{4,0},{1,5},{5,1},{2,6},{6,2},{3,7},{7,3},{8,12},{12,8},{9,1... | collective-permute-start | bytes 1572872 | tf_op jit(solution)/shard_map/ppermute | solution.py:488
  319.9 133.5 %collective-permute-start.31 = (bf16[128,2048]{1,0:T(8,128)(2,1)}, bf16[128,2048]{1,0:T(8,128)(2,1)}, u32[]{:S(2)}, u32[]{:S(2)}) collective-permute-start(bf16[128,2048]{1,0:T(8,128)(2,1)} %collective-permute-done.25.refs_5_), channel_id=1, source_target_pairs={{0,4},{4,0},{1,5},{5,1},{2,6},{6,2},{3,7},{7,3},{8,12},{12,8},{9,1... | collective-permute-start | bytes 1572872 | tf_op jit(solution)/shard_map/ppermute | solution.py:488
  320.0 133.4 %collective-permute-start.30 = (bf16[64,2048]{1,0:T(8,128)(2,1)}, bf16[64,2048]{1,0:T(8,128)(2,1)}, u32[]{:S(2)}, u32[]{:S(2)}) collective-permute-start(bf16[64,2048]{1,0:T(8,128)(2,1)} %collective-permute-done.24.refs_4_), channel_id=1, source_target_pairs={{0,4},{4,0},{1,5},{5,1},{2,6},{6,2},{3,7},{7,3},{8,12},{12,8},{9,1... | collective-permute-start | bytes 786440 | tf_op jit(solution)/shard_map/ppermute | solution.py:488
  321.6 131.9 %collective-permute-start.27 = (bf16[64,2048]{1,0:T(8,128)(2,1)}, bf16[64,2048]{1,0:T(8,128)(2,1)}, u32[]{:S(2)}, u32[]{:S(2)}) collective-permute-start(bf16[64,2048]{1,0:T(8,128)(2,1)} %copy-done.17), channel_id=1, source_target_pairs={{0,4},{4,0},{1,5},{5,1},{2,6},{6,2},{3,7},{7,3},{8,12},{12,8},{9,1... | collective-permute-start | bytes 786440 | tf_op jit(solution)/shard_map/ppermute | solution.py:488
  600.5 18.7 %collective-permute-start.48 = (f32[128,1024]{1,0:T(8,128)S(1)}, f32[128,1024]{1,0:T(8,128)S(1)}, u32[]{:S(2)}, u32[]{:S(2)}) collective-permute-start(f32[128,1024]{1,0:T(8,128)S(1)} %get-tuple-element.108), channel_id=1, source_target_pairs={{0,4},{4,0},{1,5},{5,1},{2,6},{6,2},{3,7},{7,3},{8,12},{12,8},{9,1... | collective-permute-start | bytes 1572872 | tf_op jit(solution)/shard_map/ppermute | solution.py:471
  679.5 29.6 %collective-permute-start.52 = (bf16[128,1024]{1,0:T(8,128)(2,1)}, bf16[128,1024]{1,0:T(8,128)(2,1)S(1)}, u32[]{:S(2)}, u32[]{:S(2)}) collective-permute-start(bf16[128,1024]{1,0:T(8,128)(2,1)} %get-tuple-element.110), channel_id=1, source_target_pairs={{0,4},{4,0},{1,5},{5,1},{2,6},{6,2},{3,7},{7,3},{8,12},{12,8},{9,1... | collective-permute-start | bytes 786440 | tf_op jit(solution)/shard_map/ppermute | solution.py:471
  779.9 269.0 %collective-permute-start.79 = (f32[32,552]{1,0:T(8,128)S(1)}, f32[32,552]{1,0:T(8,128)S(1)}, u32[]{:S(2)}, u32[]{:S(2)}) collective-permute-start(f32[32,552]{1,0:T(8,128)S(1)} %fusion.77), channel_id=1, source_target_pairs={{0,2},{1,3},{2,0},{3,1},{4,6},{5,7},{6,4},{7,5},{8,10},{9,11},{10,... | collective-permute-start | bytes 211976 | tf_op jit(solution)/shard_map/ppermute | solution.py:488
  1046.1 187.0 %collective-permute-start.70 = (bf16[1024,1024]{1,0:T(8,128)(2,1)}, bf16[1024,1024]{1,0:T(8,128)(2,1)}, u32[]{:S(2)}, u32[]{:S(2)}) collective-permute-start(bf16[1024,1024]{1,0:T(8,128)(2,1)} %get-tuple-element.67), channel_id=1, source_target_pairs={{0,4},{4,0},{1,5},{5,1},{2,6},{6,2},{3,7},{7,3},{8,12},{12,8},{9,1... | collective-permute-start | bytes 6291464 | tf_op jit(solution)/shard_map/ppermute | solution.py:488
  1048.9 189.7 %collective-permute-start.54 = (bf16[512,2048]{1,0:T(8,128)(2,1)}, bf16[512,2048]{1,0:T(8,128)(2,1)}, u32[]{:S(2)}, u32[]{:S(2)}) collective-permute-start(bf16[512,2048]{1,0:T(8,128)(2,1)} %get-tuple-element.63), channel_id=1, source_target_pairs={{0,4},{4,0},{1,5},{5,1},{2,6},{6,2},{3,7},{7,3},{8,12},{12,8},{9,1... | collective-permute-start | bytes 6291464 | tf_op jit(solution)/shard_map/ppermute | solution.py:488
  1059.4 166.7 %collective-permute-start.81 = (f32[32,552]{1,0:T(8,128)S(1)}, f32[32,552]{1,0:T(8,128)S(1)}, u32[]{:S(2)}, u32[]{:S(2)}) collective-permute-start(f32[32,552]{1,0:T(8,128)S(1)} %add.235), channel_id=1, source_target_pairs={{0,8},{8,0},{16,24},{24,16},{1,9},{9,1},{17,25},{25,17},{2,10},{10... | collective-permute-start | bytes 211976 | tf_op jit(solution)/shard_map/ppermute | solution.py:488
  1226.1 48.3 %collective-permute-start.62 = (bf16[512,2336]{0,1:T(8,128)(2,1)}, bf16[512,2336]{0,1:T(8,128)(2,1)}, u32[]{:S(2)}, u32[]{:S(2)}) collective-permute-start(bf16[512,2336]{0,1:T(8,128)(2,1)} %copy.88), channel_id=1, source_target_pairs={{0,4},{4,0},{1,5},{5,1},{2,6},{6,2},{3,7},{7,3},{8,12},{12,8},{9,1... | collective-permute-start | bytes 7176200 | tf_op jit(solution)/shard_map/ppermute | solution.py:488
  1241.2 21.5 %collective-permute-start.58 = (bf16[128,2048]{1,0:T(8,128)(2,1)S(1)}, bf16[128,2048]{1,0:T(8,128)(2,1)S(1)}, u32[]{:S(2)}, u32[]{:S(2)}) collective-permute-start(bf16[128,2048]{1,0:T(8,128)(2,1)S(1)} %get-tuple-element.103), channel_id=1, source_target_pairs={{0,8},{8,0},{16,24},{24,16},{1,9},{9,1},{17,25},{25,17},{2,10},{10... | collective-permute-start | bytes 1572872 | tf_op jit(solution)/shard_map/ppermute | solution.py:488
  1243.2 21.2 %collective-permute-start.55 = (bf16[128,2048]{1,0:T(8,128)(2,1)S(1)}, bf16[128,2048]{1,0:T(8,128)(2,1)S(1)}, u32[]{:S(2)}, u32[]{:S(2)}) collective-permute-start(bf16[128,2048]{1,0:T(8,128)(2,1)S(1)} %get-tuple-element.104), channel_id=1, source_target_pairs={{0,16},{8,24},{16,0},{24,8},{1,17},{9,25},{17,1},{25,9},{2,18},{10... | collective-permute-start | bytes 1572872 | tf_op jit(solution)/shard_map/ppermute | solution.py:488
  1265.9 19.5 %collective-permute-start.59 = (bf16[64,2048]{1,0:T(8,128)(2,1)}, bf16[64,2048]{1,0:T(8,128)(2,1)}, u32[]{:S(2)}, u32[]{:S(2)}) collective-permute-start(bf16[64,2048]{1,0:T(8,128)(2,1)} %slice.664), channel_id=1, source_target_pairs={{0,16},{8,24},{16,0},{24,8},{1,17},{9,25},{17,1},{25,9},{2,18},{10... | collective-permute-start | bytes 786440 | tf_op jit(solution)/shard_map/ppermute | solution.py:488
  1269.2 57.0 %collective-permute-start.73 = (bf16[64,1024]{1,0:T(8,128)(2,1)}, bf16[64,1024]{1,0:T(8,128)(2,1)}, u32[]{:S(2)}, u32[]{:S(2)}) collective-permute-start(bf16[64,1024]{1,0:T(8,128)(2,1)} %slice.667), channel_id=1, source_target_pairs={{0,1},{1,0},{2,3},{3,2},{4,5},{5,4},{6,7},{7,6},{8,9},{9,8},{10,11... | collective-permute-start | bytes 393224 | tf_op jit(solution)/shard_map/ppermute | solution.py:488
  1270.7 56.4 %collective-permute-start.76 = (bf16[64,1024]{1,0:T(8,128)(2,1)}, bf16[64,1024]{1,0:T(8,128)(2,1)}, u32[]{:S(2)}, u32[]{:S(2)}) collective-permute-start(bf16[64,1024]{1,0:T(8,128)(2,1)} %get-tuple-element.115), channel_id=1, source_target_pairs={{0,2},{1,3},{2,0},{3,1},{4,6},{5,7},{6,4},{7,5},{8,10},{9,11},{10,... | collective-permute-start | bytes 393224 | tf_op jit(solution)/shard_map/ppermute | solution.py:488
  1274.0 34.9 %collective-permute-start.57 = (bf16[32,2048]{1,0:T(8,128)(2,1)}, bf16[32,2048]{1,0:T(8,128)(2,1)}, u32[]{:S(2)}, u32[]{:S(2)}) collective-permute-start(bf16[32,2048]{1,0:T(8,128)(2,1)} %slice.668), channel_id=1, source_target_pairs={{0,1},{1,0},{2,3},{3,2},{4,5},{5,4},{6,7},{7,6},{8,9},{9,8},{10,11... | collective-permute-start | bytes 393224 | tf_op jit(solution)/shard_map/ppermute | solution.py:488
  (96 other events, 1296.9 us)

commit v2 on v1

--- a/solution.py
+++ b/solution.py
@@ -28,6 +28,8 @@
 PARAMS = pltpu.CompilerParams(
     dimension_semantics=("arbitrary",), vmem_limit_bytes=56 * 1024 * 1024
 )
+
+PLAIN = pltpu.CompilerParams(vmem_limit_bytes=56 * 1024 * 1024)
 
 
 def mm(a, b, dims=NN):
@@ -508,75 +510,82 @@
     return ((place_ref[0] ^ mask) * 2 + (place_ref[1] ^ flip)) * fsdp + (place_ref[2] ^ k)
 
 
-def place_rows(place, pieces_in, r, fsdp, total):
-    jobs = [
-        (i, at, mask, flip, k)
-        for i, (_, flip, ids) in enumerate(pieces_in)
-        for at, (mask, k) in enumerate(ids)
-    ]
-
+def place_rows(place, held, r, fsdp, total):
     def body(place_ref, *refs):
-        dst, sem = refs[-2], refs[-1]
-        copies = []
-        for j, (i, at, mask, flip, k) in enumerate(jobs):
-            row = pl.multiple_of(shard_of(place_ref, fsdp, mask, flip, k) * r, r)
-            copies.append(
-                pltpu.make_async_copy(
-                    refs[i].at[pl.ds(at * r, r)], dst.at[pl.ds(row, r)], sem.at[j]
-                )
-            )
-            copies[-1].start()
-        for copy in copies:
-            copy.wait()
-
-    arrays = [a for a, _, _ in pieces_in]
+        dst = refs[-1]
+        for src, (_, flip, ids) in zip(refs, held):
+            for at, (mask, k) in enumerate(ids):
+                row = pl.multiple_of(shard_of(place_ref, fsdp, mask, flip, k) * r, r)
+                dst[pl.ds(row, r), :] = src[at * r : (at + 1) * r, :]
+
+    arrays = [a for a, _, _ in held]
     cols = arrays[0].shape[1]
     return pl.pallas_call(
         body,
         name="place_rows",
         in_specs=[pl.BlockSpec(memory_space=pltpu.SMEM)]
-        + [pl.BlockSpec(memory_space=pl.ANY)] * len(arrays),
-        out_specs=pl.BlockSpec(memory_space=pl.ANY),
+        + [pl.BlockSpec(memory_space=pltpu.VMEM)] * len(arrays),
+        out_specs=pl.BlockSpec(memory_space=pltpu.VMEM),
         out_shape=jax.ShapeDtypeStruct((total, cols), arrays[0].dtype),
-        scratch_shapes=[pltpu.SemaphoreType.DMA((len(jobs),))],
-        cost_estimate=pl.CostEstimate(
-            flops=0, bytes_accessed=4 * total * cols, transcendentals=0
-        ),
+        compiler_params=PLAIN,
+        cost_estimate=cost(0, 4 * total * cols),
     )(place, *arrays)
 
 
-def pick_rows(place, whole_rows, r, pairs, fsdp):
+def pick_rows(place, arrays, r, pairs, fsdp):
     order = [i for ids in part_ids(pairs, fsdp) for i in ids]
     half = len(order) * r
-    cols = whole_rows.shape[1]
-
-    def body(place_ref, src, keep, give, sem):
-        copies = []
-        for flip, dst in ((1, give), (0, keep)):
+    repeat = [a.shape[0] // (2 * half) for a in arrays]
+    cols = sum(a.shape[1] * n for a, n in zip(arrays, repeat))
+
+    def body(place_ref, *refs):
+        for flip, dst in ((1, refs[-1]), (0, refs[-2])):
             for at, (mask, k) in enumerate(order):
-                row = pl.multiple_of(shard_of(place_ref, fsdp, mask, flip, k) * r, r)
-                copies.append(
-                    pltpu.make_async_copy(
-                        src.at[pl.ds(row, r)], dst.at[pl.ds(at * r, r)], sem.at[len(copies)]
-                    )
-                )
-                copies[-1].start()
-        for copy in copies:
-            copy.wait()
+                index = shard_of(place_ref, fsdp, mask, flip, k)
+                col = 0
+                for src, n in zip(refs, repeat):
+                    for m in range(n):
+                        row = pl.multiple_of((index * n + m) * r, r)
+                        width = src.shape[1]
+                        dst[at * r : (at + 1) * r, col : col + width] = src[pl.ds(row, r), :]
+                        col += width
 
     return pl.pallas_call(
         body,
         name="pick_rows",
-        in_specs=[
-            pl.BlockSpec(memory_space=pltpu.SMEM), pl.BlockSpec(memory_space=pl.ANY),
-        ],
-        out_specs=[pl.BlockSpec(memory_space=pl.ANY)] * 2,
-        out_shape=[jax.ShapeDtypeStruct((half, cols), whole_rows.dtype)] * 2,
-        scratch_shapes=[pltpu.SemaphoreType.DMA((2 * len(order),))],
-        cost_estimate=pl.CostEstimate(
-            flops=0, bytes_accessed=8 * half * cols, transcendentals=0
-        ),
-    )(place, whole_rows)
+        in_specs=[pl.BlockSpec(memory_space=pltpu.SMEM)]
+        + [pl.BlockSpec(memory_space=pltpu.VMEM)] * len(arrays),
+        out_specs=[pl.BlockSpec(memory_space=pltpu.VMEM)] * 2,
+        out_shape=[jax.ShapeDtypeStruct((half, cols), arrays[0].dtype)] * 2,
+        compiler_params=PLAIN,
+        cost_estimate=cost(0, 8 * half * cols),
+    )(place, *arrays)
+
+
+def unpack_weights(packed, r):
+    total, model = packed.shape[0], (packed.shape[1] - DI) // 2
+    if r % 16:
+        tail = packed[:, DI:].reshape(total // r, r, 2, model).transpose(0, 2, 1, 3)
+        return packed[:, :DI], tail.reshape(2 * total, model)
+    per = min(total, 256)
+
+    def body(src, gate, out):
+        gate[...] = src[:, :DI]
+        for i in range(per // r):
+            for m in range(2):
+                at, col = (2 * i + m) * r, DI + m * model
+                out[at : at + r, :] = src[i * r : (i + 1) * r, col : col + model]
+
+    return pl.pallas_call(
+        body,
+        name="unpack_weights",
+        grid=(total // per,),
+        in_specs=[rows(packed.shape[1], per=per)],
+        out_specs=[rows(DI, per=per), rows(model, per=2 * per)],
+        out_shape=[shape((total, DI), BF), shape((2 * total, model), BF)],
+        compiler_params=PARAMS,
+        cost_estimate=cost(0, 4 * total * packed.shape[1]),
+    )(packed)
 
 
 def gather_rows(w, place, pairs):
@@ -588,40 +597,48 @@
     for part, order in enumerate(bit_orders(pairs)):
         ks = range(part * fsdp // 2, (part + 1) * fsdp // 2)
         block = jnp.concatenate([line[k] for k in ks], axis=0)
-        ids = [(0, k) for k in ks]
-        held.append((block, 0, ids))
         for b in order:
-            got = swap(block, "pair", 1 << b)
-            got_ids = [(mask ^ (1 << b), k) for mask, k in ids]
-            held.append((got, 0, got_ids))
-            block = jnp.concatenate([block, got], axis=0)
-            ids = ids + got_ids
+            block = jnp.concatenate([block, swap(block, "pair", 1 << b)], axis=0)
+        held.append((block, 0, part_ids(pairs, fsdp)[part]))
     held = held + [(swap(a, "core", 1), 1, ids) for a, _, ids in held]
     return place_rows(place, held, r, fsdp, 2 * pairs * fsdp * r)
 
 
-def reduce_rows(g, place, pairs):
+def reduce_rows(arrays, place, pairs):
     fsdp = lax.axis_size("fsdp")
-    r = g.shape[0] // (2 * pairs * fsdp)
+    r = arrays[0].shape[0] // (2 * pairs * fsdp)
     if r % 16:
-        return lax.psum_scatter(g.astype(F32), ALL, scatter_dimension=0, tiled=True)
-    keep, give = pick_rows(place, g, r, pairs, fsdp)
-    summed = keep.astype(F32) + swap(give, "core", 1).astype(F32)
-    half = summed.shape[0] // 2
+        return [
+            lax.psum_scatter(g.astype(F32), ALL, scatter_dimension=0, tiled=True) for g in arrays
+        ]
+    keep, give = pick_rows(place, arrays, r, pairs, fsdp)
+    got = swap(give, "core", 1)
+    half = keep.shape[0] // 2
     ends = []
     for part, order in enumerate(bit_orders(pairs)):
-        block = summed[part * half : (part + 1) * half]
+        at = slice(part * half, (part + 1) * half)
+        block = keep[at].astype(F32) + got[at].astype(F32)
         for b in reversed(order):
             cut = block.shape[0] // 2
-            got = swap(block[cut:].astype(BF), "pair", 1 << b)
-            block = block[:cut] + got.astype(F32)
+            other = swap(block[cut:].astype(BF), "pair", 1 << b)
+            block = block[:cut] + other.astype(F32)
         ends.append(block)
     total = ends[0][:r]
     for k in range(1, fsdp):
         at = (k % (fsdp // 2)) * r
         block = ends[k // (fsdp // 2)][at : at + r]
         total = total + swap(block.astype(BF), "fsdp", k).astype(F32)
-    return total
+    out, col = [], 0
+    for g in arrays:
+        width = g.shape[1]
+        count = g.shape[0] // arrays[0].shape[0]
+        out.append(
+            jnp.concatenate(
+                [total[:, col + m * width : col + (m + 1) * width] for m in range(count)], axis=0
+            )
+        )
+        col += count * width
+    return out
 
 
 def links(pairs, fsdp):
@@ -676,8 +693,12 @@
     at += own[2]
     gate_full = small[:, at :].reshape(1, DI).astype(F32)
     w_mix = gather_rows(in_weight[:, DI:], place, pairs)
-    w_gate = gather_rows(in_weight[:, :DI], place, pairs)
-    w_out = gather_rows(out_weight, place, pairs)
+    r = in_weight.shape[0]
+    packed_weights = jnp.concatenate(
+        [in_weight[:, :DI], out_weight[:r], out_weight[r:]], axis=1
+    )
+    packed_weights = lax.all_gather(packed_weights, ALL, axis=0, tiled=True)
+    w_gate, w_out = unpack_weights(packed_weights, r)
 
     expand = jnp.asarray(np.repeat(np.eye(HEADS), HEADDIM, axis=1), BF)
     skip_wide = jnp.repeat(skip_gain, HEADDIM)[None]
@@ -784,9 +805,8 @@
     coming_back = carry_states(packed_back, pairs, True)
 
     grad_out_w = lax.dot_general(normed, upstream, TN, preferred_element_type=F32).astype(BF)
-    out_shard = reduce_rows(grad_out_w, place, pairs)
     grad_gate_w = lax.dot_general(hidden, dgate, TN, preferred_element_type=F32).astype(BF)
-    gate_shard = reduce_rows(grad_gate_w, place, pairs)
+    gate_shard, out_shard = reduce_rows([grad_gate_w, grad_out_w], place, pairs)
     block_out = (
         tokens.astype(F32) + jnp.dot(normed, w_out, preferred_element_type=F32)
     ).astype(BF)
@@ -844,7 +864,7 @@
     fixed = (grad_mix[count - 8 :].astype(F32) + edge).astype(BF)
     grad_mix = lax.dynamic_update_slice(grad_mix, fixed, (count - 8, 0))
     grad_mix_w = lax.dot_general(hidden, grad_mix, TN, preferred_element_type=F32).astype(BF)
-    mix_shard = reduce_rows(grad_mix_w, place, pairs)
+    (mix_shard,) = reduce_rows([grad_mix_w], place, pairs)
     grad_hidden = lax.dot_general(dgate, w_gate, NT, preferred_element_type=F32)
     grad_hidden = grad_hidden + lax.dot_general(grad_mix, w_mix, NT, preferred_element_type=F32)
 

time: 1340 us -> 518 us (0.39)
  Pallas kernels: 953 us -> 155 us
  starting transfers between devices: 80.8 us -> 58.4 us
    pallas_call x3 -> x1, Pallas kernels: 411 us -> 5.35 us  [place_rows(): pl.pallas_call(body, name='place_rows', in_specs=[pl.BlockSpec(memory_spa...]
    pallas_call x3 -> x2, Pallas kernels: 411 us -> 12.5 us  [pick_rows(): pl.pallas_call(body, name='pick_rows', in_specs=[pl.BlockSpec(memory_spac...]
    ppermute x73 -> x35, starting transfers between devices: 75.3 us -> 48.6 us  [swap(): return lax.ppermute(block, axis, [(i, i ^ mask) for i in range(count)])]
    ppermute x73 -> x35, waiting for transfers between devices: 98.3 us -> 79 us  [swap(): return lax.ppermute(block, axis, [(i, i ^ mask) for i in range(count)])]
  transfers between devices with their start and end apart: 83 -> 46, of which waited for: 28 -> 21; matrix products, arithmetic and copies ran while one was open for 11% -> 26% of each run, Pallas kernels for 66% -> 15%
where the time goes in v2:
time: 518 us; the launch traced here: 513 us
  Pallas kernels  155 us (30%)
  waiting for transfers between devices  111 us (21%)
  matrix products  78.2 us (15%)
  starting transfers between devices  58.4 us (11%)
  local copies, waits for them, and re-layouts  51.4 us (10%)
  other arithmetic  43.8 us (8%)
  between operations  15 us (3%)
    ppermute x35, waiting for transfers between devices, swap(): return lax.ppermute(block, axis, [(i, i ^ mask) for i in range(count)])  79 us
    ppermute x35, starting transfers between devices, swap(): return lax.ppermute(block, axis, [(i, i ^ mask) for i in range(count)])  48.6 us
    pallas_call x1, Pallas kernels, on_device(): pl.pallas_call(back_kernel, name='states_conv_back', grid=(chunks,), in_s...  37.3 us
    pallas_call x1, Pallas kernels, on_device(): pl.pallas_call(gate_kernel, name='gate_norm', grid=(chunks,), in_specs=[r...  33.1 us
    pallas_call x1, Pallas kernels, on_device(): pl.pallas_call(intra_back_kernel, name='intra_back', grid=(chunks,), in_s...  29.4 us
    ppermute x4, waiting for transfers between devices, carry_states(): lax.ppermute(pack(total, total_thru, packed.dtype), 'pair', route)  26.8 us
    pallas_call x1, Pallas kernels, on_device(): pl.pallas_call(prep_kernel, name='conv_states', grid=(chunks,), in_specs=...  18.9 us
    pallas_call x2, Pallas kernels, pick_rows(): pl.pallas_call(body, name='pick_rows', in_specs=[pl.BlockSpec(memory_spac...  12.5 us
  transfers between devices with their start and end apart: 46, of which 21 were waited for; matrix products, arithmetic and copies ran while one was open for 26% of the time, Pallas kernels for 15%

profile of v2, /device:TPU:0, one launch (start us, length us, event | category | flops | bytes accessed | tf_op | source)
XLA Modules:
  0.0 513.1 jit_solution(13423948604175683235)
XLA Ops:
  10.7 5.1 collective-permute-start.9
  36.7 4.3 collective-permute-done.10
  47.8 14.7 %collective-permute-done.11 = bf16[128,2336]{0,1:T(8,128)(2,1)S(1)} collective-permute-done((bf16[128,2336]{0,1:T(8,128)(2,1)S(1)}, bf16[128,2336]{0,1:T(8,128)(2,1)S(1)}, u32[]{:S(2)}, u32[]{:S(2)}) %collective-permute-start.11) | collective-permute-done | bytes 598048 | tf_op jit(solution)/shard_map/ppermute | solution.py:490
  85.8 5.4 %place_rows.1 = bf16[1024,2336]{1,0:T(8,128)(2,1)} custom-call(s32[3]{0:T(128)} %pad_add_fusion.place_ref, bf16[256,2336]{1,0:T(8,128)(2,1)} %copy-done.3, bf16[256,2336]{1,0:T(8,128)(2,1)} %copy-done.2, bf16[256,2336]{1,0:T(8,128)(2,1)} %copy.79.refs_2_, bf16[256,2336]{1,0:T(8,128)(2,1)} %copy.80.refs_3_), custom_call_target="tpu_custom_call" | custom-call | bytes 9568256 | tf_op jit(solution)/shard_map/place_rows/pallas_call | solution.py:523
  91.2 8.6 %convolution_convert_fusion.1.x_ref = bf16[1024,2336]{1,0:T(8,128)(2,1)S(1)} fusion(bf16[1024,2336]{1,0:T(8,128)(2,1)} %place_rows.1, bf16[1,1024,1024]{2,1,0:T(8,128)(2,1)S(1)} %copy-done.4, f32[1024]{0:T(1024)S(1)} %mul.194, f32[1024]{0:T(1024)S(1)} %add_rsqrt_fusion), kind=kOutput, calls=%fused_computation.8 | convolution fusion | flops 4905533440 | bytes 11673600 | tf_op jit(solution)/shard_map/dot_general | solution.py:727
  102.1 18.9 %conv_states.1 = (bf16[1024,2304]{1,0:T(8,128)(2,1)}, bf16[1024,2048]{1,0:T(8,128)(2,1)}, f32[1024,128]{1,0:T(8,128)}, f32[1024,128]{1,0:T(8,128)}, f32[1024,32]...) custom-call(bf16[1024,2336]{1,0:T(8,128)(2,1)} %copy-done, bf16[1024,32]{1,0:T(8,128)(2,1)} %slice.412.raw_ref, ...), custom_call_target="tpu_custom_call" | custom-call | flops 1000000000 | bytes 30000000 | tf_op jit(solution)/shard_map/conv_states/pallas_call | solution.py:732
  127.9 13.7 %collective-permute-done.16 = f32[130,1024]{1,0:T(8,128)} collective-permute-done((f32[130,1024]{1,0:T(8,128)}, f32[130,1024]{1,0:T(8,128)}, u32[]{:S(2)}, u32[]{:S(2)}) %collective-permute-start.16) | collective-permute-done | bytes 532512 | tf_op jit(solution)/shard_map/ppermute | solution.py:460
  146.7 12.4 %collective-permute-done.17 = f32[130,1024]{1,0:T(8,128)} collective-permute-done((f32[130,1024]{1,0:T(8,128)}, f32[130,1024]{1,0:T(8,128)}, u32[]{:S(2)}, u32[]{:S(2)}) %collective-permute-start.17) | collective-permute-done | bytes 532512 | tf_op jit(solution)/shard_map/ppermute | solution.py:460
  162.8 11.5 %intra.1.y_ref = f32[1024,2048]{1,0:T(8,128)} custom-call(f32[1024,128]{1,0:T(8,128)} %get-tuple-element.41.q_ref, f32[1024,128]{1,0:T(8,128)} %get-tuple-element.42.k_ref, bf16[1024,2048]{1,0:T(8,128)(2,1)} %get-tuple-element.43.v_ref, f32[1024,32]{1,0:T(8,128)} %get-tuple-element.44.rc_ref, f32[256,128]{1,0:T(8,128)} %get-tuple-element.45.rs_ref, ...), custom_call_target="tpu_custom_call" | custom-call | flops 1000000000 | bytes 30000000 | tf_op jit(solution)/shard_map/intra/pallas_call | solution.py:758
  175.4 7.1 %unpack_weights.1 = (bf16[1024,2048]{1,0:T(8,128)(2,1)}, bf16[2048,1024]{1,0:T(8,128)(2,1)}) custom-call(bf16[1024,4096]{1,0:T(8,128)(2,1)} %all-gather.2.cloned.1.call-done.src), custom_call_target="tpu_custom_call" | custom-call | bytes 16777216 | tf_op jit(solution)/shard_map/unpack_weights/pallas_call | solution.py:579
  182.5 8.6 %convolution_convert_fusion.4.gate_ref = bf16[1024,2048]{1,0:T(8,128)(2,1)} fusion(bf16[1024,2048]{1,0:T(8,128)(2,1)} %get-tuple-element.46, bf16[1,1024,1024]{2,1,0:T(8,128)(2,1)S(1)} %copy-done.4, f32[1024]{0:T(1024)S(1)} %mul.194, f32[1024]{0:T(1024)S(1)} %add_rsqrt_fusion), kind=kOutput, calls=%fused_computation.25 | convolution fusion | flops 4301258752 | bytes 10493952 | tf_op jit(solution)/shard_map/dot_general | solution.py:772
  191.1 7.3 %convolution_bitcast_fusion.dn_ref = f32[1024,2048]{1,0:T(8,128)} fusion(bf16[2048,1024]{1,0:T(8,128)(2,1)S(1)} %copy-done.17, bf16[1,1024,1024]{2,1,0:T(8,128)(2,1)S(1)} %copy-done.8), kind=kOutput, calls=%fused_computation.11 | convolution fusion | flops 4294967296 | bytes 14680064 | tf_op jit(solution)/shard_map/dot_general | solution.py:773
  198.4 33.1 %gate_norm.1 = (bf16[1024,2048]{1,0:T(8,128)(2,1)}, bf16[1024,2048]{1,0:T(8,128)(2,1)}, bf16[1024,2048]{1,0:T(8,128)(2,1)}, bf16[1024,2048]{1,0:T(8,128)(2,1)}, ...) custom-call(f32[1024,2048]{1,0:T(8,128)} %intra.1.y_ref, ...), custom_call_target="tpu_custom_call" | custom-call | flops 1000000000 | bytes 50000000 | tf_op jit(solution)/shard_map/gate_norm/pallas_call | solution.py:775
  236.9 9.4 %fusion.21 = bf16[1,1024,1024]{2,1,0:T(8,128)(2,1)} fusion(bf16[1,1024,1024]{2,1,0:T(8,128)(2,1)S(1)} %copy-done.4, bf16[1024,2048]{1,0:T(8,128)(2,1)} %get-tuple-element.49, bf16[2048,1024]{1,0:T(8,128)(2,1)} %get-tuple-element.47), kind=kOutput, calls=%fused_computation.30 | convolution fusion | flops 4298113024 | bytes 12582912 | tf_op jit(solution)/shard_map/dot_general | solution.py:811
  248.5 6.1 %fusion.56 = f32[1024,1024]{1,0:T(8,128)} fusion(bf16[1024,2048]{1,0:T(8,128)(2,1)S(1)} %copy-done.15, bf16[1024,2048]{1,0:T(8,128)(2,1)S(1)} %copy-done.16), kind=kOutput, calls=%fused_computation.171 | convolution fusion | flops 4294967296 | bytes 12582912 | tf_op jit(solution)/shard_map/dot_general | solution.py:868
  256.0 29.4 %intra_back.1 = (bf16[1024,2048]{1,0:T(8,128)(2,1)}, f32[1024,32]{1,0:T(8,128)}, f32[1024,128]{1,0:T(8,128)}, f32[1024,128]{1,0:T(8,128)}) custom-call(f32[1024,128]{1,0:T(8,128)} %get-tuple-element.41.q_ref, f32[1024,128]{1,0:T(8,128)} %get-tuple-element.42.k_ref, bf16[1024,2048]{1,0:T(8,128)(2,1)} %get-tuple-element.43.v_ref, ...), custom_call_target="tpu_custom_call" | custom-call | flops 2000000000 | bytes 40000000 | tf_op jit(solution)/shard_map/intra_back/pallas_call | solution.py:814
  286.6 37.3 %states_conv_back.1 = (bf16[1024,2336]{1,0:T(8,128)(2,1)}, f32[8,2304]{1,0:T(8,128)}, f32[40,2304]{1,0:T(8,128)}, f32[16,32]{1,0:T(8,128)}) custom-call(bf16[1024,2336]{1,0:T(8,128)(2,1)} %copy-done, bf16[1024,32]{1,0:T(8,128)(2,1)} %slice.412.raw_ref, bf16[1024,2304]{1,0:T(8,128)(2,1)} %get-tuple-element.51.z_ref, ...), custom_call_target="tpu_custom_call" | custom-call | flops 2000000000 | bytes 60000000 | tf_op jit(solution)/shard_map/states_conv_back/pallas_call | solution.py:832
  330.7 11.6 %fusion.12 = (f32[1024]{0:T(1024)S(1)}, f32[1024]{0:T(1024)S(1)}, f32[1024,1024]{1,0:T(8,128)}) fusion(bf16[1,1024,1024]{2,1,0:T(8,128)(2,1)S(1)} %copy-done.4, f32[1024]{0:T(1024)S(1)} %add_rsqrt_fusion, f32[1024]{0:T(1024)S(1)} %mul.194, f32[1024,1024]{1,0:T(8,128)} %fusion.56, bf16[1024,2336]{1,0:T(8,128)(2,1)} %fusion.34, bf16[1024,2336]{1,0:T(8,128)(2,1)} %place_rows.1), kind=kOutput, calls=%fused_computation.18 | convolution fusion | flops 4907333632 | bytes 20070400 | tf_op jit(solution)/shard_map/dot_general | solution.py:869
  343.6 9.7 %convolution_convert_fusion = bf16[1024,2336]{0,1:T(8,128)(2,1)} fusion(bf16[1024,2336]{1,0:T(8,128)(2,1)} %fusion.34, bf16[1,1024,1024]{2,1,0:T(8,128)(2,1)S(1)} %copy-done.4, f32[1024]{0:T(1024)S(1)} %mul.194, f32[1024]{0:T(1024)S(1)} %add_rsqrt_fusion), kind=kOutput, calls=%fused_computation.7 | convolution fusion | flops 4905533440 | bytes 11673600 | tf_op jit(solution)/shard_map/dot_general | solution.py:866
  353.3 7.3 %copy.92.refs_0_ = bf16[1024,2336]{1,0:T(8,128)(2,1)} copy(bf16[1024,2336]{0,1:T(8,128)(2,1)} %convolution_convert_fusion) | data formatting | bytes 9568256 | tf_op jit(solution)/shard_map/convert_element_type | solution.py:866
  360.7 5.0 pick_rows.3
  365.6 4.4 copy.93
  376.4 8.7 %convolution_convert_fusion.3.refs_0_ = bf16[1024,2048]{1,0:T(8,128)(2,1)} fusion(bf16[1024,2048]{1,0:T(8,128)(2,1)} %get-tuple-element.50, bf16[1,1024,1024]{2,1,0:T(8,128)(2,1)S(1)} %copy-done.4, f32[1024]{0:T(1024)S(1)} %mul.194, f32[1024]{0:T(1024)S(1)} %add_rsqrt_fusion), kind=kOutput, calls=%fused_computation.24 | convolution fusion | flops 4301258752 | bytes 10493952 | tf_op jit(solution)/shard_map/dot_general | solution.py:808
  385.2 6.4 %convolution_convert_fusion.2.refs_1_ = bf16[2048,1024]{1,0:T(8,128)(2,1)} fusion(bf16[1024,2048]{1,0:T(8,128)(2,1)S(1)} %copy-done.14, bf16[1,1024,1024]{2,1,0:T(8,128)(2,1)S(1)} %copy-done.9), kind=kOutput, calls=%fused_computation.23 | convolution fusion | flops 4297064448 | bytes 10485760 | tf_op jit(solution)/shard_map/dot_general | solution.py:807
  391.6 7.6 %pick_rows.2 = (bf16[512,4096]{1,0:T(8,128)(2,1)}, bf16[512,4096]{1,0:T(8,128)(2,1)}) custom-call(s32[3]{0:T(128)} %pad_add_fusion.place_ref, bf16[1024,2048]{1,0:T(8,128)(2,1)} %convolution_convert_fusion.3.refs_0_, bf16[2048,1024]{1,0:T(8,128)(2,1)} %convolution_convert_fusion.2.refs_1_), custom_call_target="tpu_custom_call" | custom-call | bytes 16777216 | tf_op jit(solution)/shard_map/pick_rows/pallas_call | solution.py:553
  404.7 3.9 fusion.11
  414.3 4.3 convert_add_fusion.3
  426.9 8.5 %collective-permute-done.36 = bf16[128,2336]{0,1:T(8,128)(2,1)} collective-permute-done((bf16[128,2336]{0,1:T(8,128)(2,1)}, bf16[128,2336]{0,1:T(8,128)(2,1)}, u32[]{:S(2)}, u32[]{:S(2)}) %collective-permute-start.36) | collective-permute-done | bytes 598048 | tf_op jit(solution)/shard_map/ppermute | solution.py:490
  444.5 5.1 convert_add_fusion.1
  454.7 17.3 %collective-permute-done.25 = bf16[128,4096]{1,0:T(8,128)(2,1)S(1)} collective-permute-done((bf16[128,4096]{1,0:T(8,128)(2,1)S(1)}, bf16[128,4096]{1,0:T(8,128)(2,1)S(1)}, u32[]{:S(2)}, u32[]{:S(2)}) %collective-permute-start.25) | collective-permute-done | bytes 1048608 | tf_op jit(solution)/shard_map/ppermute | solution.py:490
  476.4 7.2 %collective-permute-done.26 = bf16[64,4096]{1,0:T(8,128)(2,1)S(1)} collective-permute-done((bf16[64,4096]{1,0:T(8,128)(2,1)S(1)}, bf16[64,4096]{1,0:T(8,128)(2,1)S(1)}, u32[]{:S(2)}, u32[]{:S(2)}) %collective-permute-start.26) | collective-permute-done | bytes 524320 | tf_op jit(solution)/shard_map/ppermute | solution.py:490
  492.0 12.2 %collective-permute-done.30 = bf16[32,4096]{1,0:T(8,128)(2,1)S(1)} collective-permute-done((bf16[32,4096]{1,0:T(8,128)(2,1)S(1)}, bf16[32,4096]{1,0:T(8,128)(2,1)S(1)}, u32[]{:S(2)}, u32[]{:S(2)}) %collective-permute-start.30) | collective-permute-done | bytes 262176 | tf_op jit(solution)/shard_map/ppermute | solution.py:490
  (268 shorter events, 145.8 us)
Async XLA Ops:
  7.2 168.2 %all-gather.2.cloned.1.call-start = ((), (), s32[]{:S(2)}) async-start(), calls=%async_computation | async-start | bytes 8650752 | tf_op jit(solution)/shard_map/all_gather | solution.py:700
  10.7 18.7 %collective-permute-start.9 = (bf16[32,2336]{1,0:T(8,128)(2,1)S(1)}, bf16[32,2336]{1,0:T(8,128)(2,1)S(1)}, u32[]{:S(2)}, u32[]{:S(2)}) collective-permute-start(bf16[32,2336]{1,0:T(8,128)(2,1)S(1)} %slice.315), channel_id=1, source_target_pairs={{0,3},{1,2},{2,1},{3,0},{4,7},{5,6},{6,5},{7,4},{8,11},{9,10},{10,... | collective-permute-start | bytes 448520 | tf_op jit(solution)/shard_map/ppermute | solution.py:490
  15.8 17.2 %collective-permute-start.8 = (bf16[32,2336]{1,0:T(8,128)(2,1)S(1)}, bf16[32,2336]{1,0:T(8,128)(2,1)S(1)}, u32[]{:S(2)}, u32[]{:S(2)}) collective-permute-start(bf16[32,2336]{1,0:T(8,128)(2,1)S(1)} %slice.315), channel_id=1, source_target_pairs={{0,2},{1,3},{2,0},{3,1},{4,6},{5,7},{6,4},{7,5},{8,10},{9,11},{10,... | collective-permute-start | bytes 448520 | tf_op jit(solution)/shard_map/ppermute | solution.py:490
  15.8 18.9 %collective-permute-start.5 = (bf16[32,2336]{1,0:T(8,128)(2,1)S(1)}, bf16[32,2336]{1,0:T(8,128)(2,1)S(1)}, u32[]{:S(2)}, u32[]{:S(2)}) collective-permute-start(bf16[32,2336]{1,0:T(8,128)(2,1)S(1)} %slice.315), channel_id=1, source_target_pairs={{0,1},{1,0},{2,3},{3,2},{4,5},{5,4},{6,7},{7,6},{8,9},{9,8},{10,11... | collective-permute-start | bytes 448520 | tf_op jit(solution)/shard_map/ppermute | solution.py:490
  18.0 27.5 %collective-permute-start = (bf16[1,456]{1,0:T(2,128)(2,1)S(1)}, bf16[1,456]{1,0:T(2,128)(2,1)S(1)}, u32[]{:S(2)}, u32[]{:S(2)}) collective-permute-start(bf16[1,456]{1,0:T(2,128)(2,1)S(1)} %broadcast_in_dim.16), channel_id=1, source_target_pairs={{0,1},{1,0},{2,3},{3,2},{4,5},{5,4},{6,7},{7,6},{8,9},{9,8},{10,11... | collective-permute-start | bytes 2744 | tf_op jit(solution)/shard_map/ppermute | solution.py:490
  20.2 57.7 %collective-permute-start.14 = (bf16[8,1024]{1,0:T(8,128)(2,1)S(1)}, bf16[8,1024]{1,0:T(8,128)(2,1)S(1)}, u32[]{:S(2)}, u32[]{:S(2)}) collective-permute-start(bf16[8,1024]{1,0:T(8,128)(2,1)S(1)} %slice_bitcast_fusion), channel_id=1, source_target_pairs={{0,4},{4,8},{8,12},{12,16},{16,20},{20,24},{24,28},{1,5},{5,9},{9,... | collective-permute-start | bytes 49160 | tf_op jit(solution)/shard_map/ppermute | solution.py:485
  41.3 21.3 %collective-permute-start.11 = (bf16[128,2336]{0,1:T(8,128)(2,1)S(1)}, bf16[128,2336]{0,1:T(8,128)(2,1)S(1)}, u32[]{:S(2)}, u32[]{:S(2)}) collective-permute-start(bf16[128,2336]{0,1:T(8,128)(2,1)S(1)} %copy.75), channel_id=1, source_target_pairs={{0,8},{8,0},{16,24},{24,16},{1,9},{9,1},{17,25},{25,17},{2,10},{10... | collective-permute-start | bytes 1794056 | tf_op jit(solution)/shard_map/ppermute | solution.py:490
  44.1 20.7 %collective-permute-start.7 = (bf16[128,2336]{0,1:T(8,128)(2,1)}, bf16[128,2336]{0,1:T(8,128)(2,1)}, u32[]{:S(2)}, u32[]{:S(2)}) collective-permute-start(bf16[128,2336]{0,1:T(8,128)(2,1)} %copy.73), channel_id=1, source_target_pairs={{0,16},{8,24},{16,0},{24,8},{1,17},{9,25},{17,1},{25,9},{2,18},{10... | collective-permute-start | bytes 1794056 | tf_op jit(solution)/shard_map/ppermute | solution.py:490
  45.6 24.4 %collective-permute-start.1 = (bf16[2,456]{1,0:T(2,128)(2,1)S(1)}, bf16[2,456]{1,0:T(2,128)(2,1)S(1)}, u32[]{:S(2)}, u32[]{:S(2)}) collective-permute-start(bf16[2,456]{1,0:T(2,128)(2,1)S(1)} %pad_maximum_fusion.17), channel_id=1, source_target_pairs={{0,2},{1,3},{2,0},{3,1},{4,6},{5,7},{6,4},{7,5},{8,10},{9,11},{10,... | collective-permute-start | bytes 5480 | tf_op jit(solution)/shard_map/ppermute | solution.py:490
  68.7 13.2 %collective-permute-start.12 = (bf16[256,2336]{0,1:T(8,128)(2,1)}, bf16[256,2336]{0,1:T(8,128)(2,1)}, u32[]{:S(2)}, u32[]{:S(2)}) collective-permute-start(bf16[256,2336]{0,1:T(8,128)(2,1)} %copy.77), channel_id=1, source_target_pairs={{0,4},{4,0},{1,5},{5,1},{2,6},{6,2},{3,7},{7,3},{8,12},{12,8},{9,1... | collective-permute-start | bytes 3588104 | tf_op jit(solution)/shard_map/ppermute | solution.py:490
  68.7 15.6 %collective-permute-start.13 = (bf16[256,2336]{0,1:T(8,128)(2,1)}, bf16[256,2336]{0,1:T(8,128)(2,1)S(1)}, u32[]{:S(2)}, u32[]{:S(2)}) collective-permute-start(bf16[256,2336]{0,1:T(8,128)(2,1)} %copy.78), channel_id=1, source_target_pairs={{0,4},{4,0},{1,5},{5,1},{2,6},{6,2},{3,7},{7,3},{8,12},{12,8},{9,1... | collective-permute-start | bytes 3588104 | tf_op jit(solution)/shard_map/ppermute | solution.py:490
  126.7 15.0 %collective-permute-start.16 = (f32[130,1024]{1,0:T(8,128)}, f32[130,1024]{1,0:T(8,128)}, u32[]{:S(2)}, u32[]{:S(2)}) collective-permute-start(f32[130,1024]{1,0:T(8,128)} %pad_maximum_fusion.5), channel_id=1, source_target_pairs={{0,8},{8,0},{16,24},{24,16},{1,9},{9,1},{17,25},{25,17},{2,10},{10... | collective-permute-start | bytes 1597448 | tf_op jit(solution)/shard_map/ppermute | solution.py:460
  144.5 14.5 %collective-permute-start.17 = (f32[130,1024]{1,0:T(8,128)}, f32[130,1024]{1,0:T(8,128)}, u32[]{:S(2)}, u32[]{:S(2)}) collective-permute-start(f32[130,1024]{1,0:T(8,128)} %pad_maximum_fusion.6), channel_id=1, source_target_pairs={{0,16},{8,24},{16,0},{24,8},{1,17},{9,25},{17,1},{25,9},{2,18},{10... | collective-permute-start | bytes 1597448 | tf_op jit(solution)/shard_map/ppermute | solution.py:460
  161.3 13.0 %collective-permute-start.18 = (f32[128,1024]{1,0:T(8,128)}, f32[128,1024]{1,0:T(8,128)S(1)}, u32[]{:S(2)}, u32[]{:S(2)}) collective-permute-start(f32[128,1024]{1,0:T(8,128)} %get-tuple-element.96), channel_id=1, source_target_pairs={{0,4},{4,0},{1,5},{5,1},{2,6},{6,2},{3,7},{7,3},{8,12},{12,8},{9,1... | collective-permute-start | bytes 1572872 | tf_op jit(solution)/shard_map/ppermute | solution.py:473
  255.6 29.8 %collective-permute-start.22 = (bf16[128,1024]{1,0:T(8,128)(2,1)S(1)}, bf16[128,1024]{1,0:T(8,128)(2,1)S(1)}, u32[]{:S(2)}, u32[]{:S(2)}) collective-permute-start(bf16[128,1024]{1,0:T(8,128)(2,1)S(1)} %get-tuple-element.98), channel_id=1, source_target_pairs={{0,4},{4,0},{1,5},{5,1},{2,6},{6,2},{3,7},{7,3},{8,12},{12,8},{9,1... | collective-permute-start | bytes 786440 | tf_op jit(solution)/shard_map/ppermute | solution.py:473
  342.5 30.3 %collective-permute-start.40 = (f32[32,552]{1,0:T(8,128)S(1)}, f32[32,552]{1,0:T(8,128)S(1)}, u32[]{:S(2)}, u32[]{:S(2)}) collective-permute-start(f32[32,552]{1,0:T(8,128)S(1)} %maximum_maximum_fusion), channel_id=1, source_target_pairs={{0,1},{1,0},{2,3},{3,2},{4,5},{5,4},{6,7},{7,6},{8,9},{9,8},{10,11... | collective-permute-start | bytes 211976 | tf_op jit(solution)/shard_map/ppermute | solution.py:490
  370.1 39.3 %collective-permute-start.32 = (bf16[512,2336]{0,1:T(8,128)(2,1)}, bf16[512,2336]{0,1:T(8,128)(2,1)}, u32[]{:S(2)}, u32[]{:S(2)}) collective-permute-start(bf16[512,2336]{0,1:T(8,128)(2,1)} %copy.93), channel_id=1, source_target_pairs={{0,4},{4,0},{1,5},{5,1},{2,6},{6,2},{3,7},{7,3},{8,12},{12,8},{9,1... | collective-permute-start | bytes 7176200 | tf_op jit(solution)/shard_map/ppermute | solution.py:490
  372.9 12.1 %collective-permute-start.41 = (f32[32,552]{1,0:T(8,128)S(1)}, f32[32,552]{1,0:T(8,128)S(1)}, u32[]{:S(2)}, u32[]{:S(2)}) collective-permute-start(f32[32,552]{1,0:T(8,128)S(1)} %fusion.70), channel_id=1, source_target_pairs={{0,2},{1,3},{2,0},{3,1},{4,6},{5,7},{6,4},{7,5},{8,10},{9,11},{10,... | collective-permute-start | bytes 211976 | tf_op jit(solution)/shard_map/ppermute | solution.py:490
  385.1 14.6 %collective-permute-start.42 = (f32[32,552]{1,0:T(8,128)S(1)}, f32[32,552]{1,0:T(8,128)S(1)}, u32[]{:S(2)}, u32[]{:S(2)}) collective-permute-start(f32[32,552]{1,0:T(8,128)S(1)} %add.210), channel_id=1, source_target_pairs={{0,4},{4,0},{1,5},{5,1},{2,6},{6,2},{3,7},{7,3},{8,12},{12,8},{9,1... | collective-permute-start | bytes 211976 | tf_op jit(solution)/shard_map/ppermute | solution.py:490
  399.2 45.3 %collective-permute-start.24 = (bf16[512,4096]{1,0:T(8,128)(2,1)}, bf16[512,4096]{1,0:T(8,128)(2,1)}, u32[]{:S(2)}, u32[]{:S(2)}) collective-permute-start(bf16[512,4096]{1,0:T(8,128)(2,1)} %get-tuple-element.65), channel_id=1, source_target_pairs={{0,4},{4,0},{1,5},{5,1},{2,6},{6,2},{3,7},{7,3},{8,12},{12,8},{9,1... | collective-permute-start | bytes 12582920 | tf_op jit(solution)/shard_map/ppermute | solution.py:490
  421.1 14.3 %collective-permute-start.36 = (bf16[128,2336]{0,1:T(8,128)(2,1)}, bf16[128,2336]{0,1:T(8,128)(2,1)}, u32[]{:S(2)}, u32[]{:S(2)}) collective-permute-start(bf16[128,2336]{0,1:T(8,128)(2,1)} %copy.98), channel_id=1, source_target_pairs={{0,8},{8,0},{16,24},{24,16},{1,9},{9,1},{17,25},{25,17},{2,10},{10... | collective-permute-start | bytes 1794056 | tf_op jit(solution)/shard_map/ppermute | solution.py:490
  425.4 16.0 %collective-permute-start.33 = (bf16[128,2336]{0,1:T(8,128)(2,1)}, bf16[128,2336]{0,1:T(8,128)(2,1)}, u32[]{:S(2)}, u32[]{:S(2)}) collective-permute-start(bf16[128,2336]{0,1:T(8,128)(2,1)} %copy.95), channel_id=1, source_target_pairs={{0,16},{8,24},{16,0},{24,8},{1,17},{9,25},{17,1},{25,9},{2,18},{10... | collective-permute-start | bytes 1794056 | tf_op jit(solution)/shard_map/ppermute | solution.py:490
  439.9 11.0 %collective-permute-start.37 = (bf16[64,2336]{1,0:T(8,128)(2,1)}, bf16[64,2336]{1,0:T(8,128)(2,1)S(1)}, u32[]{:S(2)}, u32[]{:S(2)}) collective-permute-start(bf16[64,2336]{1,0:T(8,128)(2,1)} %slice.636), channel_id=1, source_target_pairs={{0,16},{8,24},{16,0},{24,8},{1,17},{9,25},{17,1},{25,9},{2,18},{10... | collective-permute-start | bytes 897032 | tf_op jit(solution)/shard_map/ppermute | solution.py:490
  443.0 11.1 %collective-permute-start.34 = (bf16[64,2336]{1,0:T(8,128)(2,1)S(1)}, bf16[64,2336]{1,0:T(8,128)(2,1)S(1)}, u32[]{:S(2)}, u32[]{:S(2)}) collective-permute-start(bf16[64,2336]{1,0:T(8,128)(2,1)S(1)} %slice.637), channel_id=1, source_target_pairs={{0,8},{8,0},{16,24},{24,16},{1,9},{9,1},{17,25},{25,17},{2,10},{10... | collective-permute-start | bytes 897032 | tf_op jit(solution)/shard_map/ppermute | solution.py:490
  449.8 22.3 %collective-permute-start.25 = (bf16[128,4096]{1,0:T(8,128)(2,1)S(1)}, bf16[128,4096]{1,0:T(8,128)(2,1)S(1)}, u32[]{:S(2)}, u32[]{:S(2)}) collective-permute-start(bf16[128,4096]{1,0:T(8,128)(2,1)S(1)} %slice.631), channel_id=1, source_target_pairs={{0,16},{8,24},{16,0},{24,8},{1,17},{9,25},{17,1},{25,9},{2,18},{10... | collective-permute-start | bytes 3145736 | tf_op jit(solution)/shard_map/ppermute | solution.py:490
  450.2 23.3 %collective-permute-start.28 = (bf16[128,4096]{1,0:T(8,128)(2,1)S(1)}, bf16[128,4096]{1,0:T(8,128)(2,1)S(1)}, u32[]{:S(2)}, u32[]{:S(2)}) collective-permute-start(bf16[128,4096]{1,0:T(8,128)(2,1)S(1)} %slice.630), channel_id=1, source_target_pairs={{0,8},{8,0},{16,24},{24,16},{1,9},{9,1},{17,25},{25,17},{2,10},{10... | collective-permute-start | bytes 3145736 | tf_op jit(solution)/shard_map/ppermute | solution.py:490
  451.0 35.3 %collective-permute-start.38 = (bf16[32,2336]{1,0:T(8,128)(2,1)S(1)}, bf16[32,2336]{1,0:T(8,128)(2,1)S(1)}, u32[]{:S(2)}, u32[]{:S(2)}) collective-permute-start(bf16[32,2336]{1,0:T(8,128)(2,1)S(1)} %get-tuple-element.105), channel_id=1, source_target_pairs={{0,2},{1,3},{2,0},{3,1},{4,6},{5,7},{6,4},{7,5},{8,10},{9,11},{10,... | collective-permute-start | bytes 448520 | tf_op jit(solution)/shard_map/ppermute | solution.py:490
  452.3 36.1 %collective-permute-start.39 = (bf16[32,2336]{1,0:T(8,128)(2,1)S(1)}, bf16[32,2336]{1,0:T(8,128)(2,1)S(1)}, u32[]{:S(2)}, u32[]{:S(2)}) collective-permute-start(bf16[32,2336]{1,0:T(8,128)(2,1)S(1)} %get-tuple-element.106), channel_id=1, source_target_pairs={{0,3},{1,2},{2,1},{3,0},{4,7},{5,6},{6,5},{7,4},{8,11},{9,10},{10,... | collective-permute-start | bytes 448520 | tf_op jit(solution)/shard_map/ppermute | solution.py:490
  454.2 34.3 %collective-permute-start.35 = (bf16[32,2336]{1,0:T(8,128)(2,1)S(1)}, bf16[32,2336]{1,0:T(8,128)(2,1)S(1)}, u32[]{:S(2)}, u32[]{:S(2)}) collective-permute-start(bf16[32,2336]{1,0:T(8,128)(2,1)S(1)} %slice.639), channel_id=1, source_target_pairs={{0,1},{1,0},{2,3},{3,2},{4,5},{5,4},{6,7},{7,6},{8,9},{9,8},{10,11... | collective-permute-start | bytes 448520 | tf_op jit(solution)/shard_map/ppermute | solution.py:490
  472.4 11.2 %collective-permute-start.26 = (bf16[64,4096]{1,0:T(8,128)(2,1)S(1)}, bf16[64,4096]{1,0:T(8,128)(2,1)S(1)}, u32[]{:S(2)}, u32[]{:S(2)}) collective-permute-start(bf16[64,4096]{1,0:T(8,128)(2,1)S(1)} %slice.635), channel_id=1, source_target_pairs={{0,8},{8,0},{16,24},{24,16},{1,9},{9,1},{17,25},{25,17},{2,10},{10... | collective-permute-start | bytes 1572872 | tf_op jit(solution)/shard_map/ppermute | solution.py:490
  484.3 19.9 %collective-permute-start.30 = (bf16[32,4096]{1,0:T(8,128)(2,1)S(1)}, bf16[32,4096]{1,0:T(8,128)(2,1)S(1)}, u32[]{:S(2)}, u32[]{:S(2)}) collective-permute-start(bf16[32,4096]{1,0:T(8,128)(2,1)S(1)} %get-tuple-element.103), channel_id=1, source_target_pairs={{0,2},{1,3},{2,0},{3,1},{4,6},{5,7},{6,4},{7,5},{8,10},{9,11},{10,... | collective-permute-start | bytes 786440 | tf_op jit(solution)/shard_map/ppermute | solution.py:490
  486.4 17.8 %collective-permute-start.31 = (bf16[32,4096]{1,0:T(8,128)(2,1)S(1)}, bf16[32,4096]{1,0:T(8,128)(2,1)S(1)}, u32[]{:S(2)}, u32[]{:S(2)}) collective-permute-start(bf16[32,4096]{1,0:T(8,128)(2,1)S(1)} %get-tuple-element.104), channel_id=1, source_target_pairs={{0,3},{1,2},{2,1},{3,0},{4,7},{5,6},{6,5},{7,4},{8,11},{9,10},{10,... | collective-permute-start | bytes 786440 | tf_op jit(solution)/shard_map/ppermute | solution.py:490
  (32 other events, 292.7 us)
Sparse Core Ops, SparseCore 0:
  10.9 88.1 all-gather.1

commit v3 on v2

--- a/solution.py
+++ b/solution.py
@@ -17,6 +17,8 @@
 DI = HEADS * HEADDIM
 CHANNELS = DI + 2 * STATE
 WIDE = 512
+MIX = CHANNELS + HEADS
+MIX_WIDE = -(-MIX // 128) * 128
 NEG = -1e30
 LOG2E = 1.4426950408889634
 ALL = ("pair", "core", "fsdp")
@@ -112,7 +114,7 @@
         else:
             q_ref[...] = value
 
-    raw = raw_ref[...].astype(F32) + sbias_ref[...]
+    raw = raw_ref[:, :HEADS].astype(F32) + sbias_ref[...]
     size = jnp.maximum(raw, 0.0) + jnp.log1p(jnp.exp(-jnp.abs(raw)))
     decay = -jnp.exp(rate_ref[...]) * size * LOG2E
     tri = (iota2((CHUNK, CHUNK), 0) >= iota2((CHUNK, CHUNK), 1)).astype(BF)
@@ -391,13 +393,14 @@
         + cumulate((col < row).astype(BF), later)
         + jnp.sum(through, axis=0, keepdims=True)
     )
-    raw = raw_ref[...].astype(F32) + sbias_ref[...]
+    raw = raw_ref[:, :HEADS].astype(F32) + sbias_ref[...]
     sig = sigmoid(raw)
     size = jnp.maximum(raw, 0.0) + jnp.log1p(jnp.exp(-jnp.abs(raw)))
     rate = -jnp.exp(rate_ref[...])
     ratio = jnp.where(raw < -15.0, 1.0, sig / jnp.maximum(size, 1e-37))
     draw = (uv_ref[...] + later) * ratio + ddecay * rate * sig
-    dx_ref[:, CHANNELS:] = draw.astype(BF)
+    dx_ref[:, CHANNELS:MIX] = draw.astype(BF)
+    dx_ref[:, MIX:] = jnp.zeros((CHUNK, MIX_WIDE - MIX), BF)
     hsum[0:8] += rows8(ddecay * rate * size)
     hsum[8:16] += rows8(draw)
 
@@ -417,6 +420,13 @@
     return pl.BlockSpec((per, width), lambda c: (count - 1 - c, 0))
 
 
+def raw_rows(count=None):
+    block = CHANNELS // LANES
+    if count is None:
+        return pl.BlockSpec((CHUNK, LANES), lambda c: (c, block))
+    return pl.BlockSpec((CHUNK, LANES), lambda c: (count - 1 - c, block))
+
+
 def shape(dims, kind):
     return jax.ShapeDtypeStruct(dims, kind)
 
@@ -439,15 +449,39 @@
     return packed[:STATE], packed[STATE : STATE + 1] + packed[STATE + 1 : STATE + 2]
 
 
+class Steps:
+    def __init__(self, steps):
+        self.steps, self.result, self.flight = steps, None, None
+        self.advance(None)
+
+    def advance(self, landed):
+        try:
+            self.flight = self.steps.send(landed)
+        except StopIteration as end:
+            self.flight, self.result = None, end.value
+
+    def beside(self, *work):
+        if self.flight is None:
+            return work
+        landed, work = lax.optimization_barrier((self.flight, work))
+        self.advance(landed)
+        return work
+
+    def finish(self):
+        while self.flight is not None:
+            self.advance(self.flight)
+        return self.result
+
+
 def carry_states(packed, pairs, backward):
     packed = packed[: STATE + 2]
+    kind = packed.dtype
     core = lax.axis_index("core")
     place = lax.axis_index("pair")
     half = packed.shape[1] // 2
-    swap = [(0, 1), (1, 0)]
     left, right = packed[:, :half], packed[:, half:]
     mine = jnp.where(core == 0, left, right)
-    theirs = lax.ppermute(jnp.where(core == 0, right, left), "core", swap)
+    (theirs,) = yield [swap(jnp.where(core == 0, right, left), "core", 1)]
     leads = (core == 1) if backward else (core == 0)
     first, first_thru = unpack(jnp.where(leads, mine, theirs))
     second, second_thru = unpack(jnp.where(leads, theirs, mine))
@@ -455,24 +489,19 @@
     before, before_thru = jnp.zeros_like(total), jnp.ones_like(total_thru)
     distance = 1
     while distance < pairs:
-        route = [(i, i ^ distance) for i in range(pairs)]
-        other, other_thru = unpack(
-            lax.ppermute(pack(total, total_thru, packed.dtype), "pair", route)
-        )
+        (other,) = yield [swap(pack(total, total_thru, kind), "pair", distance)]
+        other, other_thru = unpack(other)
         upper = (place & distance) != 0
         follows = jnp.logical_not(upper) if backward else upper
         before = jnp.where(follows, before + before_thru * other, before)
         before_thru = jnp.where(follows, before_thru * other_thru, before_thru)
-        total = jnp.where(
-            follows, total + total_thru * other, other + other_thru * total
-        )
+        total = jnp.where(follows, total + total_thru * other, other + other_thru * total)
         total_thru = total_thru * other_thru
         distance *= 2
     after = first + first_thru * before
     keep = jnp.where(leads, before, after)
-    other = lax.ppermute(
-        jnp.where(leads, after, before).astype(packed.dtype), "core", swap
-    ).astype(F32)
+    (other,) = yield [swap(jnp.where(leads, after, before).astype(kind), "core", 1)]
+    other = other.astype(F32)
     return jnp.where(
         core == 0,
         jnp.concatenate([keep, other], axis=1),
@@ -593,6 +622,7 @@
     if r % 16:
         return lax.all_gather(w, ALL, axis=0, tiled=True)
     line = [w] + [swap(w, "fsdp", k) for k in range(1, fsdp)]
+    yield line[1:]
     held = []
     for part, order in enumerate(bit_orders(pairs)):
         ks = range(part * fsdp // 2, (part + 1) * fsdp // 2)
@@ -612,22 +642,29 @@
             lax.psum_scatter(g.astype(F32), ALL, scatter_dimension=0, tiled=True) for g in arrays
         ]
     keep, give = pick_rows(place, arrays, r, pairs, fsdp)
-    got = swap(give, "core", 1)
+    (got,) = yield [swap(give, "core", 1)]
     half = keep.shape[0] // 2
-    ends = []
-    for part, order in enumerate(bit_orders(pairs)):
+    orders = bit_orders(pairs)
+    blocks = []
+    for part in range(2):
         at = slice(part * half, (part + 1) * half)
-        block = keep[at].astype(F32) + got[at].astype(F32)
-        for b in reversed(order):
-            cut = block.shape[0] // 2
-            other = swap(block[cut:].astype(BF), "pair", 1 << b)
-            block = block[:cut] + other.astype(F32)
-        ends.append(block)
-    total = ends[0][:r]
-    for k in range(1, fsdp):
-        at = (k % (fsdp // 2)) * r
-        block = ends[k // (fsdp // 2)][at : at + r]
-        total = total + swap(block.astype(BF), "fsdp", k).astype(F32)
+        blocks.append(keep[at].astype(F32) + got[at].astype(F32))
+    for level in reversed(range(len(orders[0]))):
+        cut = blocks[0].shape[0] // 2
+        others = yield [
+            swap(block[cut:].astype(BF), "pair", 1 << order[level])
+            for block, order in zip(blocks, orders)
+        ]
+        blocks = [block[:cut] + other.astype(F32) for block, other in zip(blocks, others)]
+    others = yield [
+        swap(
+            blocks[k // (fsdp // 2)][(k % (fsdp // 2)) * r :][:r].astype(BF), "fsdp", k
+        )
+        for k in range(1, fsdp)
+    ]
+    total = blocks[0][:r]
+    for other in others:
+        total = total + other.astype(F32)
     out, col = [], 0
     for g in arrays:
         width = g.shape[1]
@@ -681,7 +718,20 @@
     place = jnp.stack([lax.axis_index(a) for a in ALL])
     device = (place[0] * 2 + place[1]) * fsdp + place[2]
     small = jnp.concatenate([conv_weight.reshape(-1), conv_bias, norm_gain, gate_gain])
-    small = gather_small(small, device, pairs, fsdp)
+    r, slot = in_weight.shape[0], MIX_WIDE - MIX
+    small_rows = -(-small.size // slot)
+    small = jnp.pad(small, (0, r * slot - small.size)).reshape(r, slot)
+    mix_gather = Steps(
+        gather_rows(jnp.concatenate([in_weight[:, DI:], small], axis=1), place, pairs)
+    )
+    in_weight, out_weight = mix_gather.beside(in_weight, out_weight)
+    packed_weights = jnp.concatenate(
+        [in_weight[:, :DI], out_weight[:r], out_weight[r:]], axis=1
+    )
+    packed_weights = lax.all_gather(packed_weights, ALL, axis=0, tiled=True)
+    w_mix = mix_gather.finish()
+    small = w_mix[:, MIX:].reshape(-1, r, slot)[:, :small_rows].reshape(-1, small_rows * slot)
+    small = small[:, : sum(own)]
     conv_full = (
         small[:, : own[0]].reshape(-1, taps, own[0] // taps).transpose(1, 0, 2)
         .reshape(taps, CHANNELS).astype(F32)
@@ -692,12 +742,6 @@
     norm_full = small[:, at : at + own[2]].reshape(1, model).astype(F32)
     at += own[2]
     gate_full = small[:, at :].reshape(1, DI).astype(F32)
-    w_mix = gather_rows(in_weight[:, DI:], place, pairs)
-    r = in_weight.shape[0]
-    packed_weights = jnp.concatenate(
-        [in_weight[:, :DI], out_weight[:r], out_weight[r:]], axis=1
-    )
-    packed_weights = lax.all_gather(packed_weights, ALL, axis=0, tiled=True)
     w_gate, w_out = unpack_weights(packed_weights, r)
 
     expand = jnp.asarray(np.repeat(np.eye(HEADS), HEADDIM, axis=1), BF)
@@ -725,7 +769,6 @@
     hidden = hidden_of(tokens, norm_full)
     halo_hidden = hidden_of(tail, norm_full)
     mix = jnp.dot(hidden, w_mix, preferred_element_type=F32).astype(BF)
-    raw_step = mix[:, CHANNELS:]
     halo = jnp.dot(halo_hidden, w_mix[:, :CHANNELS], preferred_element_type=F32)
     halo = halo.astype(BF).astype(F32)
 
@@ -734,7 +777,7 @@
         name="conv_states",
         grid=(chunks,),
         in_specs=[
-            rows(CHANNELS), rows(HEADS), rows(8), whole((8, CHANNELS)), whole((taps, CHANNELS)),
+            rows(CHANNELS), raw_rows(), rows(8), whole((8, CHANNELS)), whole((taps, CHANNELS)),
             whole((1, CHANNELS)), whole((1, HEADS)), whole((1, HEADS)), whole((HEADS, DI)),
         ],
         out_specs=[
@@ -751,9 +794,10 @@
         ],
         compiler_params=PARAMS,
         cost_estimate=cost(10**9, 30 * 10**6),
-    )(mix, raw_step, info, halo, conv_full, bias_full, rate, sbias, expand)
-
-    incoming = carry_states(packed, pairs, False)
+    )(mix, mix, info, halo, conv_full, bias_full, rate, sbias, expand)
+
+    forward = Steps(carry_states(packed, pairs, False))
+    forward.beside()
 
     y_local = pl.pallas_call(
         intra_kernel,
@@ -769,8 +813,11 @@
         cost_estimate=cost(10**9, 30 * 10**6),
     )(q, k, v, rc, rs, info, label_rows)
 
+    (y_local,) = forward.beside(y_local)
     gate = jnp.dot(hidden, w_gate, preferred_element_type=F32).astype(BF)
     grad_normed = lax.dot_general(upstream, w_out, NT, preferred_element_type=F32)
+    gate, grad_normed = forward.beside(gate, grad_normed)
+    incoming = forward.finish()
 
     normed, dy, dy_lo, dgate, u, dq, states, packed_back, gate_sums = pl.pallas_call(
         gate_kernel,
@@ -802,14 +849,17 @@
         expand,
     )
 
-    coming_back = carry_states(packed_back, pairs, True)
-
+    backward = Steps(carry_states(packed_back, pairs, True))
+    grad_gate_w = lax.dot_general(hidden, dgate, TN, preferred_element_type=F32).astype(BF)
+    (grad_gate_w,) = backward.beside(grad_gate_w)
     grad_out_w = lax.dot_general(normed, upstream, TN, preferred_element_type=F32).astype(BF)
-    grad_gate_w = lax.dot_general(hidden, dgate, TN, preferred_element_type=F32).astype(BF)
-    gate_shard, out_shard = reduce_rows([grad_gate_w, grad_out_w], place, pairs)
+    (grad_out_w,) = backward.beside(grad_out_w)
+    gate_steps = Steps(reduce_rows([grad_gate_w, grad_out_w], place, pairs))
     block_out = (
         tokens.astype(F32) + jnp.dot(normed, w_out, preferred_element_type=F32)
     ).astype(BF)
+    (block_out,) = gate_steps.beside(block_out)
+    block_out, dy = backward.beside(block_out, dy)
 
     dv, uv, dq, dk = pl.pallas_call(
         intra_back_kernel,
@@ -828,24 +878,27 @@
         cost_estimate=cost(2 * 10**9, 40 * 10**6),
     )(q, k, v, dy, dy_lo, rc, rs, info, label_rows, expand, dq)
 
+    (dv,) = gate_steps.beside(dv)
+    (dv,) = backward.beside(dv)
+    coming_back = backward.finish()
     back = functools.partial(rows, count=chunks)
     grad_mix, dhalo, conv_sums, head_sums = pl.pallas_call(
         back_kernel,
         name="states_conv_back",
         grid=(chunks,),
         in_specs=[
-            back(CHANNELS), back(HEADS), back(CHANNELS), back(DI), back(STATE), back(STATE),
+            back(CHANNELS), raw_rows(chunks), back(CHANNELS), back(DI), back(STATE), back(STATE),
             back(HEADS), back(CHUNK, per=HEADS), back(8), back(DI), back(DI), back(HEADS),
             back(HEADS), back(STATE), back(STATE), back(DI), whole((STATE, DI)),
             whole((8, CHANNELS)), whole((taps, CHANNELS)), whole((1, HEADS)),
             whole((1, HEADS)), whole((1, DI)), whole((HEADS, DI)),
         ],
         out_specs=[
-            back(CHANNELS + HEADS), whole((8, CHANNELS)), whole((40, CHANNELS)),
+            back(MIX_WIDE), whole((8, CHANNELS)), whole((40, CHANNELS)),
             whole((16, HEADS)),
         ],
         out_shape=[
-            shape((count, CHANNELS + HEADS), BF), shape((8, CHANNELS), F32),
+            shape((count, MIX_WIDE), BF), shape((8, CHANNELS), F32),
             shape((40, CHANNELS), F32), shape((16, HEADS), F32),
         ],
         scratch_shapes=[
@@ -855,16 +908,17 @@
         compiler_params=PARAMS,
         cost_estimate=cost(2 * 10**9, 60 * 10**6),
     )(
-        mix, raw_step, z, v, k, q, rc, rs, info, dy, dv, uv, u, dq, dk, states, coming_back,
+        mix, mix, z, v, k, q, rc, rs, info, dy, dv, uv, u, dq, dk, states, coming_back,
         halo, conv_full, rate, sbias, skip_wide, expand,
     )
 
+    grad_mix, dhalo = gate_steps.beside(grad_mix, dhalo)
     edge = shift(dhalo, 2 * pairs, -1)
-    edge = jnp.pad(edge, ((0, 0), (0, HEADS)))
+    edge = jnp.pad(edge, ((0, 0), (0, MIX_WIDE - CHANNELS)))
     fixed = (grad_mix[count - 8 :].astype(F32) + edge).astype(BF)
     grad_mix = lax.dynamic_update_slice(grad_mix, fixed, (count - 8, 0))
     grad_mix_w = lax.dot_general(hidden, grad_mix, TN, preferred_element_type=F32).astype(BF)
-    (mix_shard,) = reduce_rows([grad_mix_w], place, pairs)
+    mix_steps = Steps(reduce_rows([grad_mix_w], place, pairs))
     grad_hidden = lax.dot_general(dgate, w_gate, NT, preferred_element_type=F32)
     grad_hidden = grad_hidden + lax.dot_general(grad_mix, w_mix, NT, preferred_element_type=F32)
 
@@ -901,7 +955,9 @@
         mine[a:b] for a, b in zip([0] + ends[:-1], ends)
     ]
     conv_shard = conv_shard.reshape(taps, -1)
-    in_shard = jnp.concatenate([gate_shard, mix_shard], axis=1)
+    (mix_shard,) = mix_steps.finish()
+    gate_shard, out_shard = gate_steps.finish()
+    in_shard = jnp.concatenate([gate_shard, mix_shard[:, :MIX]], axis=1)
     return (
         block_out[None],
         grad_tokens[None],

time: 518 us -> 443 us (0.86)
  waiting for transfers between devices: 111 us -> 75.5 us
  local copies, waits for them, and re-layouts: 51.4 us -> 23.7 us
  starting transfers between devices: 58.4 us -> 48.2 us
    ppermute x8 -> x0, waiting for transfers between devices: 30 us -> none  [the longest x4 26.8 us: carry_states(): lax.ppermute(pack(total, total_thru, packed.dtype), 'pair', route)]
    ppermute x6 -> x0, local copies, waits for them, and re-layouts: 8.32 us -> none  [swap(): return lax.ppermute(block, axis, [(i, i ^ mask) for i in range(count)])]
    ppermute x8 -> x0, starting transfers between devices: 7.24 us -> none  [the longest x4 6.59 us: carry_states(): lax.ppermute(pack(total, total_thru, packed.dtype), 'pair', route)]
    ppermute x35 -> x38, waiting for transfers between devices: 79 us -> 75.5 us  [swap(): return lax.ppermute(block, axis, [(i, i ^ mask) for i in range(count)])]
    ppermute x35 -> x38, starting transfers between devices: 48.6 us -> 45.6 us  [swap(): return lax.ppermute(block, axis, [(i, i ^ mask) for i in range(count)])]
  transfers between devices with their start and end apart: 46 -> 41, of which waited for: 21 -> 17; matrix products, arithmetic and copies ran while one was open for 26% -> 29% of each run, Pallas kernels for 15% -> 26%
where the time goes in v3:
time: 443 us; the launch traced here: 438 us
  Pallas kernels  155 us (35%)
  matrix products  75.9 us (17%)
  waiting for transfers between devices  75.5 us (17%)
  starting transfers between devices  48.2 us (11%)
  other arithmetic  45.2 us (10%)
  local copies, waits for them, and re-layouts  23.7 us (5%)
  between operations  15 us (3%)
    ppermute x38, waiting for transfers between devices, swap(): return lax.ppermute(block, axis, [(i, i ^ mask) for i in range(count)])  75.5 us
    ppermute x38, starting transfers between devices, swap(): return lax.ppermute(block, axis, [(i, i ^ mask) for i in range(count)])  45.6 us
    pallas_call x1, Pallas kernels, on_device(): pl.pallas_call(back_kernel, name='states_conv_back', grid=(chunks,), in_s...  37.5 us
    pallas_call x1, Pallas kernels, on_device(): pl.pallas_call(gate_kernel, name='gate_norm', grid=(chunks,), in_specs=[r...  33.3 us
    pallas_call x1, Pallas kernels, on_device(): pl.pallas_call(intra_back_kernel, name='intra_back', grid=(chunks,), in_s...  29.3 us
    pallas_call x1, Pallas kernels, on_device(): pl.pallas_call(prep_kernel, name='conv_states', grid=(chunks,), in_specs=...  18.9 us
    pallas_call x2, Pallas kernels, pick_rows(): pl.pallas_call(body, name='pick_rows', in_specs=[pl.BlockSpec(memory_spac...  12.4 us
    pallas_call x1, Pallas kernels, on_device(): pl.pallas_call(intra_kernel, name='intra', grid=(chunks,), in_specs=[rows...  11.4 us
  transfers between devices with their start and end apart: 41, of which 17 were waited for; matrix products, arithmetic and copies ran while one was open for 29% of the time, Pallas kernels for 26%

profile of v3, /device:TPU:0, one launch (start us, length us, event | category | flops | bytes accessed | tf_op | source)
XLA Modules:
  0.0 438.4 jit_solution(15753889092954266855)
XLA Ops:
  9.9 5.1 %collective-permute-start.4 = (bf16[32,2432]{1,0:T(8,128)(2,1)S(1)}, bf16[32,2432]{1,0:T(8,128)(2,1)S(1)}, u32[]{:S(2)}, u32[]{:S(2)}) collective-permute-start(bf16[32,2432]{1,0:T(8,128)(2,1)S(1)} %pad_maximum_fusion.12), channel_id=1, source_target_pairs={{0,3},{1,2},{2,1},{3,0},{4,7},{5,6},{6,5},{7,4},{8,11},{9,10},{10,... | collective-permute-start | bytes 466952 | tf_op jit(solution)/shard_map/ppermute | solution.py:519
  15.6 4.3 collective-permute-done.4
  19.9 8.2 %collective-permute-done.3 = bf16[32,2432]{1,0:T(8,128)(2,1)S(1)} collective-permute-done((bf16[32,2432]{1,0:T(8,128)(2,1)S(1)}, bf16[32,2432]{1,0:T(8,128)(2,1)S(1)}, u32[]{:S(2)}, u32[]{:S(2)}) %collective-permute-start.3) | collective-permute-done | bytes 155680 | tf_op jit(solution)/shard_map/ppermute | solution.py:519
  38.6 7.4 %collective-permute-done.5 = bf16[64,2432]{1,0:T(8,128)(2,1)S(1)} collective-permute-done((bf16[64,2432]{1,0:T(8,128)(2,1)S(1)}, bf16[64,2432]{1,0:T(8,128)(2,1)S(1)}, u32[]{:S(2)}, u32[]{:S(2)}) %collective-permute-start.5) | collective-permute-done | bytes 311328 | tf_op jit(solution)/shard_map/ppermute | solution.py:519
  46.1 2.5 collective-permute-start.6
  50.2 16.7 %collective-permute-done.6 = bf16[128,2432]{1,0:T(8,128)(2,1)S(1)} collective-permute-done((bf16[128,2432]{1,0:T(8,128)(2,1)S(1)}, bf16[128,2432]{1,0:T(8,128)(2,1)S(1)}, u32[]{:S(2)}, u32[]{:S(2)}) %collective-permute-start.6) | collective-permute-done | bytes 622624 | tf_op jit(solution)/shard_map/ppermute | solution.py:519
  74.6 5.0 %place_rows.1 = bf16[1024,2432]{1,0:T(8,128)(2,1)} custom-call(s32[3]{0:T(128)} %pad_add_fusion.place_ref, bf16[256,2432]{1,0:T(8,128)(2,1)} %copy-done.7, bf16[256,2432]{1,0:T(8,128)(2,1)} %copy-done.16, bf16[256,2432]{1,0:T(8,128)(2,1)} %collective-permute-done.7.refs_2_, bf16[256,2432]{1,0:T(8,128)(2,1)} %collective-permute-done.8.refs_3_), custom_call_target="tpu_custom_call" | custom-call | bytes 9961472 | tf_op jit(solution)/shard_map/place_rows/pallas_call | solution.py:552
  82.8 3.7 fusion.18.halo_ref
  86.5 10.2 %convolution_convert_fusion.1.x_ref.raw_ref = bf16[1024,2432]{1,0:T(8,128)(2,1)} fusion(bf16[1024,2432]{1,0:T(8,128)(2,1)} %place_rows.1, bf16[1,1024,1024]{2,1,0:T(8,128)(2,1)S(1)} %copy-done.4, f32[1024]{0:T(1024)S(1)} %reshape.213, f32[1024]{0:T(1024)S(1)} %add_rsqrt_fusion), kind=kOutput, calls=%fused_computation.8 | convolution fusion | flops 5106958336 | bytes 12066816 | tf_op jit(solution)/shard_map/dot_general | solution.py:771
  96.7 18.9 %conv_states.1 = (bf16[1024,2304]{1,0:T(8,128)(2,1)}, bf16[1024,2048]{1,0:T(8,128)(2,1)}, f32[1024,128]{1,0:T(8,128)}, f32[1024,128]{1,0:T(8,128)}, f32[1024,32]...) custom-call(bf16[1024,2432]{1,0:T(8,128)(2,1)} %convolution_convert_fusion.1.x_ref.raw_ref, ...), custom_call_target="tpu_custom_call" | custom-call | flops 1000000000 | bytes 30000000 | tf_op jit(solution)/shard_map/conv_states/pallas_call | solution.py:775
  122.9 11.4 %intra.1.y_ref = f32[1024,2048]{1,0:T(8,128)} custom-call(f32[1024,128]{1,0:T(8,128)} %get-tuple-element.67.q_ref, f32[1024,128]{1,0:T(8,128)} %get-tuple-element.68.k_ref, bf16[1024,2048]{1,0:T(8,128)(2,1)} %get-tuple-element.69.v_ref, f32[1024,32]{1,0:T(8,128)} %get-tuple-element.70.rc_ref, f32[256,128]{1,0:T(8,128)} %get-tuple-element.71.rs_ref, ...), custom_call_target="tpu_custom_call" | custom-call | flops 1000000000 | bytes 30000000 | tf_op jit(solution)/shard_map/intra/pallas_call | solution.py:802
  140.7 7.1 %unpack_weights.1 = (bf16[1024,2048]{1,0:T(8,128)(2,1)}, bf16[2048,1024]{1,0:T(8,128)(2,1)}) custom-call(bf16[1024,4096]{1,0:T(8,128)(2,1)} %all-gather.2.cloned.1.call-done.src), custom_call_target="tpu_custom_call" | custom-call | bytes 16777216 | tf_op jit(solution)/shard_map/unpack_weights/pallas_call | solution.py:608
  147.8 8.6 %convolution_convert_fusion.4.gate_ref = bf16[1024,2048]{1,0:T(8,128)(2,1)} fusion(bf16[1024,2048]{1,0:T(8,128)(2,1)} %get-tuple-element.76, bf16[1,1024,1024]{2,1,0:T(8,128)(2,1)S(1)} %copy-done.4, f32[1024]{0:T(1024)S(1)} %reshape.213, f32[1024]{0:T(1024)S(1)} %add_rsqrt_fusion), kind=kOutput, calls=%fused_computation.25 | convolution fusion | flops 4301258752 | bytes 10493952 | tf_op jit(solution)/shard_map/dot_general | solution.py:817
  156.4 6.8 %convolution_bitcast_fusion.dn_ref = f32[1024,2048]{1,0:T(8,128)} fusion(bf16[2048,1024]{1,0:T(8,128)(2,1)S(1)} %copy-done.24, bf16[1,1024,1024]{2,1,0:T(8,128)(2,1)S(1)} %copy-done.13), kind=kOutput, calls=%fused_computation.11 | convolution fusion | flops 4294967296 | bytes 14680064 | tf_op jit(solution)/shard_map/dot_general | solution.py:818
  168.7 33.3 %gate_norm.1 = (bf16[1024,2048]{1,0:T(8,128)(2,1)}, bf16[1024,2048]{1,0:T(8,128)(2,1)}, bf16[1024,2048]{1,0:T(8,128)(2,1)}, bf16[1024,2048]{1,0:T(8,128)(2,1)}, ...) custom-call(f32[1024,2048]{1,0:T(8,128)} %intra.1.y_ref, ...), custom_call_target="tpu_custom_call" | custom-call | flops 1000000000 | bytes 50000000 | tf_op jit(solution)/shard_map/gate_norm/pallas_call | solution.py:822
  203.2 8.9 %convolution_convert_fusion.3.refs_0_ = bf16[1024,2048]{1,0:T(8,128)(2,1)} fusion(bf16[1024,2048]{1,0:T(8,128)(2,1)} %get-tuple-element.82, bf16[1,1024,1024]{2,1,0:T(8,128)(2,1)S(1)} %copy-done.4, f32[1024]{0:T(1024)S(1)} %reshape.213, f32[1024]{0:T(1024)S(1)} %add_rsqrt_fusion), kind=kOutput, calls=%fused_computation.24 | convolution fusion | flops 4301258752 | bytes 10493952 | tf_op jit(solution)/shard_map/dot_general | solution.py:853
  214.0 6.6 %convolution_convert_fusion.2.refs_1_ = bf16[2048,1024]{1,0:T(8,128)(2,1)} fusion(bf16[1024,2048]{1,0:T(8,128)(2,1)S(1)} %copy-done.25, bf16[1,1024,1024]{2,1,0:T(8,128)(2,1)S(1)} %copy-done.14), kind=kOutput, calls=%fused_computation.23 | convolution fusion | flops 4297064448 | bytes 10485760 | tf_op jit(solution)/shard_map/dot_general | solution.py:855
  221.3 7.4 %pick_rows.2 = (bf16[512,4096]{1,0:T(8,128)(2,1)}, bf16[512,4096]{1,0:T(8,128)(2,1)}) custom-call(s32[3]{0:T(128)} %pad_add_fusion.place_ref, bf16[1024,2048]{1,0:T(8,128)(2,1)} %convolution_convert_fusion.3.refs_0_, bf16[2048,1024]{1,0:T(8,128)(2,1)} %convolution_convert_fusion.2.refs_1_), custom_call_target="tpu_custom_call" | custom-call | bytes 16777216 | tf_op jit(solution)/shard_map/pick_rows/pallas_call | solution.py:582
  228.7 9.4 %fusion.14 = bf16[1024,1024]{1,0:T(8,128)(2,1)} fusion(bf16[1,1024,1024]{2,1,0:T(8,128)(2,1)S(1)} %copy-done.4, bf16[1024,2048]{1,0:T(8,128)(2,1)} %get-tuple-element.84, bf16[2048,1024]{1,0:T(8,128)(2,1)} %get-tuple-element.77), kind=kOutput, calls=%fused_computation.20 | convolution fusion | flops 4298113024 | bytes 12582912 | tf_op jit(solution)/shard_map/dot_general | solution.py:859
  239.1 3.9 convert_add_fusion.1
  248.3 6.1 %fusion.59 = f32[1024,1024]{1,0:T(8,128)} fusion(bf16[1024,2048]{1,0:T(8,128)(2,1)S(1)} %copy-done.23, bf16[1024,2048]{1,0:T(8,128)(2,1)S(1)} %copy-done.22), kind=kOutput, calls=%fused_computation.175 | convolution fusion | flops 4294967296 | bytes 12582912 | tf_op jit(solution)/shard_map/dot_general | solution.py:922
  256.3 29.3 %intra_back.1 = (bf16[1024,2048]{1,0:T(8,128)(2,1)}, f32[1024,32]{1,0:T(8,128)}, f32[1024,128]{1,0:T(8,128)}, f32[1024,128]{1,0:T(8,128)}) custom-call(f32[1024,128]{1,0:T(8,128)} %get-tuple-element.67.q_ref, f32[1024,128]{1,0:T(8,128)} %get-tuple-element.68.k_ref, bf16[1024,2048]{1,0:T(8,128)(2,1)} %get-tuple-element.69.v_ref, ...), custom_call_target="tpu_custom_call" | custom-call | flops 2000000000 | bytes 40000000 | tf_op jit(solution)/shard_map/intra_back/pallas_call | solution.py:864
  295.8 37.5 %states_conv_back.1 = (bf16[1024,2432]{1,0:T(8,128)(2,1)}, f32[8,2304]{1,0:T(8,128)}, f32[40,2304]{1,0:T(8,128)}, f32[16,32]{1,0:T(8,128)}) custom-call(bf16[1024,2432]{1,0:T(8,128)(2,1)} %convolution_convert_fusion.1.x_ref.raw_ref, bf16[1024,2432]{1,0:T(8,128)(2,1)} %convolution_convert_fusion.1.x_ref.raw_ref, bf16[1024,2304]{1,0:T(8,128)(2,1)} %get-tuple-element.100.z_ref, ...), custom_call_target="tpu_custom_call" | custom-call | flops 2000000000 | bytes 60000000 | tf_op jit(solution)/shard_map/states_conv_back/pallas_call | solution.py:885
  342.4 3.5 collective-permute-start.25
  346.8 7.8 %convolution_convert_fusion.refs_0_ = bf16[1024,2432]{1,0:T(8,128)(2,1)} fusion(bf16[1024,2432]{1,0:T(8,128)(2,1)S(1)} %fusion.33, bf16[1,1024,1024]{2,1,0:T(8,128)(2,1)S(1)} %copy-done.4, f32[1024]{0:T(1024)S(1)} %reshape.213, f32[1024]{0:T(1024)S(1)} %add_rsqrt_fusion), kind=kOutput, calls=%fused_computation.7 | convolution fusion | flops 5106958336 | bytes 12066816 | tf_op jit(solution)/shard_map/dot_general | solution.py:920
  354.7 7.8 %fusion.12 = (f32[1024]{0:T(1024)S(1)}, f32[1024]{0:T(1024)S(1)}, f32[1024,1024]{1,0:T(8,128)}) fusion(bf16[1,1024,1024]{2,1,0:T(8,128)(2,1)S(1)} %copy-done.4, f32[1024]{0:T(1024)S(1)} %add_rsqrt_fusion, f32[1024]{0:T(1024)S(1)} %reshape.213, f32[1024,1024]{1,0:T(8,128)S(1)} %copy-done.27, bf16[1024,2432]{1,0:T(8,128)(2,1)S(1)} %fusion.33, ...), kind=kOutput, calls=%fused_computation.18 | convolution fusion | flops 5108660224 | bytes 20463616 | tf_op jit(solution)/shard_map/dot_general | solution.py:923
  362.5 5.0 %pick_rows.3 = (bf16[512,2432]{1,0:T(8,128)(2,1)}, bf16[512,2432]{1,0:T(8,128)(2,1)}) custom-call(s32[3]{0:T(128)} %pad_add_fusion.place_ref, bf16[1024,2432]{1,0:T(8,128)(2,1)} %convolution_convert_fusion.refs_0_), custom_call_target="tpu_custom_call" | custom-call | bytes 9961472 | tf_op jit(solution)/shard_map/pick_rows/pallas_call | solution.py:582
  368.1 4.6 %collective-permute-done.35 = f32[32,552]{1,0:T(8,128)S(1)} collective-permute-done((f32[32,552]{1,0:T(8,128)S(1)}, f32[32,552]{1,0:T(8,128)S(1)}, u32[]{:S(2)}, u32[]{:S(2)}) %collective-permute-start.35) | collective-permute-done | bytes 70688 | tf_op jit(solution)/shard_map/ppermute | solution.py:519
  374.6 4.8 %fusion.11 = f32[1,1024,1024]{2,1,0:T(8,128)} fusion(f32[1024,1024]{1,0:T(8,128)} %get-tuple-element.171, bf16[1,1024,1024]{2,1,0:T(8,128)(2,1)} %param.24, bf16[1,1024,1024]{2,1,0:T(8,128)(2,1)S(1)} %copy-done.4, f32[1024]{0:T(1024)S(1)} %broadcast_multiply_fusion, f32[1024]{0:T(1024)S(1)} %reshape.213, f32[1024]{0:T(1024)S(1)} %add_rsqrt_fusion), kind=kLoop, calls=%fused_computation.17 | loop fusion | flops 8388608 | bytes 12595200 | tf_op jit(solution)/shard_map/broadcast_in_dim | solution.py:963
  396.0 11.2 %collective-permute-done.28 = bf16[128,2432]{1,0:T(8,128)(2,1)S(1)} collective-permute-done((bf16[128,2432]{1,0:T(8,128)(2,1)}, bf16[128,2432]{1,0:T(8,128)(2,1)S(1)}, u32[]{:S(2)}, u32[]{:S(2)}) %collective-permute-start.28) | collective-permute-done | bytes 622624 | tf_op jit(solution)/shard_map/ppermute | solution.py:519
  411.2 5.0 %collective-permute-done.29 = bf16[64,2432]{1,0:T(8,128)(2,1)S(1)} collective-permute-done((bf16[64,2432]{1,0:T(8,128)(2,1)S(1)}, bf16[64,2432]{1,0:T(8,128)(2,1)S(1)}, u32[]{:S(2)}, u32[]{:S(2)}) %collective-permute-start.29) | collective-permute-done | bytes 311328 | tf_op jit(solution)/shard_map/ppermute | solution.py:519
  422.7 7.7 %collective-permute-done.33 = bf16[32,2432]{1,0:T(8,128)(2,1)S(1)} collective-permute-done((bf16[32,2432]{1,0:T(8,128)(2,1)S(1)}, bf16[32,2432]{1,0:T(8,128)(2,1)S(1)}, u32[]{:S(2)}, u32[]{:S(2)}) %collective-permute-start.33) | collective-permute-done | bytes 155680 | tf_op jit(solution)/shard_map/ppermute | solution.py:519
  (267 shorter events, 107.6 us)
Async XLA Ops:
  7.2 133.5 %all-gather.2.cloned.1.call-start = ((), (), s32[]{:S(2)}) async-start(), calls=%async_computation | async-start | bytes 8650752 | tf_op jit(solution)/shard_map/all_gather | solution.py:731
  9.9 10.0 %collective-permute-start.4 = (bf16[32,2432]{1,0:T(8,128)(2,1)S(1)}, bf16[32,2432]{1,0:T(8,128)(2,1)S(1)}, u32[]{:S(2)}, u32[]{:S(2)}) collective-permute-start(bf16[32,2432]{1,0:T(8,128)(2,1)S(1)} %pad_maximum_fusion.12), channel_id=1, source_target_pairs={{0,3},{1,2},{2,1},{3,0},{4,7},{5,6},{6,5},{7,4},{8,11},{9,10},{10,... | collective-permute-start | bytes 466952 | tf_op jit(solution)/shard_map/ppermute | solution.py:519
  14.9 13.2 %collective-permute-start.3 = (bf16[32,2432]{1,0:T(8,128)(2,1)S(1)}, bf16[32,2432]{1,0:T(8,128)(2,1)S(1)}, u32[]{:S(2)}, u32[]{:S(2)}) collective-permute-start(bf16[32,2432]{1,0:T(8,128)(2,1)S(1)} %pad_maximum_fusion.12), channel_id=1, source_target_pairs={{0,2},{1,3},{2,0},{3,1},{4,6},{5,7},{6,4},{7,5},{8,10},{9,11},{10,... | collective-permute-start | bytes 466952 | tf_op jit(solution)/shard_map/ppermute | solution.py:519
  14.9 13.2 %collective-permute-start = (bf16[32,2432]{1,0:T(8,128)(2,1)S(1)}, bf16[32,2432]{1,0:T(8,128)(2,1)S(1)}, u32[]{:S(2)}, u32[]{:S(2)}) collective-permute-start(bf16[32,2432]{1,0:T(8,128)(2,1)S(1)} %pad_maximum_fusion.12), channel_id=1, source_target_pairs={{0,1},{1,0},{2,3},{3,2},{4,5},{5,4},{6,7},{7,6},{8,9},{9,8},{10,11... | collective-permute-start | bytes 466952 | tf_op jit(solution)/shard_map/ppermute | solution.py:519
  31.4 43.1 %collective-permute-start.9 = (bf16[8,1024]{1,0:T(8,128)(2,1)S(1)}, bf16[8,1024]{1,0:T(8,128)(2,1)S(1)}, u32[]{:S(2)}, u32[]{:S(2)}) collective-permute-start(bf16[8,1024]{1,0:T(8,128)(2,1)S(1)} %slice_bitcast_fusion), channel_id=1, source_target_pairs={{0,4},{4,8},{8,12},{12,16},{16,20},{20,24},{24,28},{1,5},{5,9},{9,... | collective-permute-start | bytes 49160 | tf_op jit(solution)/shard_map/ppermute | solution.py:514
  34.8 11.3 %collective-permute-start.5 = (bf16[64,2432]{1,0:T(8,128)(2,1)S(1)}, bf16[64,2432]{1,0:T(8,128)(2,1)S(1)}, u32[]{:S(2)}, u32[]{:S(2)}) collective-permute-start(bf16[64,2432]{1,0:T(8,128)(2,1)S(1)} %pad_maximum_fusion.7), channel_id=1, source_target_pairs={{0,16},{8,24},{16,0},{24,8},{1,17},{9,25},{17,1},{25,9},{2,18},{10... | collective-permute-start | bytes 933896 | tf_op jit(solution)/shard_map/ppermute | solution.py:519
  37.0 11.8 %collective-permute-start.1 = (bf16[64,2432]{1,0:T(8,128)(2,1)S(1)}, bf16[64,2432]{1,0:T(8,128)(2,1)S(1)}, u32[]{:S(2)}, u32[]{:S(2)}) collective-permute-start(bf16[64,2432]{1,0:T(8,128)(2,1)S(1)} %pad_maximum_fusion.6), channel_id=1, source_target_pairs={{0,8},{8,0},{16,24},{24,16},{1,9},{9,1},{17,25},{25,17},{2,10},{10... | collective-permute-start | bytes 933896 | tf_op jit(solution)/shard_map/ppermute | solution.py:519
  46.1 20.8 %collective-permute-start.6 = (bf16[128,2432]{1,0:T(8,128)(2,1)S(1)}, bf16[128,2432]{1,0:T(8,128)(2,1)S(1)}, u32[]{:S(2)}, u32[]{:S(2)}) collective-permute-start(bf16[128,2432]{1,0:T(8,128)(2,1)S(1)} %pad_maximum_fusion.2), channel_id=1, source_target_pairs={{0,8},{8,0},{16,24},{24,16},{1,9},{9,1},{17,25},{25,17},{2,10},{10... | collective-permute-start | bytes 1867784 | tf_op jit(solution)/shard_map/ppermute | solution.py:519
  48.9 20.0 %collective-permute-start.2 = (bf16[128,2432]{1,0:T(8,128)(2,1)S(1)}, bf16[128,2432]{1,0:T(8,128)(2,1)S(1)}, u32[]{:S(2)}, u32[]{:S(2)}) collective-permute-start(bf16[128,2432]{1,0:T(8,128)(2,1)S(1)} %pad_maximum_fusion.1), channel_id=1, source_target_pairs={{0,16},{8,24},{16,0},{24,8},{1,17},{9,25},{17,1},{25,9},{2,18},{10... | collective-permute-start | bytes 1867784 | tf_op jit(solution)/shard_map/ppermute | solution.py:519
  67.0 7.6 %collective-permute-start.8 = (bf16[256,2432]{1,0:T(8,128)(2,1)S(1)}, bf16[256,2432]{1,0:T(8,128)(2,1)}, u32[]{:S(2)}, u32[]{:S(2)}) collective-permute-start(bf16[256,2432]{1,0:T(8,128)(2,1)S(1)} %constant_dynamic-update-slice_fusion.refs_1_), channel_id=1, source_target_pairs={{0,4},{4,0},{1,5},{5,1},{2,6},{6,2},{3,7},{7,3},{8,12},{12,8},{9,1... | collective-permute-start | bytes 3735560 | tf_op jit(solution)/shard_map/ppermute | solution.py:519
  121.2 15.2 %collective-permute-start.11 = (f32[130,1024]{1,0:T(8,128)}, f32[130,1024]{1,0:T(8,128)}, u32[]{:S(2)}, u32[]{:S(2)}) collective-permute-start(f32[130,1024]{1,0:T(8,128)} %pad_maximum_fusion.4), channel_id=1, source_target_pairs={{0,8},{8,0},{16,24},{24,16},{1,9},{9,1},{17,25},{25,17},{2,10},{10... | collective-permute-start | bytes 1597448 | tf_op jit(solution)/shard_map/ppermute | solution.py:519
  139.2 24.0 %collective-permute-start.12 = (f32[130,1024]{1,0:T(8,128)}, f32[130,1024]{1,0:T(8,128)}, u32[]{:S(2)}, u32[]{:S(2)}) collective-permute-start(f32[130,1024]{1,0:T(8,128)} %pad_maximum_fusion.5), channel_id=1, source_target_pairs={{0,16},{8,24},{16,0},{24,8},{1,17},{9,25},{17,1},{25,9},{2,18},{10... | collective-permute-start | bytes 1597448 | tf_op jit(solution)/shard_map/ppermute | solution.py:519
  203.0 9.1 %collective-permute-start.14 = (bf16[130,1024]{1,0:T(8,128)(2,1)S(1)}, bf16[130,1024]{1,0:T(8,128)(2,1)S(1)}, u32[]{:S(2)}, u32[]{:S(2)}) collective-permute-start(bf16[130,1024]{1,0:T(8,128)(2,1)S(1)} %broadcast_select_fusion.1), channel_id=1, source_target_pairs={{0,4},{4,0},{1,5},{5,1},{2,6},{6,2},{3,7},{7,3},{8,12},{12,8},{9,1... | collective-permute-start | bytes 798728 | tf_op jit(solution)/shard_map/ppermute | solution.py:519
  212.4 9.0 %collective-permute-start.15 = (bf16[130,1024]{1,0:T(8,128)(2,1)S(1)}, bf16[130,1024]{1,0:T(8,128)(2,1)S(1)}, u32[]{:S(2)}, u32[]{:S(2)}) collective-permute-start(bf16[130,1024]{1,0:T(8,128)(2,1)S(1)} %pad_maximum_fusion.8), channel_id=1, source_target_pairs={{0,8},{8,0},{16,24},{24,16},{1,9},{9,1},{17,25},{25,17},{2,10},{10... | collective-permute-start | bytes 798728 | tf_op jit(solution)/shard_map/ppermute | solution.py:519
  228.7 10.3 %collective-permute-start.17 = (bf16[512,4096]{1,0:T(8,128)(2,1)}, bf16[512,4096]{1,0:T(8,128)(2,1)}, u32[]{:S(2)}, u32[]{:S(2)}) collective-permute-start(bf16[512,4096]{1,0:T(8,128)(2,1)} %get-tuple-element.88), channel_id=1, source_target_pairs={{0,4},{4,0},{1,5},{5,1},{2,6},{6,2},{3,7},{7,3},{8,12},{12,8},{9,1... | collective-permute-start | bytes 12582920 | tf_op jit(solution)/shard_map/ppermute | solution.py:519
  238.4 16.4 %collective-permute-start.16 = (bf16[130,1024]{1,0:T(8,128)(2,1)S(1)}, bf16[130,1024]{1,0:T(8,128)(2,1)}, u32[]{:S(2)}, u32[]{:S(2)}) collective-permute-start(bf16[130,1024]{1,0:T(8,128)(2,1)S(1)} %pad_maximum_fusion.9), channel_id=1, source_target_pairs={{0,16},{8,24},{16,0},{24,8},{1,17},{9,25},{17,1},{25,9},{2,18},{10... | collective-permute-start | bytes 798728 | tf_op jit(solution)/shard_map/ppermute | solution.py:519
  245.3 40.4 %collective-permute-start.18 = (bf16[128,4096]{1,0:T(8,128)(2,1)}, bf16[128,4096]{1,0:T(8,128)(2,1)}, u32[]{:S(2)}, u32[]{:S(2)}) collective-permute-start(bf16[128,4096]{1,0:T(8,128)(2,1)} %slice.649), channel_id=1, source_target_pairs={{0,16},{8,24},{16,0},{24,8},{1,17},{9,25},{17,1},{25,9},{2,18},{10... | collective-permute-start | bytes 3145736 | tf_op jit(solution)/shard_map/ppermute | solution.py:519
  246.8 38.9 %collective-permute-start.19 = (bf16[128,4096]{1,0:T(8,128)(2,1)}, bf16[128,4096]{1,0:T(8,128)(2,1)}, u32[]{:S(2)}, u32[]{:S(2)}) collective-permute-start(bf16[128,4096]{1,0:T(8,128)(2,1)} %slice.648), channel_id=1, source_target_pairs={{0,8},{8,0},{16,24},{24,16},{1,9},{9,1},{17,25},{25,17},{2,10},{10... | collective-permute-start | bytes 3145736 | tf_op jit(solution)/shard_map/ppermute | solution.py:519
  255.9 34.5 %collective-permute-start.22 = (bf16[128,1024]{1,0:T(8,128)(2,1)S(1)}, bf16[128,1024]{1,0:T(8,128)(2,1)S(1)}, u32[]{:S(2)}, u32[]{:S(2)}) collective-permute-start(bf16[128,1024]{1,0:T(8,128)(2,1)S(1)} %get-tuple-element.146), channel_id=1, source_target_pairs={{0,4},{4,0},{1,5},{5,1},{2,6},{6,2},{3,7},{7,3},{8,12},{12,8},{9,1... | collective-permute-start | bytes 786440 | tf_op jit(solution)/shard_map/ppermute | solution.py:519
  291.9 43.8 %collective-permute-start.21 = (bf16[64,4096]{1,0:T(8,128)(2,1)}, bf16[64,4096]{1,0:T(8,128)(2,1)}, u32[]{:S(2)}, u32[]{:S(2)}) collective-permute-start(bf16[64,4096]{1,0:T(8,128)(2,1)} %slice.652), channel_id=1, source_target_pairs={{0,16},{8,24},{16,0},{24,8},{1,17},{9,25},{17,1},{25,9},{2,18},{10... | collective-permute-start | bytes 1572872 | tf_op jit(solution)/shard_map/ppermute | solution.py:519
  293.2 42.5 %collective-permute-start.20 = (bf16[64,4096]{1,0:T(8,128)(2,1)S(1)}, bf16[64,4096]{1,0:T(8,128)(2,1)S(1)}, u32[]{:S(2)}, u32[]{:S(2)}) collective-permute-start(bf16[64,4096]{1,0:T(8,128)(2,1)S(1)} %slice.653), channel_id=1, source_target_pairs={{0,8},{8,0},{16,24},{24,16},{1,9},{9,1},{17,25},{25,17},{2,10},{10... | collective-permute-start | bytes 1572872 | tf_op jit(solution)/shard_map/ppermute | solution.py:519
  339.6 7.2 %collective-permute-start.23 = (f32[8,2304]{1,0:T(8,128)S(1)}, f32[8,2304]{1,0:T(8,128)S(1)}, u32[]{:S(2)}, u32[]{:S(2)}) collective-permute-start(f32[8,2304]{1,0:T(8,128)S(1)} %copy-done.26), channel_id=1, source_target_pairs={{4,0},{8,4},{12,8},{16,12},{20,16},{24,20},{28,24},{5,1},{9,5},{13... | collective-permute-start | bytes 221192 | tf_op jit(solution)/shard_map/ppermute | solution.py:514
  342.4 37.1 %collective-permute-start.24 = (bf16[32,4096]{1,0:T(8,128)(2,1)}, bf16[32,4096]{1,0:T(8,128)(2,1)}, u32[]{:S(2)}, u32[]{:S(2)}) collective-permute-start(bf16[32,4096]{1,0:T(8,128)(2,1)} %slice.656), channel_id=1, source_target_pairs={{0,1},{1,0},{2,3},{3,2},{4,5},{5,4},{6,7},{7,6},{8,9},{9,8},{10,11... | collective-permute-start | bytes 786440 | tf_op jit(solution)/shard_map/ppermute | solution.py:519
  342.4 37.1 %collective-permute-start.25 = (bf16[32,4096]{1,0:T(8,128)(2,1)}, bf16[32,4096]{1,0:T(8,128)(2,1)}, u32[]{:S(2)}, u32[]{:S(2)}) collective-permute-start(bf16[32,4096]{1,0:T(8,128)(2,1)} %get-tuple-element.151), channel_id=1, source_target_pairs={{0,2},{1,3},{2,0},{3,1},{4,6},{5,7},{6,4},{7,5},{8,10},{9,11},{10,... | collective-permute-start | bytes 786440 | tf_op jit(solution)/shard_map/ppermute | solution.py:519
  346.0 33.5 %collective-permute-start.26 = (bf16[32,4096]{1,0:T(8,128)(2,1)}, bf16[32,4096]{1,0:T(8,128)(2,1)}, u32[]{:S(2)}, u32[]{:S(2)}) collective-permute-start(bf16[32,4096]{1,0:T(8,128)(2,1)} %get-tuple-element.152), channel_id=1, source_target_pairs={{0,3},{1,2},{2,1},{3,0},{4,7},{5,6},{6,5},{7,4},{8,11},{9,10},{10,... | collective-permute-start | bytes 786440 | tf_op jit(solution)/shard_map/ppermute | solution.py:519
  367.6 20.2 %collective-permute-start.27 = (bf16[512,2432]{1,0:T(8,128)(2,1)}, bf16[512,2432]{1,0:T(8,128)(2,1)S(1)}, u32[]{:S(2)}, u32[]{:S(2)}) collective-permute-start(bf16[512,2432]{1,0:T(8,128)(2,1)} %get-tuple-element.117), channel_id=1, source_target_pairs={{0,4},{4,0},{1,5},{5,1},{2,6},{6,2},{3,7},{7,3},{8,12},{12,8},{9,1... | collective-permute-start | bytes 7471112 | tf_op jit(solution)/shard_map/ppermute | solution.py:519
  391.9 15.3 %collective-permute-start.28 = (bf16[128,2432]{1,0:T(8,128)(2,1)}, bf16[128,2432]{1,0:T(8,128)(2,1)S(1)}, u32[]{:S(2)}, u32[]{:S(2)}) collective-permute-start(bf16[128,2432]{1,0:T(8,128)(2,1)} %slice.651), channel_id=1, source_target_pairs={{0,16},{8,24},{16,0},{24,8},{1,17},{9,25},{17,1},{25,9},{2,18},{10... | collective-permute-start | bytes 1867784 | tf_op jit(solution)/shard_map/ppermute | solution.py:519
  394.2 15.3 %collective-permute-start.31 = (bf16[128,2432]{1,0:T(8,128)(2,1)S(1)}, bf16[128,2432]{1,0:T(8,128)(2,1)S(1)}, u32[]{:S(2)}, u32[]{:S(2)}) collective-permute-start(bf16[128,2432]{1,0:T(8,128)(2,1)S(1)} %slice.650), channel_id=1, source_target_pairs={{0,8},{8,0},{16,24},{24,16},{1,9},{9,1},{17,25},{25,17},{2,10},{10... | collective-permute-start | bytes 1867784 | tf_op jit(solution)/shard_map/ppermute | solution.py:519
  408.7 7.5 %collective-permute-start.29 = (bf16[64,2432]{1,0:T(8,128)(2,1)S(1)}, bf16[64,2432]{1,0:T(8,128)(2,1)S(1)}, u32[]{:S(2)}, u32[]{:S(2)}) collective-permute-start(bf16[64,2432]{1,0:T(8,128)(2,1)S(1)} %slice.655), channel_id=1, source_target_pairs={{0,8},{8,0},{16,24},{24,16},{1,9},{9,1},{17,25},{25,17},{2,10},{10... | collective-permute-start | bytes 933896 | tf_op jit(solution)/shard_map/ppermute | solution.py:519
  409.7 8.3 %collective-permute-start.32 = (bf16[64,2432]{1,0:T(8,128)(2,1)S(1)}, bf16[64,2432]{1,0:T(8,128)(2,1)S(1)}, u32[]{:S(2)}, u32[]{:S(2)}) collective-permute-start(bf16[64,2432]{1,0:T(8,128)(2,1)S(1)} %slice.654), channel_id=1, source_target_pairs={{0,16},{8,24},{16,0},{24,8},{1,17},{9,25},{17,1},{25,9},{2,18},{10... | collective-permute-start | bytes 933896 | tf_op jit(solution)/shard_map/ppermute | solution.py:519
  418.1 12.4 %collective-permute-start.33 = (bf16[32,2432]{1,0:T(8,128)(2,1)S(1)}, bf16[32,2432]{1,0:T(8,128)(2,1)S(1)}, u32[]{:S(2)}, u32[]{:S(2)}) collective-permute-start(bf16[32,2432]{1,0:T(8,128)(2,1)S(1)} %get-tuple-element.153), channel_id=1, source_target_pairs={{0,2},{1,3},{2,0},{3,1},{4,6},{5,7},{6,4},{7,5},{8,10},{9,11},{10,... | collective-permute-start | bytes 466952 | tf_op jit(solution)/shard_map/ppermute | solution.py:519
  420.3 10.1 %collective-permute-start.34 = (bf16[32,2432]{1,0:T(8,128)(2,1)S(1)}, bf16[32,2432]{1,0:T(8,128)(2,1)S(1)}, u32[]{:S(2)}, u32[]{:S(2)}) collective-permute-start(bf16[32,2432]{1,0:T(8,128)(2,1)S(1)} %get-tuple-element.154), channel_id=1, source_target_pairs={{0,3},{1,2},{2,1},{3,0},{4,7},{5,6},{6,5},{7,4},{8,11},{9,10},{10,... | collective-permute-start | bytes 466952 | tf_op jit(solution)/shard_map/ppermute | solution.py:519
  (40 other events, 344.7 us)
Sparse Core Ops, SparseCore 0:
  30.8 81.2 all-gather.1

commit v4 on v3

--- a/solution.py
+++ b/solution.py
@@ -48,12 +48,16 @@
 
 
 def spread(x, expand):
-    hi, lo = pieces(x, 2)
-    return mm(hi, expand) + mm(lo, expand)
+    both = jnp.concatenate(pieces(x, 2), axis=1)
+    return mm(both, jnp.concatenate([expand, expand], axis=0))
 
 
 def head_sum(x, expand):
     hi, lo = pieces(x, 2)
+    if x.shape[1] == LANES:
+        return mm(
+            jnp.concatenate([hi, lo], axis=1), jnp.concatenate([expand, expand], axis=1), NT
+        )
     return mm(hi, expand, NT) + mm(lo, expand, NT)
 
 
@@ -69,7 +73,7 @@
 
 
 def sigmoid(x):
-    return 1.0 / (1.0 + jnp.exp(-x))
+    return 0.5 * jnp.tanh(0.5 * x) + 0.5
 
 
 def iota2(shape, dim):
@@ -89,7 +93,7 @@
 
     @pl.when(step == 0)
     def _():
-        carry[...] = halo_ref[...]
+        carry[...] = halo_ref[:8].astype(F32)
         state[...] = jnp.zeros_like(state)
         thru[...] = jnp.ones_like(thru)
         pad[...] = jnp.zeros_like(pad)
@@ -129,7 +133,7 @@
     keys = k_ref[...].astype(BF)
     for g in range(DI // WIDE):
         sl = slice(g * WIDE, (g + 1) * WIDE)
-        scaled = (spread(weight, e_ref[:, sl]) * v_ref[:, sl].astype(F32)).astype(BF)
+        scaled = (mm(weight.astype(BF), e_ref[:, sl]) * v_ref[:, sl].astype(F32)).astype(BF)
         factor = spread(carried, e_ref[:, sl])[7:8]
         state[:, sl] = factor * state[:, sl] + mm(keys, scaled, TN)
         thru[:, sl] = factor * thru[:, sl]
@@ -194,6 +198,8 @@
     entering = jnp.exp2(running) * info[:, 2:3]
     queries, queries_lo = pieces(q_ref[...], 2)
     keys = k_ref[...].astype(BF)
+    low_weight = weight.astype(BF)
+    both_queries = jnp.concatenate([queries, queries_lo], axis=1)
     squares = jnp.zeros((CHUNK, LANES), F32)
     dots = jnp.zeros((CHUNK, LANES), F32)
     for g in range(DI // WIDE):
@@ -203,7 +209,8 @@
         ent = spread(entering, e_ref[:, sl])
         enter[:, sl] = ent
         y = y_ref[:, sl] + ent * (
-            mm(queries, low_state) + (mm(queries_lo, low_state) + mm(queries, rest))
+            mm(both_queries, jnp.concatenate([low_state, low_state], axis=0))
+            + mm(queries, rest)
         )
         scan[:, sl] = y
         gate = gate_ref[:, sl].astype(F32)
@@ -243,12 +250,11 @@
         ent = enter[:, sl]
         dy_in, dy_in_lo = pieces(ent * dy, 2)
         state_hi, state_lo = pieces(state[:, sl], 2)
-        dq = dq + (
-            mm(dy_in, state_hi, NT) + (mm(dy_in_lo, state_hi, NT) + mm(dy_in, state_lo, NT))
-        )
+        both = mm(dy_in, jnp.concatenate([state_hi, state_lo], axis=0), NT)
+        dq = dq + (both[:, :STATE] + (both[:, STATE:] + mm(dy_in_lo, state_hi, NT)))
         adj[:, sl] += reach[:, sl] * mm(queries, dy_in, TN)
         factor = ent[CHUNK - 1 :]
-        scaled = (spread(weight, e_ref[:, sl]) * v).astype(BF)
+        scaled = (mm(low_weight, e_ref[:, sl]) * v).astype(BF)
         state[:, sl] = factor * state[:, sl] + mm(keys, scaled, TN)
         reach[:, sl] = factor * reach[:, sl]
     u_ref[...] = head_dots
@@ -288,9 +294,8 @@
             differ = (rc_ref[:, h : h + 1] - rs_ref[h : h + 1, :]) + bias
             factor = jnp.exp2(differ)
             dscores = dscores + dmix[:, i * CHUNK : (i + 1) * CHUNK] * factor
-            mixing.append((factor * scores).astype(BF))
-        both = mm(jnp.concatenate(mixing, axis=1), dy, TN)
-        dv = jnp.where(low_half, both[:CHUNK], both[CHUNK:])
+            mixing.append((factor * scores).astype(BF).T)
+        dv = mm(jnp.concatenate(mixing, axis=1), two_heads(dy, low_half))
         dv_ref[:, sl] = dv.astype(BF)
         head_dots = head_dots + head_sum(v.astype(F32) * dv, e_ref[:, sl])
     uv_ref[...] = head_dots
@@ -326,6 +331,8 @@
     keys = k_ref[...].astype(BF)
     dq = dq_ref[...]
     dk = dk_ref[...]
+    low_weight = weight.astype(BF)
+    low_entering = entering.astype(BF)
     later = jnp.zeros((CHUNK, HEADS), F32)
     through = jnp.zeros((8, HEADS), F32)
     for g in range(DI // WIDE):
@@ -333,17 +340,16 @@
         e = e_ref[:, sl]
         v = v_ref[:, sl].astype(F32)
         dy = dy_ref[:, sl].astype(F32)
-        ent = spread(entering, e)
-        wide = spread(weight, e)
-        dy_in = (ent * dy).astype(BF)
+        wide = mm(low_weight, e)
+        dy_in = (mm(low_entering, e) * dy).astype(BF)
         scaled = (wide * v).astype(BF)
         adjoint = adj[:, sl]
         low_adj = adjoint.astype(BF)
         states = sc_ref[:, sl]
         dv = wide * mm(keys, low_adj)
-        later = later + head_sum(v * dv, e)
+        later = later + mm((v * dv).astype(BF), e, NT)
         dk = dk + mm(scaled, low_adj, NT)
-        factor = ent[CHUNK - 1 :]
+        factor = spread(entering[CHUNK - 8 :], e)[7:8]
         through = through + head_sum(rows8(adjoint * states.astype(F32)) * factor, e)
         adj[:, sl] = factor * adjoint + mm(queries, dy_in, TN)
         dmix[:, sl] = dv_ref[:, sl].astype(F32) + dv + skip_ref[:, sl] * dy
@@ -374,7 +380,7 @@
 
         @pl.when(step == pl.num_programs(0) - 1)
         def _():
-            halo = halo_ref[:, sl]
+            halo = halo_ref[:8, sl].astype(F32)
             acc = jnp.zeros((8, LANES), F32)
             for d in (1, 2, 3):
                 ext = jnp.concatenate(
@@ -566,11 +572,15 @@
     half = len(order) * r
     repeat = [a.shape[0] // (2 * half) for a in arrays]
     cols = sum(a.shape[1] * n for a, n in zip(arrays, repeat))
+    quarter = len(order) // 4
 
     def body(place_ref, *refs):
-        for flip, dst in ((1, refs[-1]), (0, refs[-2])):
-            for at, (mask, k) in enumerate(order):
+        for flip in range(2):
+            for spot, (mask, k) in enumerate(order):
                 index = shard_of(place_ref, fsdp, mask, flip, k)
+                dst, at = refs[-1], spot
+                if not flip:
+                    dst, at = refs[spot // quarter - 5], spot % quarter
                 col = 0
                 for src, n in zip(refs, repeat):
                     for m in range(n):
@@ -584,8 +594,9 @@
         name="pick_rows",
         in_specs=[pl.BlockSpec(memory_space=pltpu.SMEM)]
         + [pl.BlockSpec(memory_space=pltpu.VMEM)] * len(arrays),
-        out_specs=[pl.BlockSpec(memory_space=pltpu.VMEM)] * 2,
-        out_shape=[jax.ShapeDtypeStruct((half, cols), arrays[0].dtype)] * 2,
+        out_specs=[pl.BlockSpec(memory_space=pltpu.VMEM)] * 5,
+        out_shape=[jax.ShapeDtypeStruct((half // 4, cols), arrays[0].dtype)] * 4
+        + [jax.ShapeDtypeStruct((half, cols), arrays[0].dtype)],
         compiler_params=PLAIN,
         cost_estimate=cost(0, 8 * half * cols),
     )(place, *arrays)
@@ -622,14 +633,17 @@
     if r % 16:
         return lax.all_gather(w, ALL, axis=0, tiled=True)
     line = [w] + [swap(w, "fsdp", k) for k in range(1, fsdp)]
-    yield line[1:]
-    held = []
-    for part, order in enumerate(bit_orders(pairs)):
-        ks = range(part * fsdp // 2, (part + 1) * fsdp // 2)
-        block = jnp.concatenate([line[k] for k in ks], axis=0)
-        for b in order:
-            block = jnp.concatenate([block, swap(block, "pair", 1 << b)], axis=0)
-        held.append((block, 0, part_ids(pairs, fsdp)[part]))
+    orders = bit_orders(pairs)
+    blocks = [
+        jnp.concatenate(line[part * fsdp // 2 : (part + 1) * fsdp // 2], axis=0)
+        for part in range(2)
+    ]
+    for level in range(len(orders[0])):
+        got = [swap(a, "pair", 1 << order[level]) for a, order in zip(blocks, orders)]
+        if level == 0:
+            got = yield got
+        blocks = [jnp.concatenate([a, b], axis=0) for a, b in zip(blocks, got)]
+    held = [(a, 0, ids) for a, ids in zip(blocks, part_ids(pairs, fsdp))]
     held = held + [(swap(a, "core", 1), 1, ids) for a, _, ids in held]
     return place_rows(place, held, r, fsdp, 2 * pairs * fsdp * r)
 
@@ -641,21 +655,27 @@
         return [
             lax.psum_scatter(g.astype(F32), ALL, scatter_dimension=0, tiled=True) for g in arrays
         ]
-    keep, give = pick_rows(place, arrays, r, pairs, fsdp)
+    *keep, give = pick_rows(place, arrays, r, pairs, fsdp)
     (got,) = yield [swap(give, "core", 1)]
-    half = keep.shape[0] // 2
+    cut = keep[0].shape[0]
     orders = bit_orders(pairs)
-    blocks = []
-    for part in range(2):
-        at = slice(part * half, (part + 1) * half)
-        blocks.append(keep[at].astype(F32) + got[at].astype(F32))
+    quarters = [
+        (a.astype(F32) + got[i * cut : (i + 1) * cut].astype(F32)).astype(BF)
+        for i, a in enumerate(keep)
+    ]
+    near, far = quarters[0::2], quarters[1::2]
     for level in reversed(range(len(orders[0]))):
-        cut = blocks[0].shape[0] // 2
         others = yield [
-            swap(block[cut:].astype(BF), "pair", 1 << order[level])
-            for block, order in zip(blocks, orders)
+            swap(a, "pair", 1 << order[level]) for a, order in zip(far, orders)
         ]
-        blocks = [block[:cut] + other.astype(F32) for block, other in zip(blocks, others)]
+        blocks = [(a, b) for a, b in zip(near, others)]
+        if level:
+            cut = near[0].shape[0] // 2
+            near = [
+                (a[:cut].astype(F32) + b[:cut].astype(F32)).astype(BF) for a, b in blocks
+            ]
+            far = [(a[cut:].astype(F32) + b[cut:].astype(F32)).astype(BF) for a, b in blocks]
+    blocks = [a.astype(F32) + b.astype(F32) for a, b in blocks]
     others = yield [
         swap(
             blocks[k // (fsdp // 2)][(k % (fsdp // 2)) * r :][:r].astype(BF), "fsdp", k
@@ -764,20 +784,22 @@
     )
     label_rows = labels.astype(F32).reshape(chunks, 1, CHUNK)
     row_spec = pl.BlockSpec((1, 1, CHUNK), lambda c: (c, 0, 0))
+    halo_spec = pl.BlockSpec((16, CHANNELS), lambda c: (count // 16, 0))
 
     tail = shift(tokens[count - 8 :], 2 * pairs, 1)
+    tail = jnp.concatenate([tail, jnp.zeros_like(tail)], axis=0)
     hidden = hidden_of(tokens, norm_full)
-    halo_hidden = hidden_of(tail, norm_full)
-    mix = jnp.dot(hidden, w_mix, preferred_element_type=F32).astype(BF)
-    halo = jnp.dot(halo_hidden, w_mix[:, :CHANNELS], preferred_element_type=F32)
-    halo = halo.astype(BF).astype(F32)
+    mix = jnp.dot(
+        hidden_of(jnp.concatenate([tokens, tail], axis=0), norm_full), w_mix,
+        preferred_element_type=F32,
+    ).astype(BF)
 
     z, v, k, q, rc, rs, packed = pl.pallas_call(
         prep_kernel,
         name="conv_states",
         grid=(chunks,),
         in_specs=[
-            rows(CHANNELS), raw_rows(), rows(8), whole((8, CHANNELS)), whole((taps, CHANNELS)),
+            rows(CHANNELS), raw_rows(), rows(8), halo_spec, whole((taps, CHANNELS)),
             whole((1, CHANNELS)), whole((1, HEADS)), whole((1, HEADS)), whole((HEADS, DI)),
         ],
         out_specs=[
@@ -794,7 +816,7 @@
         ],
         compiler_params=PARAMS,
         cost_estimate=cost(10**9, 30 * 10**6),
-    )(mix, mix, info, halo, conv_full, bias_full, rate, sbias, expand)
+    )(mix, mix, info, mix, conv_full, bias_full, rate, sbias, expand)
 
     forward = Steps(carry_states(packed, pairs, False))
     forward.beside()
@@ -890,7 +912,7 @@
             back(CHANNELS), raw_rows(chunks), back(CHANNELS), back(DI), back(STATE), back(STATE),
             back(HEADS), back(CHUNK, per=HEADS), back(8), back(DI), back(DI), back(HEADS),
             back(HEADS), back(STATE), back(STATE), back(DI), whole((STATE, DI)),
-            whole((8, CHANNELS)), whole((taps, CHANNELS)), whole((1, HEADS)),
+            halo_spec, whole((taps, CHANNELS)), whole((1, HEADS)),
             whole((1, HEADS)), whole((1, DI)), whole((HEADS, DI)),
         ],
         out_specs=[
@@ -909,7 +931,7 @@
         cost_estimate=cost(2 * 10**9, 60 * 10**6),
     )(
         mix, mix, z, v, k, q, rc, rs, info, dy, dv, uv, u, dq, dk, states, coming_back,
-        halo, conv_full, rate, sbias, skip_wide, expand,
+        mix, conv_full, rate, sbias, skip_wide, expand,
     )
 
     grad_mix, dhalo = gate_steps.beside(grad_mix, dhalo)

time: 443 us -> 419 us (0.946)
  Pallas kernels: 155 us -> 147 us
  waiting for transfers between devices: 75.5 us -> 70.7 us
    add x8 -> x2, other arithmetic: 12.7 us -> 1.64 us  [reduce_rows(): blocks = [a.astype(F32) + b.astype(F32) for a, b in blocks]]
    convert_element_type x0 -> x6, other arithmetic: none -> 11 us  [the longest x2 5.96 us: reduce_rows(): (a.astype(F32) + got[i * cut:(i + 1) * cut].astype(F32)).astype(BF)]
    slice x8 -> x0, local copies, waits for them, and re-layouts: 5.71 us -> none  [reduce_rows(): block[cut:].astype(BF)]
    ppermute x38, waiting for transfers between devices: 75.5 us -> 70.7 us  [swap(): return lax.ppermute(block, axis, [(i, i ^ mask) for i in range(count)])]
    dot_general x2 -> x1, matrix products: 13.9 us -> 10.8 us  [on_device(): jnp.dot(hidden_of(jnp.concatenate([tokens, tail], axis=0), norm_full), w_...]
  transfers between devices with their start and end apart: 41 -> 41, of which waited for: 17 -> 19; matrix products, arithmetic and copies ran while one was open for 29% -> 29% of each run, Pallas kernels for 26% -> 26%
where the time goes in v4:
time: 419 us; the launch traced here: 415 us
  Pallas kernels  147 us (35%)
  matrix products  73 us (17%)
  waiting for transfers between devices  70.7 us (17%)
  starting transfers between devices  44.7 us (11%)
  other arithmetic  42.6 us (10%)
  local copies, waits for them, and re-layouts  21.7 us (5%)
  between operations  15.1 us (4%)
    ppermute x38, waiting for transfers between devices, swap(): return lax.ppermute(block, axis, [(i, i ^ mask) for i in range(count)])  70.7 us
    ppermute x38, starting transfers between devices, swap(): return lax.ppermute(block, axis, [(i, i ^ mask) for i in range(count)])  42.1 us
    pallas_call x1, Pallas kernels, on_device(): pl.pallas_call(back_kernel, name='states_conv_back', grid=(chunks,), in_s...  35.3 us
    pallas_call x1, Pallas kernels, on_device(): pl.pallas_call(gate_kernel, name='gate_norm', grid=(chunks,), in_specs=[r...  31.3 us
    pallas_call x1, Pallas kernels, on_device(): pl.pallas_call(intra_back_kernel, name='intra_back', grid=(chunks,), in_s...  26.5 us
    pallas_call x1, Pallas kernels, on_device(): pl.pallas_call(prep_kernel, name='conv_states', grid=(chunks,), in_specs=...  17.9 us
    pallas_call x2, Pallas kernels, pick_rows(): pl.pallas_call(body, name='pick_rows', in_specs=[pl.BlockSpec(memory_spac...  12.3 us
    pallas_call x1, Pallas kernels, on_device(): pl.pallas_call(intra_kernel, name='intra', grid=(chunks,), in_specs=[rows...  11.5 us
  transfers between devices with their start and end apart: 41, of which 19 were waited for; matrix products, arithmetic and copies ran while one was open for 29% of the time, Pallas kernels for 26%

profile of v4, /device:TPU:0, one launch (start us, length us, event | category | flops | bytes accessed | tf_op | source)
XLA Modules:
  0.0 414.7 jit_solution(5384892103700187624)
XLA Ops:
  9.9 5.1 %collective-permute-start.4 = (bf16[32,2432]{1,0:T(8,128)(2,1)S(1)}, bf16[32,2432]{1,0:T(8,128)(2,1)S(1)}, u32[]{:S(2)}, u32[]{:S(2)}) collective-permute-start(bf16[32,2432]{1,0:T(8,128)(2,1)S(1)} %pad_maximum_fusion.12), channel_id=1, source_target_pairs={{0,3},{1,2},{2,1},{3,0},{4,7},{5,6},{6,5},{7,4},{8,11},{9,10},{10,... | collective-permute-start | bytes 466952 | tf_op jit(solution)/shard_map/ppermute | solution.py:525
  15.6 4.3 %collective-permute-done.4 = bf16[32,2432]{1,0:T(8,128)(2,1)S(1)} collective-permute-done((bf16[32,2432]{1,0:T(8,128)(2,1)S(1)}, bf16[32,2432]{1,0:T(8,128)(2,1)S(1)}, u32[]{:S(2)}, u32[]{:S(2)}) %collective-permute-start.4) | collective-permute-done | bytes 155680 | tf_op jit(solution)/shard_map/ppermute | solution.py:525
  19.9 8.2 %collective-permute-done.3 = bf16[32,2432]{1,0:T(8,128)(2,1)S(1)} collective-permute-done((bf16[32,2432]{1,0:T(8,128)(2,1)S(1)}, bf16[32,2432]{1,0:T(8,128)(2,1)S(1)}, u32[]{:S(2)}, u32[]{:S(2)}) %collective-permute-start.3) | collective-permute-done | bytes 155680 | tf_op jit(solution)/shard_map/ppermute | solution.py:525
  31.3 5.3 %collective-permute-done.5 = bf16[64,2432]{1,0:T(8,128)(2,1)S(1)} collective-permute-done((bf16[64,2432]{1,0:T(8,128)(2,1)S(1)}, bf16[64,2432]{1,0:T(8,128)(2,1)S(1)}, u32[]{:S(2)}, u32[]{:S(2)}) %collective-permute-start.5) | collective-permute-done | bytes 311328 | tf_op jit(solution)/shard_map/ppermute | solution.py:525
  52.5 12.9 %collective-permute-done.7 = bf16[128,2432]{1,0:T(8,128)(2,1)S(1)} collective-permute-done((bf16[128,2432]{1,0:T(8,128)(2,1)S(1)}, bf16[128,2432]{1,0:T(8,128)(2,1)S(1)}, u32[]{:S(2)}, u32[]{:S(2)}) %collective-permute-start.7) | collective-permute-done | bytes 622624 | tf_op jit(solution)/shard_map/ppermute | solution.py:525
  72.8 5.1 %place_rows.1 = bf16[1024,2432]{1,0:T(8,128)(2,1)} custom-call(s32[3]{0:T(128)} %pad_add_fusion.place_ref, bf16[256,2432]{1,0:T(8,128)(2,1)} %copy-done.1, bf16[256,2432]{1,0:T(8,128)(2,1)} %constant_dynamic-update-slice_fusion.refs_1_, bf16[256,2432]{1,0:T(8,128)(2,1)} %collective-permute-done.8.refs_2_, bf16[256,2432]{1,0:T(8,128)(2,1)} %collective-permute-done.9.refs_3_), custom_call_target="tpu_custom_call" | custom-call | bytes 9961472 | tf_op jit(solution)/shard_map/place_rows/pallas_call | solution.py:558
  80.9 10.8 %convolution_convert_fusion.x_ref.raw_ref.halo_ref = bf16[1040,2432]{1,0:T(8,128)(2,1)} fusion(bf16[1024,2432]{1,0:T(8,128)(2,1)} %place_rows.1, f32[1024]{0:T(1024)S(1)} %reshape.210, f32[1040]{0:T(1024)S(1)} %add_rsqrt_fusion, bf16[8,1024]{1,0:T(8,128)(2,1)S(1)} %collective-permute-done, bf16[1024,1024]{1,0:T(8,128)(2,1)S(1)} %bitcast.92, ...), kind=kOutput, calls=%fused_computation | convolution fusion | flops 5192079360 | bytes 12163168 | tf_op jit(solution)/shard_map/dot_general | solution.py:792
  91.7 17.9 %conv_states.1 = (bf16[1024,2304]{1,0:T(8,128)(2,1)}, bf16[1024,2048]{1,0:T(8,128)(2,1)}, f32[1024,128]{1,0:T(8,128)}, f32[1024,128]{1,0:T(8,128)}, f32[1024,32]...) custom-call(bf16[1040,2432]{1,0:T(8,128)(2,1)} %convolution_convert_fusion.x_ref.raw_ref.halo_ref, ...), custom_call_target="tpu_custom_call" | custom-call | flops 1000000000 | bytes 30000000 | tf_op jit(solution)/shard_map/conv_states/pallas_call | solution.py:797
  116.6 11.5 %intra.1.y_ref = f32[1024,2048]{1,0:T(8,128)} custom-call(f32[1024,128]{1,0:T(8,128)} %get-tuple-element.77.q_ref, f32[1024,128]{1,0:T(8,128)} %get-tuple-element.78.k_ref, bf16[1024,2048]{1,0:T(8,128)(2,1)} %get-tuple-element.79.v_ref, f32[1024,32]{1,0:T(8,128)} %get-tuple-element.80.rc_ref, f32[256,128]{1,0:T(8,128)} %get-tuple-element.81.rs_ref, ...), custom_call_target="tpu_custom_call" | custom-call | flops 1000000000 | bytes 30000000 | tf_op jit(solution)/shard_map/intra/pallas_call | solution.py:824
  131.6 7.1 %unpack_weights.1 = (bf16[1024,2048]{1,0:T(8,128)(2,1)}, bf16[2048,1024]{1,0:T(8,128)(2,1)}) custom-call(bf16[1024,4096]{1,0:T(8,128)(2,1)} %all-gather.2.cloned.1.call-done.src), custom_call_target="tpu_custom_call" | custom-call | bytes 16777216 | tf_op jit(solution)/shard_map/unpack_weights/pallas_call | solution.py:619
  138.7 8.6 %convolution_convert_fusion.4.gate_ref = bf16[1024,2048]{1,0:T(8,128)(2,1)} fusion(bf16[1024,2048]{1,0:T(8,128)(2,1)} %get-tuple-element.86, f32[1024]{0:T(1024)S(1)} %reshape.210, f32[1024]{0:T(1024)S(1)} %add_rsqrt_fusion.1, bf16[1,1024,1024]{2,1,0:T(8,128)(2,1)S(1)} %copy-done), kind=kOutput, calls=%fused_computation.26 | convolution fusion | flops 4301258752 | bytes 10493952 | tf_op jit(solution)/shard_map/dot_general | solution.py:839
  147.3 6.8 %convolution_bitcast_fusion.dn_ref = f32[1024,2048]{1,0:T(8,128)} fusion(bf16[2048,1024]{1,0:T(8,128)(2,1)S(1)} %copy-done.29, bf16[1,1024,1024]{2,1,0:T(8,128)(2,1)S(1)} %copy-done.7), kind=kOutput, calls=%fused_computation.11 | convolution fusion | flops 4294967296 | bytes 14680064 | tf_op jit(solution)/shard_map/dot_general | solution.py:840
  159.4 31.3 %gate_norm.1 = (bf16[1024,2048]{1,0:T(8,128)(2,1)}, bf16[1024,2048]{1,0:T(8,128)(2,1)}, bf16[1024,2048]{1,0:T(8,128)(2,1)}, bf16[1024,2048]{1,0:T(8,128)(2,1)}, ...) custom-call(f32[1024,2048]{1,0:T(8,128)} %intra.1.y_ref, ...), custom_call_target="tpu_custom_call" | custom-call | flops 1000000000 | bytes 50000000 | tf_op jit(solution)/shard_map/gate_norm/pallas_call | solution.py:844
  191.9 8.8 %convolution_convert_fusion.3.refs_0_ = bf16[1024,2048]{1,0:T(8,128)(2,1)} fusion(bf16[1024,2048]{1,0:T(8,128)(2,1)} %get-tuple-element.92, f32[1024]{0:T(1024)S(1)} %reshape.210, f32[1024]{0:T(1024)S(1)} %add_rsqrt_fusion.1, bf16[1,1024,1024]{2,1,0:T(8,128)(2,1)S(1)} %copy-done), kind=kOutput, calls=%fused_computation.25 | convolution fusion | flops 4301258752 | bytes 10493952 | tf_op jit(solution)/shard_map/dot_general | solution.py:875
  201.5 6.7 %convolution_convert_fusion.2.refs_1_ = bf16[2048,1024]{1,0:T(8,128)(2,1)} fusion(bf16[1024,2048]{1,0:T(8,128)(2,1)S(1)} %copy-done.30, bf16[1,1024,1024]{2,1,0:T(8,128)(2,1)S(1)} %copy-done.8), kind=kOutput, calls=%fused_computation.24 | convolution fusion | flops 4297064448 | bytes 10485760 | tf_op jit(solution)/shard_map/dot_general | solution.py:877
  210.0 7.3 %pick_rows.2 = (bf16[128,4096]{1,0:T(8,128)(2,1)}, bf16[128,4096]{1,0:T(8,128)(2,1)}, bf16[128,4096]{1,0:T(8,128)(2,1)}, bf16[128,4096]{1,0:T(8,128)(2,1)}, bf16[512,4096]{1,0:T(8,128)(2,1)}) custom-call(s32[3]{0:T(128)} %pad_add_fusion.place_ref, bf16[1024,2048]{1,0:T(8,128)(2,1)} %convolution_convert_fusion.3.refs_0_, ...), custom_call_target="tpu_custom_call" | custom-call | bytes 16777216 | tf_op jit(solution)/shard_map/pick_rows/pallas_call | solution.py:592
  217.3 9.4 %fusion.15 = bf16[1024,1024]{1,0:T(8,128)(2,1)} fusion(bf16[1024,2048]{1,0:T(8,128)(2,1)} %get-tuple-element.94, bf16[2048,1024]{1,0:T(8,128)(2,1)} %get-tuple-element.87, bf16[1,1024,1024]{2,1,0:T(8,128)(2,1)S(1)} %copy-done), kind=kOutput, calls=%fused_computation.23 | convolution fusion | flops 4298113024 | bytes 12582912 | tf_op jit(solution)/shard_map/dot_general | solution.py:881
  227.8 5.4 %add_convert_fusion = (bf16[128,4096]{1,0:T(8,128)(2,1)}, bf16[128,4096]{1,0:T(8,128)(2,1)}, bf16[128,4096]{1,0:T(8,128)(2,1)}, bf16[128,4096]{1,0:T(8,128)(2,1)}) fusion(bf16[128,4096]{1,0:T(8,128)(2,1)S(1)} %copy-done.17, bf16[512,4096]{1,0:T(8,128)(2,1)} %collective-permute-done.17, bf16[128,4096]{1,0:T(8,128)(2,1)S(1)} %copy-done.18, ...), kind=kLoop, calls=%fused_computation.32 | loop fusion | flops 8388608 | bytes 12582912 | tf_op jit(solution)/shard_map/convert_element_type | solution.py:663
  235.0 6.1 %fusion.50 = f32[1024,1024]{1,0:T(8,128)} fusion(bf16[1024,2048]{1,0:T(8,128)(2,1)S(1)} %copy-done.28, bf16[1024,2048]{1,0:T(8,128)(2,1)S(1)} %copy-done.27), kind=kOutput, calls=%fused_computation.172 | convolution fusion | flops 4294967296 | bytes 12582912 | tf_op jit(solution)/shard_map/dot_general | solution.py:944
  242.5 26.5 %intra_back.1 = (bf16[1024,2048]{1,0:T(8,128)(2,1)}, f32[1024,32]{1,0:T(8,128)}, f32[1024,128]{1,0:T(8,128)}, f32[1024,128]{1,0:T(8,128)}) custom-call(f32[1024,128]{1,0:T(8,128)} %get-tuple-element.77.q_ref, f32[1024,128]{1,0:T(8,128)} %get-tuple-element.78.k_ref, bf16[1024,2048]{1,0:T(8,128)(2,1)} %get-tuple-element.79.v_ref, ...), custom_call_target="tpu_custom_call" | custom-call | flops 2000000000 | bytes 40000000 | tf_op jit(solution)/shard_map/intra_back/pallas_call | solution.py:886
  277.5 35.3 %states_conv_back.1 = (bf16[1024,2432]{1,0:T(8,128)(2,1)}, f32[8,2304]{1,0:T(8,128)}, f32[40,2304]{1,0:T(8,128)}, f32[16,32]{1,0:T(8,128)}) custom-call(bf16[1040,2432]{1,0:T(8,128)(2,1)} %convolution_convert_fusion.x_ref.raw_ref.halo_ref, bf16[1040,2432]{1,0:T(8,128)(2,1)} %convolution_convert_fusion.x_ref.raw_ref.halo_ref, ...), custom_call_target="tpu_custom_call" | custom-call | flops 2000000000 | bytes 60000000 | tf_op jit(solution)/shard_map/states_conv_back/pallas_call | solution.py:907
  321.6 3.0 collective-permute-start.25
  325.1 7.8 %convolution_convert_fusion.1.refs_0_ = bf16[1024,2432]{1,0:T(8,128)(2,1)} fusion(bf16[1024,2432]{1,0:T(8,128)(2,1)S(1)} %fusion.30, f32[1024]{0:T(1024)S(1)} %reshape.210, f32[1024]{0:T(1024)S(1)} %add_rsqrt_fusion.1, bf16[1,1024,1024]{2,1,0:T(8,128)(2,1)S(1)} %copy-done), kind=kOutput, calls=%fused_computation.8 | convolution fusion | flops 5106958336 | bytes 12066816 | tf_op jit(solution)/shard_map/dot_general | solution.py:942
  333.0 7.8 %fusion.13 = (f32[1024]{0:T(1024)S(1)}, f32[1024]{0:T(1024)S(1)}, f32[1024,1024]{1,0:T(8,128)}) fusion(f32[1024]{0:T(1024)S(1)} %add_rsqrt_fusion.1, bf16[1,1024,1024]{2,1,0:T(8,128)(2,1)S(1)} %copy-done, f32[1024]{0:T(1024)S(1)} %reshape.210, f32[1024,1024]{1,0:T(8,128)S(1)} %copy-done.32, bf16[1024,2432]{1,0:T(8,128)(2,1)S(1)} %fusion.30, ...), kind=kOutput, calls=%fused_computation.21 | convolution fusion | flops 5108660224 | bytes 20463616 | tf_op jit(solution)/shard_map/dot_general | solution.py:945
  340.8 5.0 %pick_rows.3 = (bf16[128,2432]{1,0:T(8,128)(2,1)}, bf16[128,2432]{1,0:T(8,128)(2,1)}, bf16[128,2432]{1,0:T(8,128)(2,1)}, bf16[128,2432]{1,0:T(8,128)(2,1)}, bf16[512,2432]{1,0:T(8,128)(2,1)}) custom-call(s32[3]{0:T(128)} %pad_add_fusion.place_ref, bf16[1024,2432]{1,0:T(8,128)(2,1)} %convolution_convert_fusion.1.refs_0_), custom_call_target="tpu_custom_call" | custom-call | bytes 9961472 | tf_op jit(solution)/shard_map/pick_rows/pallas_call | solution.py:592
  346.6 4.3 %collective-permute-done.35 = f32[32,552]{1,0:T(8,128)S(1)} collective-permute-done((f32[32,552]{1,0:T(8,128)S(1)}, f32[32,552]{1,0:T(8,128)S(1)}, u32[]{:S(2)}, u32[]{:S(2)}) %collective-permute-start.35) | collective-permute-done | bytes 70688 | tf_op jit(solution)/shard_map/ppermute | solution.py:525
  353.2 4.9 %fusion.12 = f32[1,1024,1024]{2,1,0:T(8,128)} fusion(f32[1024,1024]{1,0:T(8,128)} %get-tuple-element.191, bf16[1,1024,1024]{2,1,0:T(8,128)(2,1)} %param.24, f32[1024]{0:T(1024)S(1)} %broadcast_multiply_fusion, f32[1024]{0:T(1024)S(1)} %reshape.210, f32[1024]{0:T(1024)S(1)} %add_rsqrt_fusion.1, bf16[1,1024,1024]{2,1,0:T(8,128)(2,1)S(1)} %copy-done), kind=kLoop, calls=%fused_computation.20 | loop fusion | flops 8388608 | bytes 12595200 | tf_op jit(solution)/shard_map/broadcast_in_dim | solution.py:985
  373.1 9.5 %collective-permute-done.31 = bf16[128,2432]{1,0:T(8,128)(2,1)} collective-permute-done((bf16[128,2432]{1,0:T(8,128)(2,1)S(1)}, bf16[128,2432]{1,0:T(8,128)(2,1)}, u32[]{:S(2)}, u32[]{:S(2)}) %collective-permute-start.31) | collective-permute-done | bytes 622624 | tf_op jit(solution)/shard_map/ppermute | solution.py:525
  384.0 2.9 collective-permute-done.28
  388.2 4.0 collective-permute-done.32
  394.5 2.8 collective-permute-start.34
  398.1 8.3 %collective-permute-done.33 = bf16[32,2432]{1,0:T(8,128)(2,1)S(1)} collective-permute-done((bf16[32,2432]{1,0:T(8,128)(2,1)S(1)}, bf16[32,2432]{1,0:T(8,128)(2,1)S(1)}, u32[]{:S(2)}, u32[]{:S(2)}) %collective-permute-start.33) | collective-permute-done | bytes 155680 | tf_op jit(solution)/shard_map/ppermute | solution.py:525
  (270 shorter events, 99.0 us)
Async XLA Ops:
  7.2 124.4 %all-gather.2.cloned.1.call-start = ((), (), s32[]{:S(2)}) async-start(), calls=%async_computation | async-start | bytes 8650752 | tf_op jit(solution)/shard_map/all_gather | solution.py:751
  9.9 10.0 %collective-permute-start.4 = (bf16[32,2432]{1,0:T(8,128)(2,1)S(1)}, bf16[32,2432]{1,0:T(8,128)(2,1)S(1)}, u32[]{:S(2)}, u32[]{:S(2)}) collective-permute-start(bf16[32,2432]{1,0:T(8,128)(2,1)S(1)} %pad_maximum_fusion.12), channel_id=1, source_target_pairs={{0,3},{1,2},{2,1},{3,0},{4,7},{5,6},{6,5},{7,4},{8,11},{9,10},{10,... | collective-permute-start | bytes 466952 | tf_op jit(solution)/shard_map/ppermute | solution.py:525
  14.9 13.2 %collective-permute-start.3 = (bf16[32,2432]{1,0:T(8,128)(2,1)S(1)}, bf16[32,2432]{1,0:T(8,128)(2,1)S(1)}, u32[]{:S(2)}, u32[]{:S(2)}) collective-permute-start(bf16[32,2432]{1,0:T(8,128)(2,1)S(1)} %pad_maximum_fusion.12), channel_id=1, source_target_pairs={{0,2},{1,3},{2,0},{3,1},{4,6},{5,7},{6,4},{7,5},{8,10},{9,11},{10,... | collective-permute-start | bytes 466952 | tf_op jit(solution)/shard_map/ppermute | solution.py:525
  14.9 14.8 %collective-permute-start.1 = (bf16[32,2432]{1,0:T(8,128)(2,1)S(1)}, bf16[32,2432]{1,0:T(8,128)(2,1)S(1)}, u32[]{:S(2)}, u32[]{:S(2)}) collective-permute-start(bf16[32,2432]{1,0:T(8,128)(2,1)S(1)} %pad_maximum_fusion.12), channel_id=1, source_target_pairs={{0,1},{1,0},{2,3},{3,2},{4,5},{5,4},{6,7},{7,6},{8,9},{9,8},{10,11... | collective-permute-start | bytes 466952 | tf_op jit(solution)/shard_map/ppermute | solution.py:525
  28.1 8.5 %collective-permute-start.5 = (bf16[64,2432]{1,0:T(8,128)(2,1)S(1)}, bf16[64,2432]{1,0:T(8,128)(2,1)S(1)}, u32[]{:S(2)}, u32[]{:S(2)}) collective-permute-start(bf16[64,2432]{1,0:T(8,128)(2,1)S(1)} %pad_maximum_fusion.7), channel_id=1, source_target_pairs={{0,16},{8,24},{16,0},{24,8},{1,17},{9,25},{17,1},{25,9},{2,18},{10... | collective-permute-start | bytes 933896 | tf_op jit(solution)/shard_map/ppermute | solution.py:525
  29.7 8.2 %collective-permute-start.2 = (bf16[64,2432]{1,0:T(8,128)(2,1)S(1)}, bf16[64,2432]{1,0:T(8,128)(2,1)S(1)}, u32[]{:S(2)}, u32[]{:S(2)}) collective-permute-start(bf16[64,2432]{1,0:T(8,128)(2,1)S(1)} %pad_maximum_fusion.6), channel_id=1, source_target_pairs={{0,8},{8,0},{16,24},{24,16},{1,9},{9,1},{17,25},{25,17},{2,10},{10... | collective-permute-start | bytes 933896 | tf_op jit(solution)/shard_map/ppermute | solution.py:525
  41.5 30.5 %collective-permute-start = (bf16[8,1024]{1,0:T(8,128)(2,1)S(1)}, bf16[8,1024]{1,0:T(8,128)(2,1)S(1)}, u32[]{:S(2)}, u32[]{:S(2)}) collective-permute-start(bf16[8,1024]{1,0:T(8,128)(2,1)S(1)} %slice_bitcast_fusion), channel_id=1, source_target_pairs={{0,4},{4,8},{8,12},{12,16},{16,20},{20,24},{24,28},{1,5},{5,9},{9,... | collective-permute-start | bytes 49160 | tf_op jit(solution)/shard_map/ppermute | solution.py:520
  49.0 16.4 %collective-permute-start.7 = (bf16[128,2432]{1,0:T(8,128)(2,1)S(1)}, bf16[128,2432]{1,0:T(8,128)(2,1)S(1)}, u32[]{:S(2)}, u32[]{:S(2)}) collective-permute-start(bf16[128,2432]{1,0:T(8,128)(2,1)S(1)} %pad_maximum_fusion.2), channel_id=1, source_target_pairs={{0,8},{8,0},{16,24},{24,16},{1,9},{9,1},{17,25},{25,17},{2,10},{10... | collective-permute-start | bytes 1867784 | tf_op jit(solution)/shard_map/ppermute | solution.py:525
  51.2 16.3 %collective-permute-start.6 = (bf16[128,2432]{1,0:T(8,128)(2,1)S(1)}, bf16[128,2432]{1,0:T(8,128)(2,1)S(1)}, u32[]{:S(2)}, u32[]{:S(2)}) collective-permute-start(bf16[128,2432]{1,0:T(8,128)(2,1)S(1)} %pad_maximum_fusion.1), channel_id=1, source_target_pairs={{0,16},{8,24},{16,0},{24,8},{1,17},{9,25},{17,1},{25,9},{2,18},{10... | collective-permute-start | bytes 1867784 | tf_op jit(solution)/shard_map/ppermute | solution.py:525
  114.5 14.8 %collective-permute-start.11 = (f32[130,1024]{1,0:T(8,128)S(1)}, f32[130,1024]{1,0:T(8,128)S(1)}, u32[]{:S(2)}, u32[]{:S(2)}) collective-permute-start(f32[130,1024]{1,0:T(8,128)S(1)} %pad_maximum_fusion.4), channel_id=1, source_target_pairs={{0,8},{8,0},{16,24},{24,16},{1,9},{9,1},{17,25},{25,17},{2,10},{10... | collective-permute-start | bytes 1597448 | tf_op jit(solution)/shard_map/ppermute | solution.py:525
  130.2 23.9 %collective-permute-start.12 = (f32[130,1024]{1,0:T(8,128)S(1)}, f32[130,1024]{1,0:T(8,128)}, u32[]{:S(2)}, u32[]{:S(2)}) collective-permute-start(f32[130,1024]{1,0:T(8,128)S(1)} %pad_maximum_fusion.5), channel_id=1, source_target_pairs={{0,16},{8,24},{16,0},{24,8},{1,17},{9,25},{17,1},{25,9},{2,18},{10... | collective-permute-start | bytes 1597448 | tf_op jit(solution)/shard_map/ppermute | solution.py:525
  191.7 9.0 %collective-permute-start.14 = (bf16[130,1024]{1,0:T(8,128)(2,1)S(1)}, bf16[130,1024]{1,0:T(8,128)(2,1)S(1)}, u32[]{:S(2)}, u32[]{:S(2)}) collective-permute-start(bf16[130,1024]{1,0:T(8,128)(2,1)S(1)} %broadcast_select_fusion.1), channel_id=1, source_target_pairs={{0,4},{4,0},{1,5},{5,1},{2,6},{6,2},{3,7},{7,3},{8,12},{12,8},{9,1... | collective-permute-start | bytes 798728 | tf_op jit(solution)/shard_map/ppermute | solution.py:525
  201.0 9.0 %collective-permute-start.15 = (bf16[130,1024]{1,0:T(8,128)(2,1)S(1)}, bf16[130,1024]{1,0:T(8,128)(2,1)S(1)}, u32[]{:S(2)}, u32[]{:S(2)}) collective-permute-start(bf16[130,1024]{1,0:T(8,128)(2,1)S(1)} %pad_maximum_fusion.8), channel_id=1, source_target_pairs={{0,8},{8,0},{16,24},{24,16},{1,9},{9,1},{17,25},{25,17},{2,10},{10... | collective-permute-start | bytes 798728 | tf_op jit(solution)/shard_map/ppermute | solution.py:525
  217.3 10.4 %collective-permute-start.17 = (bf16[512,4096]{1,0:T(8,128)(2,1)}, bf16[512,4096]{1,0:T(8,128)(2,1)}, u32[]{:S(2)}, u32[]{:S(2)}) collective-permute-start(bf16[512,4096]{1,0:T(8,128)(2,1)} %get-tuple-element.98), channel_id=1, source_target_pairs={{0,4},{4,0},{1,5},{5,1},{2,6},{6,2},{3,7},{7,3},{8,12},{12,8},{9,1... | collective-permute-start | bytes 12582920 | tf_op jit(solution)/shard_map/ppermute | solution.py:525
  227.1 14.2 %collective-permute-start.16 = (bf16[130,1024]{1,0:T(8,128)(2,1)S(1)}, bf16[130,1024]{1,0:T(8,128)(2,1)S(1)}, u32[]{:S(2)}, u32[]{:S(2)}) collective-permute-start(bf16[130,1024]{1,0:T(8,128)(2,1)S(1)} %pad_maximum_fusion.9), channel_id=1, source_target_pairs={{0,16},{8,24},{16,0},{24,8},{1,17},{9,25},{17,1},{25,9},{2,18},{10... | collective-permute-start | bytes 798728 | tf_op jit(solution)/shard_map/ppermute | solution.py:525
  233.2 35.9 %collective-permute-start.19 = (bf16[128,4096]{1,0:T(8,128)(2,1)}, bf16[128,4096]{1,0:T(8,128)(2,1)}, u32[]{:S(2)}, u32[]{:S(2)}) collective-permute-start(bf16[128,4096]{1,0:T(8,128)(2,1)} %get-tuple-element.154), channel_id=1, source_target_pairs={{0,8},{8,0},{16,24},{24,16},{1,9},{9,1},{17,25},{25,17},{2,10},{10... | collective-permute-start | bytes 3145736 | tf_op jit(solution)/shard_map/ppermute | solution.py:525
  234.5 34.6 %collective-permute-start.18 = (bf16[128,4096]{1,0:T(8,128)(2,1)}, bf16[128,4096]{1,0:T(8,128)(2,1)}, u32[]{:S(2)}, u32[]{:S(2)}) collective-permute-start(bf16[128,4096]{1,0:T(8,128)(2,1)} %get-tuple-element.155), channel_id=1, source_target_pairs={{0,16},{8,24},{16,0},{24,8},{1,17},{9,25},{17,1},{25,9},{2,18},{10... | collective-permute-start | bytes 3145736 | tf_op jit(solution)/shard_map/ppermute | solution.py:525
  242.2 26.9 %collective-permute-start.22 = (bf16[128,1024]{1,0:T(8,128)(2,1)S(1)}, bf16[128,1024]{1,0:T(8,128)(2,1)}, u32[]{:S(2)}, u32[]{:S(2)}) collective-permute-start(bf16[128,1024]{1,0:T(8,128)(2,1)S(1)} %get-tuple-element.166), channel_id=1, source_target_pairs={{0,4},{4,0},{1,5},{5,1},{2,6},{6,2},{3,7},{7,3},{8,12},{12,8},{9,1... | collective-permute-start | bytes 786440 | tf_op jit(solution)/shard_map/ppermute | solution.py:525
  272.1 43.0 %collective-permute-start.21 = (bf16[64,4096]{1,0:T(8,128)(2,1)}, bf16[64,4096]{1,0:T(8,128)(2,1)}, u32[]{:S(2)}, u32[]{:S(2)}) collective-permute-start(bf16[64,4096]{1,0:T(8,128)(2,1)} %add_convert_fusion.11), channel_id=1, source_target_pairs={{0,16},{8,24},{16,0},{24,8},{1,17},{9,25},{17,1},{25,9},{2,18},{10... | collective-permute-start | bytes 1572872 | tf_op jit(solution)/shard_map/ppermute | solution.py:525
  275.6 39.5 %collective-permute-start.20 = (bf16[64,4096]{1,0:T(8,128)(2,1)}, bf16[64,4096]{1,0:T(8,128)(2,1)}, u32[]{:S(2)}, u32[]{:S(2)}) collective-permute-start(bf16[64,4096]{1,0:T(8,128)(2,1)} %add_convert_fusion.12), channel_id=1, source_target_pairs={{0,8},{8,0},{16,24},{24,16},{1,9},{9,1},{17,25},{25,17},{2,10},{10... | collective-permute-start | bytes 1572872 | tf_op jit(solution)/shard_map/ppermute | solution.py:525
  320.6 37.5 %collective-permute-start.24 = (bf16[32,4096]{1,0:T(8,128)(2,1)S(1)}, bf16[32,4096]{1,0:T(8,128)(2,1)S(1)}, u32[]{:S(2)}, u32[]{:S(2)}) collective-permute-start(bf16[32,4096]{1,0:T(8,128)(2,1)S(1)} %slice.623), channel_id=1, source_target_pairs={{0,1},{1,0},{2,3},{3,2},{4,5},{5,4},{6,7},{7,6},{8,9},{9,8},{10,11... | collective-permute-start | bytes 786440 | tf_op jit(solution)/shard_map/ppermute | solution.py:525
  321.6 36.6 %collective-permute-start.25 = (bf16[32,4096]{1,0:T(8,128)(2,1)}, bf16[32,4096]{1,0:T(8,128)(2,1)S(1)}, u32[]{:S(2)}, u32[]{:S(2)}) collective-permute-start(bf16[32,4096]{1,0:T(8,128)(2,1)} %get-tuple-element.171), channel_id=1, source_target_pairs={{0,2},{1,3},{2,0},{3,1},{4,6},{5,7},{6,4},{7,5},{8,10},{9,11},{10,... | collective-permute-start | bytes 786440 | tf_op jit(solution)/shard_map/ppermute | solution.py:525
  324.5 33.7 %collective-permute-start.26 = (bf16[32,4096]{1,0:T(8,128)(2,1)}, bf16[32,4096]{1,0:T(8,128)(2,1)S(1)}, u32[]{:S(2)}, u32[]{:S(2)}) collective-permute-start(bf16[32,4096]{1,0:T(8,128)(2,1)} %get-tuple-element.172), channel_id=1, source_target_pairs={{0,3},{1,2},{2,1},{3,0},{4,7},{5,6},{6,5},{7,4},{8,11},{9,10},{10,... | collective-permute-start | bytes 786440 | tf_op jit(solution)/shard_map/ppermute | solution.py:525
  345.9 20.9 %collective-permute-start.27 = (bf16[512,2432]{1,0:T(8,128)(2,1)}, bf16[512,2432]{1,0:T(8,128)(2,1)S(1)}, u32[]{:S(2)}, u32[]{:S(2)}) collective-permute-start(bf16[512,2432]{1,0:T(8,128)(2,1)} %get-tuple-element.130), channel_id=1, source_target_pairs={{0,4},{4,0},{1,5},{5,1},{2,6},{6,2},{3,7},{7,3},{8,12},{12,8},{9,1... | collective-permute-start | bytes 7471112 | tf_op jit(solution)/shard_map/ppermute | solution.py:525
  351.0 7.0 %collective-permute-start.36 = (f32[32,552]{1,0:T(8,128)S(1)}, f32[32,552]{1,0:T(8,128)S(1)}, u32[]{:S(2)}, u32[]{:S(2)}) collective-permute-start(f32[32,552]{1,0:T(8,128)S(1)} %fusion.63), channel_id=1, source_target_pairs={{0,2},{1,3},{2,0},{3,1},{4,6},{5,7},{6,4},{7,5},{8,10},{9,11},{10,... | collective-permute-start | bytes 211976 | tf_op jit(solution)/shard_map/ppermute | solution.py:525
  367.4 15.2 %collective-permute-start.31 = (bf16[128,2432]{1,0:T(8,128)(2,1)S(1)}, bf16[128,2432]{1,0:T(8,128)(2,1)}, u32[]{:S(2)}, u32[]{:S(2)}) collective-permute-start(bf16[128,2432]{1,0:T(8,128)(2,1)S(1)} %get-tuple-element.158), channel_id=1, source_target_pairs={{0,8},{8,0},{16,24},{24,16},{1,9},{9,1},{17,25},{25,17},{2,10},{10... | collective-permute-start | bytes 1867784 | tf_op jit(solution)/shard_map/ppermute | solution.py:525
  371.1 15.8 %collective-permute-start.28 = (bf16[128,2432]{1,0:T(8,128)(2,1)S(1)}, bf16[128,2432]{1,0:T(8,128)(2,1)S(1)}, u32[]{:S(2)}, u32[]{:S(2)}) collective-permute-start(bf16[128,2432]{1,0:T(8,128)(2,1)S(1)} %get-tuple-element.159), channel_id=1, source_target_pairs={{0,16},{8,24},{16,0},{24,8},{1,17},{9,25},{17,1},{25,9},{2,18},{10... | collective-permute-start | bytes 1867784 | tf_op jit(solution)/shard_map/ppermute | solution.py:525
  383.6 8.5 %collective-permute-start.32 = (bf16[64,2432]{1,0:T(8,128)(2,1)S(1)}, bf16[64,2432]{1,0:T(8,128)(2,1)S(1)}, u32[]{:S(2)}, u32[]{:S(2)}) collective-permute-start(bf16[64,2432]{1,0:T(8,128)(2,1)S(1)} %add_convert_fusion.14), channel_id=1, source_target_pairs={{0,16},{8,24},{16,0},{24,8},{1,17},{9,25},{17,1},{25,9},{2,18},{10... | collective-permute-start | bytes 933896 | tf_op jit(solution)/shard_map/ppermute | solution.py:525
  387.0 10.3 %collective-permute-start.29 = (bf16[64,2432]{1,0:T(8,128)(2,1)S(1)}, bf16[64,2432]{1,0:T(8,128)(2,1)S(1)}, u32[]{:S(2)}, u32[]{:S(2)}) collective-permute-start(bf16[64,2432]{1,0:T(8,128)(2,1)S(1)} %add_convert_fusion.16), channel_id=1, source_target_pairs={{0,8},{8,0},{16,24},{24,16},{1,9},{9,1},{17,25},{25,17},{2,10},{10... | collective-permute-start | bytes 933896 | tf_op jit(solution)/shard_map/ppermute | solution.py:525
  393.3 13.1 %collective-permute-start.33 = (bf16[32,2432]{1,0:T(8,128)(2,1)S(1)}, bf16[32,2432]{1,0:T(8,128)(2,1)S(1)}, u32[]{:S(2)}, u32[]{:S(2)}) collective-permute-start(bf16[32,2432]{1,0:T(8,128)(2,1)S(1)} %get-tuple-element.173), channel_id=1, source_target_pairs={{0,2},{1,3},{2,0},{3,1},{4,6},{5,7},{6,4},{7,5},{8,10},{9,11},{10,... | collective-permute-start | bytes 466952 | tf_op jit(solution)/shard_map/ppermute | solution.py:525
  394.5 11.9 %collective-permute-start.34 = (bf16[32,2432]{1,0:T(8,128)(2,1)S(1)}, bf16[32,2432]{1,0:T(8,128)(2,1)S(1)}, u32[]{:S(2)}, u32[]{:S(2)}) collective-permute-start(bf16[32,2432]{1,0:T(8,128)(2,1)S(1)} %get-tuple-element.174), channel_id=1, source_target_pairs={{0,3},{1,2},{2,1},{3,0},{4,7},{5,6},{6,5},{7,4},{8,11},{9,10},{10,... | collective-permute-start | bytes 466952 | tf_op jit(solution)/shard_map/ppermute | solution.py:525
  397.4 9.3 %collective-permute-start.30 = (bf16[32,2432]{1,0:T(8,128)(2,1)S(1)}, bf16[32,2432]{1,0:T(8,128)(2,1)S(1)}, u32[]{:S(2)}, u32[]{:S(2)}) collective-permute-start(bf16[32,2432]{1,0:T(8,128)(2,1)S(1)} %slice.624), channel_id=1, source_target_pairs={{0,1},{1,0},{2,3},{3,2},{4,5},{5,4},{6,7},{7,6},{8,9},{9,8},{10,11... | collective-permute-start | bytes 466952 | tf_op jit(solution)/shard_map/ppermute | solution.py:525
  (45 other events, 496.9 us)
Sparse Core Ops, SparseCore 0:
  40.7 77.9 all-gather.1

commit v5 on v4

--- a/solution.py
+++ b/solution.py
@@ -16,7 +16,7 @@
 LANES = 128
 DI = HEADS * HEADDIM
 CHANNELS = DI + 2 * STATE
-WIDE = 512
+WIDE = 256
 MIX = CHANNELS + HEADS
 MIX_WIDE = -(-MIX // 128) * 128
 NEG = -1e30
@@ -656,6 +656,7 @@
             lax.psum_scatter(g.astype(F32), ALL, scatter_dimension=0, tiled=True) for g in arrays
         ]
     *keep, give = pick_rows(place, arrays, r, pairs, fsdp)
+    (give,) = yield [give]
     (got,) = yield [swap(give, "core", 1)]
     cut = keep[0].shape[0]
     orders = bit_orders(pairs)
@@ -744,10 +745,10 @@
     mix_gather = Steps(
         gather_rows(jnp.concatenate([in_weight[:, DI:], small], axis=1), place, pairs)
     )
-    in_weight, out_weight = mix_gather.beside(in_weight, out_weight)
     packed_weights = jnp.concatenate(
         [in_weight[:, :DI], out_weight[:r], out_weight[r:]], axis=1
     )
+    (packed_weights,) = mix_gather.beside(packed_weights)
     packed_weights = lax.all_gather(packed_weights, ALL, axis=0, tiled=True)
     w_mix = mix_gather.finish()
     small = w_mix[:, MIX:].reshape(-1, r, slot)[:, :small_rows].reshape(-1, small_rows * slot)
@@ -877,6 +878,7 @@
     grad_out_w = lax.dot_general(normed, upstream, TN, preferred_element_type=F32).astype(BF)
     (grad_out_w,) = backward.beside(grad_out_w)
     gate_steps = Steps(reduce_rows([grad_gate_w, grad_out_w], place, pairs))
+    (normed,) = gate_steps.beside(normed)
     block_out = (
         tokens.astype(F32) + jnp.dot(normed, w_out, preferred_element_type=F32)
     ).astype(BF)
@@ -934,15 +936,17 @@
         mix, conv_full, rate, sbias, skip_wide, expand,
     )
 
-    grad_mix, dhalo = gate_steps.beside(grad_mix, dhalo)
     edge = shift(dhalo, 2 * pairs, -1)
     edge = jnp.pad(edge, ((0, 0), (0, MIX_WIDE - CHANNELS)))
     fixed = (grad_mix[count - 8 :].astype(F32) + edge).astype(BF)
     grad_mix = lax.dynamic_update_slice(grad_mix, fixed, (count - 8, 0))
     grad_mix_w = lax.dot_general(hidden, grad_mix, TN, preferred_element_type=F32).astype(BF)
     mix_steps = Steps(reduce_rows([grad_mix_w], place, pairs))
+    (grad_mix,) = mix_steps.beside(grad_mix)
     grad_hidden = lax.dot_general(dgate, w_gate, NT, preferred_element_type=F32)
     grad_hidden = grad_hidden + lax.dot_general(grad_mix, w_mix, NT, preferred_element_type=F32)
+    (grad_hidden,) = gate_steps.beside(grad_hidden)
+    (grad_hidden,) = mix_steps.beside(grad_hidden)
 
     x = tokens.astype(F32)
     inv = lax.rsqrt(jnp.mean(x * x, axis=-1, keepdims=True) + 1e-05)
@@ -951,6 +955,7 @@
     mean = jnp.mean(scaled * unit, axis=-1, keepdims=True)
     grad_tokens = upstream.astype(F32) + inv * (scaled - unit * mean)
     grad_norm = jnp.sum(grad_hidden * unit, axis=0)
+    grad_tokens, grad_norm = mix_steps.beside(grad_tokens, grad_norm)
 
     conv_sums = conv_sums.reshape(taps + 1, 8, CHANNELS).sum(axis=1)
     gate_sums = gate_sums.reshape(2, 8, DI).sum(axis=1)

time: 419 us -> 435 us (1.038)
  waiting for transfers between devices: 70.7 us -> 81.5 us
  starting transfers between devices: 44.7 us -> 50.4 us
    ppermute x38, waiting for transfers between devices: 70.7 us -> 81.4 us  [swap(): return lax.ppermute(block, axis, [(i, i ^ mask) for i in range(count)])]
    ppermute x38, starting transfers between devices: 42.1 us -> 47.8 us  [swap(): return lax.ppermute(block, axis, [(i, i ^ mask) for i in range(count)])]
    broadcast_in_dim x1 -> x0, other arithmetic: 4.87 us -> none  [on_device(): grad_tokens[None]]
  transfers between devices with their start and end apart: 41 -> 41, of which waited for: 19 -> 20; matrix products, arithmetic and copies ran while one was open for 29% -> 29% of each run, Pallas kernels for 26% -> 17%
where the time goes in v5:
time: 435 us; the launch traced here: 430 us
  Pallas kernels  144 us (33%)
  waiting for transfers between devices  81.5 us (19%)
  matrix products  76.2 us (18%)
  starting transfers between devices  50.4 us (12%)
  other arithmetic  40.9 us (9%)
  local copies, waits for them, and re-layouts  22.6 us (5%)
  between operations  15.1 us (3%)
    ppermute x38, waiting for transfers between devices, swap(): return lax.ppermute(block, axis, [(i, i ^ mask) for i in range(count)])  81.4 us
    ppermute x38, starting transfers between devices, swap(): return lax.ppermute(block, axis, [(i, i ^ mask) for i in range(count)])  47.8 us
    pallas_call x1, Pallas kernels, on_device(): pl.pallas_call(back_kernel, name='states_conv_back', grid=(chunks,), in_s...  35.2 us
    pallas_call x1, Pallas kernels, on_device(): pl.pallas_call(gate_kernel, name='gate_norm', grid=(chunks,), in_specs=[r...  28.4 us
    pallas_call x1, Pallas kernels, on_device(): pl.pallas_call(intra_back_kernel, name='intra_back', grid=(chunks,), in_s...  26.4 us
    pallas_call x1, Pallas kernels, on_device(): pl.pallas_call(prep_kernel, name='conv_states', grid=(chunks,), in_specs=...  17.8 us
    pallas_call x2, Pallas kernels, pick_rows(): pl.pallas_call(body, name='pick_rows', in_specs=[pl.BlockSpec(memory_spac...  12.3 us
    pallas_call x1, Pallas kernels, on_device(): pl.pallas_call(intra_kernel, name='intra', grid=(chunks,), in_specs=[rows...  11.5 us
  transfers between devices with their start and end apart: 41, of which 20 were waited for; matrix products, arithmetic and copies ran while one was open for 29% of the time, Pallas kernels for 17%

profile of v5, /device:TPU:0, one launch (start us, length us, event | category | flops | bytes accessed | tf_op | source)
XLA Modules:
  0.0 430.3 jit_solution(8556514784394003664)
XLA Ops:
  9.9 5.1 %collective-permute-start.4 = (bf16[32,2432]{1,0:T(8,128)(2,1)S(1)}, bf16[32,2432]{1,0:T(8,128)(2,1)S(1)}, u32[]{:S(2)}, u32[]{:S(2)}) collective-permute-start(bf16[32,2432]{1,0:T(8,128)(2,1)S(1)} %pad_maximum_fusion.12), channel_id=1, source_target_pairs={{0,3},{1,2},{2,1},{3,0},{4,7},{5,6},{6,5},{7,4},{8,11},{9,10},{10,... | collective-permute-start | bytes 466952 | tf_op jit(solution)/shard_map/ppermute | solution.py:525
  19.9 8.2 %collective-permute-done.3 = bf16[32,2432]{1,0:T(8,128)(2,1)S(1)} collective-permute-done((bf16[32,2432]{1,0:T(8,128)(2,1)S(1)}, bf16[32,2432]{1,0:T(8,128)(2,1)S(1)}, u32[]{:S(2)}, u32[]{:S(2)}) %collective-permute-start.3) | collective-permute-done | bytes 155680 | tf_op jit(solution)/shard_map/ppermute | solution.py:525
  32.0 4.6 %collective-permute-done.5 = bf16[64,2432]{1,0:T(8,128)(2,1)S(1)} collective-permute-done((bf16[64,2432]{1,0:T(8,128)(2,1)S(1)}, bf16[64,2432]{1,0:T(8,128)(2,1)S(1)}, u32[]{:S(2)}, u32[]{:S(2)}) %collective-permute-start.5) | collective-permute-done | bytes 311328 | tf_op jit(solution)/shard_map/ppermute | solution.py:525
  49.9 12.9 %collective-permute-done.7 = bf16[128,2432]{1,0:T(8,128)(2,1)S(1)} collective-permute-done((bf16[128,2432]{1,0:T(8,128)(2,1)S(1)}, bf16[128,2432]{1,0:T(8,128)(2,1)S(1)}, u32[]{:S(2)}, u32[]{:S(2)}) %collective-permute-start.7) | collective-permute-done | bytes 622624 | tf_op jit(solution)/shard_map/ppermute | solution.py:525
  70.1 5.1 %place_rows.1 = bf16[1024,2432]{1,0:T(8,128)(2,1)} custom-call(s32[3]{0:T(128)} %pad_add_fusion.place_ref, bf16[256,2432]{1,0:T(8,128)(2,1)} %copy-done.1, bf16[256,2432]{1,0:T(8,128)(2,1)} %constant_dynamic-update-slice_fusion.refs_1_, bf16[256,2432]{1,0:T(8,128)(2,1)} %collective-permute-done.8.refs_2_, bf16[256,2432]{1,0:T(8,128)(2,1)} %collective-permute-done.9.refs_3_), custom_call_target="tpu_custom_call" | custom-call | bytes 9961472 | tf_op jit(solution)/shard_map/place_rows/pallas_call | solution.py:558
  78.2 10.9 %convolution_convert_fusion.x_ref.raw_ref.halo_ref = bf16[1040,2432]{1,0:T(8,128)(2,1)} fusion(bf16[1024,2432]{1,0:T(8,128)(2,1)} %place_rows.1, f32[1024]{0:T(1024)S(1)} %reshape.210, f32[1040]{0:T(1024)S(1)} %add_rsqrt_fusion, bf16[8,1024]{1,0:T(8,128)(2,1)S(1)} %collective-permute-done, bf16[1024,1024]{1,0:T(8,128)(2,1)S(1)} %bitcast.91, ...), kind=kOutput, calls=%fused_computation | convolution fusion | flops 5192079360 | bytes 12163168 | tf_op jit(solution)/shard_map/dot_general | solution.py:793
  89.1 17.8 %conv_states.1 = (bf16[1024,2304]{1,0:T(8,128)(2,1)}, bf16[1024,2048]{1,0:T(8,128)(2,1)}, f32[1024,128]{1,0:T(8,128)}, f32[1024,128]{1,0:T(8,128)}, f32[1024,32]...) custom-call(bf16[1040,2432]{1,0:T(8,128)(2,1)} %convolution_convert_fusion.x_ref.raw_ref.halo_ref, ...), custom_call_target="tpu_custom_call" | custom-call | flops 1000000000 | bytes 30000000 | tf_op jit(solution)/shard_map/conv_states/pallas_call | solution.py:798
  114.0 11.5 %intra.1.y_ref = f32[1024,2048]{1,0:T(8,128)} custom-call(f32[1024,128]{1,0:T(8,128)} %get-tuple-element.85.q_ref, f32[1024,128]{1,0:T(8,128)} %get-tuple-element.86.k_ref, bf16[1024,2048]{1,0:T(8,128)(2,1)} %get-tuple-element.87.v_ref, f32[1024,32]{1,0:T(8,128)} %get-tuple-element.88.rc_ref, f32[256,128]{1,0:T(8,128)} %get-tuple-element.89.rs_ref, ...), custom_call_target="tpu_custom_call" | custom-call | flops 1000000000 | bytes 30000000 | tf_op jit(solution)/shard_map/intra/pallas_call | solution.py:825
  128.9 7.1 %unpack_weights.1 = (bf16[1024,2048]{1,0:T(8,128)(2,1)}, bf16[2048,1024]{1,0:T(8,128)(2,1)}) custom-call(bf16[1024,4096]{1,0:T(8,128)(2,1)} %all-gather.2.cloned.1.call-done.src), custom_call_target="tpu_custom_call" | custom-call | bytes 16777216 | tf_op jit(solution)/shard_map/unpack_weights/pallas_call | solution.py:619
  136.0 8.6 %convolution_convert_fusion.4.gate_ref = bf16[1024,2048]{1,0:T(8,128)(2,1)} fusion(bf16[1024,2048]{1,0:T(8,128)(2,1)} %get-tuple-element.93, f32[1024]{0:T(1024)S(1)} %reshape.210, f32[1024]{0:T(1024)S(1)} %add_rsqrt_fusion.1, bf16[1,1024,1024]{2,1,0:T(8,128)(2,1)S(1)} %copy-done), kind=kOutput, calls=%fused_computation.25 | convolution fusion | flops 4301258752 | bytes 10493952 | tf_op jit(solution)/shard_map/dot_general | solution.py:840
  144.6 6.8 %convolution_bitcast_fusion.dn_ref = f32[1024,2048]{1,0:T(8,128)} fusion(bf16[2048,1024]{1,0:T(8,128)(2,1)S(1)} %copy-done.28, bf16[1,1024,1024]{2,1,0:T(8,128)(2,1)S(1)} %copy-done.5), kind=kOutput, calls=%fused_computation.11 | convolution fusion | flops 4294967296 | bytes 14680064 | tf_op jit(solution)/shard_map/dot_general | solution.py:841
  156.7 28.4 %gate_norm.1 = (bf16[1024,2048]{1,0:T(8,128)(2,1)}, bf16[1024,2048]{1,0:T(8,128)(2,1)}, bf16[1024,2048]{1,0:T(8,128)(2,1)}, bf16[1024,2048]{1,0:T(8,128)(2,1)}, ...) custom-call(f32[1024,2048]{1,0:T(8,128)} %intra.1.y_ref, ...), custom_call_target="tpu_custom_call" | custom-call | flops 1000000000 | bytes 50000000 | tf_op jit(solution)/shard_map/gate_norm/pallas_call | solution.py:845
  186.4 8.8 %convolution_convert_fusion.3.refs_0_ = bf16[1024,2048]{1,0:T(8,128)(2,1)} fusion(bf16[1024,2048]{1,0:T(8,128)(2,1)} %get-tuple-element.99, f32[1024]{0:T(1024)S(1)} %reshape.210, f32[1024]{0:T(1024)S(1)} %add_rsqrt_fusion.1, bf16[1,1024,1024]{2,1,0:T(8,128)(2,1)S(1)} %copy-done), kind=kOutput, calls=%fused_computation.24 | convolution fusion | flops 4301258752 | bytes 10493952 | tf_op jit(solution)/shard_map/dot_general | solution.py:876
  195.9 6.8 %convolution_convert_fusion.2.refs_1_ = bf16[2048,1024]{1,0:T(8,128)(2,1)} fusion(bf16[1024,2048]{1,0:T(8,128)(2,1)S(1)} %copy-done.30, bf16[1,1024,1024]{2,1,0:T(8,128)(2,1)S(1)} %copy-done.6), kind=kOutput, calls=%fused_computation.23 | convolution fusion | flops 4297064448 | bytes 10485760 | tf_op jit(solution)/shard_map/dot_general | solution.py:878
  204.4 7.3 %pick_rows.2 = (bf16[128,4096]{1,0:T(8,128)(2,1)}, bf16[128,4096]{1,0:T(8,128)(2,1)}, bf16[128,4096]{1,0:T(8,128)(2,1)}, bf16[128,4096]{1,0:T(8,128)(2,1)}, bf16[512,4096]{1,0:T(8,128)(2,1)}) custom-call(s32[3]{0:T(128)} %pad_add_fusion.place_ref, bf16[1024,2048]{1,0:T(8,128)(2,1)} %convolution_convert_fusion.3.refs_0_, ...), custom_call_target="tpu_custom_call" | custom-call | bytes 16777216 | tf_op jit(solution)/shard_map/pick_rows/pallas_call | solution.py:592
  212.8 9.6 %fusion.14 = bf16[1024,1024]{1,0:T(8,128)(2,1)} fusion(bf16[1024,2048]{1,0:T(8,128)(2,1)} %get-tuple-element.107, bf16[2048,1024]{1,0:T(8,128)(2,1)} %get-tuple-element.94, bf16[1,1024,1024]{2,1,0:T(8,128)(2,1)S(1)} %copy-done), kind=kOutput, calls=%fused_computation.22 | convolution fusion | flops 4298113024 | bytes 12582912 | tf_op jit(solution)/shard_map/dot_general | solution.py:883
  222.4 5.4 %add_convert_fusion = (bf16[128,4096]{1,0:T(8,128)(2,1)}, bf16[128,4096]{1,0:T(8,128)(2,1)}, bf16[128,4096]{1,0:T(8,128)(2,1)}, bf16[128,4096]{1,0:T(8,128)(2,1)}) fusion(bf16[128,4096]{1,0:T(8,128)(2,1)S(1)} %copy-done.14, bf16[512,4096]{1,0:T(8,128)(2,1)} %collective-permute-done.17, bf16[128,4096]{1,0:T(8,128)(2,1)S(1)} %copy-done.12, ...), kind=kLoop, calls=%fused_computation.31 | loop fusion | flops 8388608 | bytes 12582912 | tf_op jit(solution)/shard_map/convert_element_type | solution.py:664
  229.6 6.1 %fusion.49 = f32[1024,1024]{1,0:T(8,128)} fusion(bf16[1024,2048]{1,0:T(8,128)(2,1)S(1)} %copy-done.29, bf16[1024,2048]{1,0:T(8,128)(2,1)S(1)} %copy-done.27), kind=kOutput, calls=%fused_computation.171 | convolution fusion | flops 4294967296 | bytes 12582912 | tf_op jit(solution)/shard_map/dot_general | solution.py:946
  236.4 26.4 %intra_back.1 = (bf16[1024,2048]{1,0:T(8,128)(2,1)}, f32[1024,32]{1,0:T(8,128)}, f32[1024,128]{1,0:T(8,128)}, f32[1024,128]{1,0:T(8,128)}) custom-call(f32[1024,128]{1,0:T(8,128)} %get-tuple-element.85.q_ref, f32[1024,128]{1,0:T(8,128)} %get-tuple-element.86.k_ref, bf16[1024,2048]{1,0:T(8,128)(2,1)} %get-tuple-element.87.v_ref, ...), custom_call_target="tpu_custom_call" | custom-call | flops 2000000000 | bytes 40000000 | tf_op jit(solution)/shard_map/intra_back/pallas_call | solution.py:888
  264.0 35.2 %states_conv_back.1 = (bf16[1024,2432]{1,0:T(8,128)(2,1)}, f32[8,2304]{1,0:T(8,128)}, f32[40,2304]{1,0:T(8,128)}, f32[16,32]{1,0:T(8,128)}) custom-call(bf16[1040,2432]{1,0:T(8,128)(2,1)} %convolution_convert_fusion.x_ref.raw_ref.halo_ref, bf16[1040,2432]{1,0:T(8,128)(2,1)} %convolution_convert_fusion.x_ref.raw_ref.halo_ref, ...), custom_call_target="tpu_custom_call" | custom-call | flops 2000000000 | bytes 60000000 | tf_op jit(solution)/shard_map/states_conv_back/pallas_call | solution.py:909
  303.3 3.6 collective-permute-start.24
  311.5 10.2 %convolution_convert_fusion.1.refs_0_ = bf16[1024,2432]{1,0:T(8,128)(2,1)} fusion(bf16[1024,2432]{1,0:T(8,128)(2,1)} %fusion.29, f32[1024]{0:T(1024)S(1)} %reshape.210, f32[1024]{0:T(1024)S(1)} %add_rsqrt_fusion.1, bf16[1,1024,1024]{2,1,0:T(8,128)(2,1)S(1)} %copy-done), kind=kOutput, calls=%fused_computation.8 | convolution fusion | flops 5106958336 | bytes 12066816 | tf_op jit(solution)/shard_map/dot_general | solution.py:943
  321.8 5.0 %pick_rows.3 = (bf16[128,2432]{1,0:T(8,128)(2,1)}, bf16[128,2432]{1,0:T(8,128)(2,1)}, bf16[128,2432]{1,0:T(8,128)(2,1)}, bf16[128,2432]{1,0:T(8,128)(2,1)}, bf16[512,2432]{1,0:T(8,128)(2,1)}) custom-call(s32[3]{0:T(128)} %pad_add_fusion.place_ref, bf16[1024,2432]{1,0:T(8,128)(2,1)} %convolution_convert_fusion.1.refs_0_), custom_call_target="tpu_custom_call" | custom-call | bytes 9961472 | tf_op jit(solution)/shard_map/pick_rows/pallas_call | solution.py:592
  326.8 8.3 %convolution_add_fusion = f32[1024,1024]{1,0:T(8,128)S(1)} fusion(f32[1024,1024]{1,0:T(8,128)} %fusion.49, bf16[1024,2432]{1,0:T(8,128)(2,1)} %fusion.29, bf16[1024,2432]{1,0:T(8,128)(2,1)S(1)} %bitcast.93), kind=kOutput, calls=%fused_computation.35 | convolution fusion | flops 5101322240 | bytes 18350080 | tf_op jit(solution)/shard_map/dot_general | solution.py:947
  342.5 9.0 %collective-permute-done.27 = bf16[32,4096]{1,0:T(8,128)(2,1)S(1)} collective-permute-done((bf16[32,4096]{1,0:T(8,128)(2,1)S(1)}, bf16[32,4096]{1,0:T(8,128)(2,1)S(1)}, u32[]{:S(2)}, u32[]{:S(2)}) %collective-permute-start.27) | collective-permute-done | bytes 262176 | tf_op jit(solution)/shard_map/ppermute | solution.py:525
  351.5 8.7 %collective-permute-done.28 = bf16[32,4096]{1,0:T(8,128)(2,1)S(1)} collective-permute-done((bf16[32,4096]{1,0:T(8,128)(2,1)S(1)}, bf16[32,4096]{1,0:T(8,128)(2,1)S(1)}, u32[]{:S(2)}, u32[]{:S(2)}) %collective-permute-start.28) | collective-permute-done | bytes 262176 | tf_op jit(solution)/shard_map/ppermute | solution.py:525
  367.6 10.3 %collective-permute-done.26 = bf16[128,2432]{1,0:T(8,128)(2,1)S(1)} collective-permute-done((bf16[128,2432]{1,0:T(8,128)(2,1)S(1)}, bf16[128,2432]{1,0:T(8,128)(2,1)S(1)}, u32[]{:S(2)}, u32[]{:S(2)}) %collective-permute-start.26) | collective-permute-done | bytes 622624 | tf_op jit(solution)/shard_map/ppermute | solution.py:525
  380.3 6.4 %collective-permute-start.35 = (f32[32,552]{1,0:T(8,128)S(1)}, f32[32,552]{1,0:T(8,128)S(1)}, u32[]{:S(2)}, u32[]{:S(2)}) collective-permute-start(f32[32,552]{1,0:T(8,128)S(1)} %maximum_maximum_fusion.2), channel_id=1, source_target_pairs={{0,1},{1,0},{2,3},{3,2},{4,5},{5,4},{6,7},{7,6},{8,9},{9,8},{10,11... | collective-permute-start | bytes 211976 | tf_op jit(solution)/shard_map/ppermute | solution.py:525
  389.2 3.1 collective-permute-start.36
  402.7 3.4 collective-permute-done.32
  407.8 3.0 collective-permute-start.33
  414.7 7.5 %collective-permute-done.33 = bf16[32,2432]{1,0:T(8,128)(2,1)S(1)} collective-permute-done((bf16[32,2432]{1,0:T(8,128)(2,1)S(1)}, bf16[32,2432]{1,0:T(8,128)(2,1)S(1)}, u32[]{:S(2)}, u32[]{:S(2)}) %collective-permute-start.33) | collective-permute-done | bytes 155680 | tf_op jit(solution)/shard_map/ppermute | solution.py:525
  (267 shorter events, 104.3 us)
Async XLA Ops:
  7.2 121.7 %all-gather.2.cloned.1.call-start = ((), (), s32[]{:S(2)}) async-start(), calls=%async_computation | async-start | bytes 8650752 | tf_op jit(solution)/shard_map/all_gather | solution.py:752
  9.9 10.0 %collective-permute-start.4 = (bf16[32,2432]{1,0:T(8,128)(2,1)S(1)}, bf16[32,2432]{1,0:T(8,128)(2,1)S(1)}, u32[]{:S(2)}, u32[]{:S(2)}) collective-permute-start(bf16[32,2432]{1,0:T(8,128)(2,1)S(1)} %pad_maximum_fusion.12), channel_id=1, source_target_pairs={{0,3},{1,2},{2,1},{3,0},{4,7},{5,6},{6,5},{7,4},{8,11},{9,10},{10,... | collective-permute-start | bytes 466952 | tf_op jit(solution)/shard_map/ppermute | solution.py:525
  14.9 13.2 %collective-permute-start.3 = (bf16[32,2432]{1,0:T(8,128)(2,1)S(1)}, bf16[32,2432]{1,0:T(8,128)(2,1)S(1)}, u32[]{:S(2)}, u32[]{:S(2)}) collective-permute-start(bf16[32,2432]{1,0:T(8,128)(2,1)S(1)} %pad_maximum_fusion.12), channel_id=1, source_target_pairs={{0,2},{1,3},{2,0},{3,1},{4,6},{5,7},{6,4},{7,5},{8,10},{9,11},{10,... | collective-permute-start | bytes 466952 | tf_op jit(solution)/shard_map/ppermute | solution.py:525
  14.9 14.8 %collective-permute-start.1 = (bf16[32,2432]{1,0:T(8,128)(2,1)S(1)}, bf16[32,2432]{1,0:T(8,128)(2,1)S(1)}, u32[]{:S(2)}, u32[]{:S(2)}) collective-permute-start(bf16[32,2432]{1,0:T(8,128)(2,1)S(1)} %pad_maximum_fusion.12), channel_id=1, source_target_pairs={{0,1},{1,0},{2,3},{3,2},{4,5},{5,4},{6,7},{7,6},{8,9},{9,8},{10,11... | collective-permute-start | bytes 466952 | tf_op jit(solution)/shard_map/ppermute | solution.py:525
  38.9 30.5 %collective-permute-start = (bf16[8,1024]{1,0:T(8,128)(2,1)S(1)}, bf16[8,1024]{1,0:T(8,128)(2,1)S(1)}, u32[]{:S(2)}, u32[]{:S(2)}) collective-permute-start(bf16[8,1024]{1,0:T(8,128)(2,1)S(1)} %slice_bitcast_fusion), channel_id=1, source_target_pairs={{0,4},{4,8},{8,12},{12,16},{16,20},{20,24},{24,28},{1,5},{5,9},{9,... | collective-permute-start | bytes 49160 | tf_op jit(solution)/shard_map/ppermute | solution.py:520
  46.3 16.4 %collective-permute-start.7 = (bf16[128,2432]{1,0:T(8,128)(2,1)S(1)}, bf16[128,2432]{1,0:T(8,128)(2,1)S(1)}, u32[]{:S(2)}, u32[]{:S(2)}) collective-permute-start(bf16[128,2432]{1,0:T(8,128)(2,1)S(1)} %pad_maximum_fusion.2), channel_id=1, source_target_pairs={{0,8},{8,0},{16,24},{24,16},{1,9},{9,1},{17,25},{25,17},{2,10},{10... | collective-permute-start | bytes 1867784 | tf_op jit(solution)/shard_map/ppermute | solution.py:525
  48.6 16.3 %collective-permute-start.6 = (bf16[128,2432]{1,0:T(8,128)(2,1)S(1)}, bf16[128,2432]{1,0:T(8,128)(2,1)S(1)}, u32[]{:S(2)}, u32[]{:S(2)}) collective-permute-start(bf16[128,2432]{1,0:T(8,128)(2,1)S(1)} %pad_maximum_fusion.1), channel_id=1, source_target_pairs={{0,16},{8,24},{16,0},{24,8},{1,17},{9,25},{17,1},{25,9},{2,18},{10... | collective-permute-start | bytes 1867784 | tf_op jit(solution)/shard_map/ppermute | solution.py:525
  111.9 14.8 %collective-permute-start.11 = (f32[130,1024]{1,0:T(8,128)S(1)}, f32[130,1024]{1,0:T(8,128)S(1)}, u32[]{:S(2)}, u32[]{:S(2)}) collective-permute-start(f32[130,1024]{1,0:T(8,128)S(1)} %pad_maximum_fusion.4), channel_id=1, source_target_pairs={{0,8},{8,0},{16,24},{24,16},{1,9},{9,1},{17,25},{25,17},{2,10},{10... | collective-permute-start | bytes 1597448 | tf_op jit(solution)/shard_map/ppermute | solution.py:525
  127.5 23.9 %collective-permute-start.12 = (f32[130,1024]{1,0:T(8,128)S(1)}, f32[130,1024]{1,0:T(8,128)}, u32[]{:S(2)}, u32[]{:S(2)}) collective-permute-start(f32[130,1024]{1,0:T(8,128)S(1)} %pad_maximum_fusion.5), channel_id=1, source_target_pairs={{0,16},{8,24},{16,0},{24,8},{1,17},{9,25},{17,1},{25,9},{2,18},{10... | collective-permute-start | bytes 1597448 | tf_op jit(solution)/shard_map/ppermute | solution.py:525
  186.2 9.0 %collective-permute-start.14 = (bf16[130,1024]{1,0:T(8,128)(2,1)S(1)}, bf16[130,1024]{1,0:T(8,128)(2,1)S(1)}, u32[]{:S(2)}, u32[]{:S(2)}) collective-permute-start(bf16[130,1024]{1,0:T(8,128)(2,1)S(1)} %broadcast_select_fusion.1), channel_id=1, source_target_pairs={{0,4},{4,0},{1,5},{5,1},{2,6},{6,2},{3,7},{7,3},{8,12},{12,8},{9,1... | collective-permute-start | bytes 798728 | tf_op jit(solution)/shard_map/ppermute | solution.py:525
  195.4 9.0 %collective-permute-start.15 = (bf16[130,1024]{1,0:T(8,128)(2,1)S(1)}, bf16[130,1024]{1,0:T(8,128)(2,1)S(1)}, u32[]{:S(2)}, u32[]{:S(2)}) collective-permute-start(bf16[130,1024]{1,0:T(8,128)(2,1)S(1)} %pad_maximum_fusion.8), channel_id=1, source_target_pairs={{0,8},{8,0},{16,24},{24,16},{1,9},{9,1},{17,25},{25,17},{2,10},{10... | collective-permute-start | bytes 798728 | tf_op jit(solution)/shard_map/ppermute | solution.py:525
  211.7 10.6 %collective-permute-start.17 = (bf16[512,4096]{1,0:T(8,128)(2,1)}, bf16[512,4096]{1,0:T(8,128)(2,1)}, u32[]{:S(2)}, u32[]{:S(2)}) collective-permute-start(bf16[512,4096]{1,0:T(8,128)(2,1)} %get-tuple-element.106), channel_id=1, source_target_pairs={{0,4},{4,0},{1,5},{5,1},{2,6},{6,2},{3,7},{7,3},{8,12},{12,8},{9,1... | collective-permute-start | bytes 12582920 | tf_op jit(solution)/shard_map/ppermute | solution.py:525
  212.1 23.7 %collective-permute-start.16 = (bf16[130,1024]{1,0:T(8,128)(2,1)S(1)}, bf16[130,1024]{1,0:T(8,128)(2,1)S(1)}, u32[]{:S(2)}, u32[]{:S(2)}) collective-permute-start(bf16[130,1024]{1,0:T(8,128)(2,1)S(1)} %pad_maximum_fusion.9), channel_id=1, source_target_pairs={{0,16},{8,24},{16,0},{24,8},{1,17},{9,25},{17,1},{25,9},{2,18},{10... | collective-permute-start | bytes 798728 | tf_op jit(solution)/shard_map/ppermute | solution.py:525
  227.8 34.9 %collective-permute-start.20 = (bf16[128,4096]{1,0:T(8,128)(2,1)}, bf16[128,4096]{1,0:T(8,128)(2,1)}, u32[]{:S(2)}, u32[]{:S(2)}) collective-permute-start(bf16[128,4096]{1,0:T(8,128)(2,1)} %get-tuple-element.171), channel_id=1, source_target_pairs={{0,8},{8,0},{16,24},{24,16},{1,9},{9,1},{17,25},{25,17},{2,10},{10... | collective-permute-start | bytes 3145736 | tf_op jit(solution)/shard_map/ppermute | solution.py:525
  228.8 33.9 %collective-permute-start.19 = (bf16[128,4096]{1,0:T(8,128)(2,1)}, bf16[128,4096]{1,0:T(8,128)(2,1)}, u32[]{:S(2)}, u32[]{:S(2)}) collective-permute-start(bf16[128,4096]{1,0:T(8,128)(2,1)} %get-tuple-element.172), channel_id=1, source_target_pairs={{0,16},{8,24},{16,0},{24,8},{1,17},{9,25},{17,1},{25,9},{2,18},{10... | collective-permute-start | bytes 3145736 | tf_op jit(solution)/shard_map/ppermute | solution.py:525
  236.0 26.8 %collective-permute-start.18 = (bf16[128,1024]{1,0:T(8,128)(2,1)S(1)}, bf16[128,1024]{1,0:T(8,128)(2,1)S(1)}, u32[]{:S(2)}, u32[]{:S(2)}) collective-permute-start(bf16[128,1024]{1,0:T(8,128)(2,1)S(1)} %get-tuple-element.182), channel_id=1, source_target_pairs={{0,4},{4,0},{1,5},{5,1},{2,6},{6,2},{3,7},{7,3},{8,12},{12,8},{9,1... | collective-permute-start | bytes 786440 | tf_op jit(solution)/shard_map/ppermute | solution.py:525
  300.6 9.5 %collective-permute-start.21 = (f32[8,2304]{1,0:T(8,128)}, f32[8,2304]{1,0:T(8,128)S(1)}, u32[]{:S(2)}, u32[]{:S(2)}) collective-permute-start(f32[8,2304]{1,0:T(8,128)} %get-tuple-element.129), channel_id=1, source_target_pairs={{4,0},{8,4},{12,8},{16,12},{20,16},{24,20},{28,24},{5,1},{9,5},{13... | collective-permute-start | bytes 221192 | tf_op jit(solution)/shard_map/ppermute | solution.py:520
  303.3 31.9 %collective-permute-start.24 = (bf16[64,4096]{1,0:T(8,128)(2,1)S(1)}, bf16[64,4096]{1,0:T(8,128)(2,1)}, u32[]{:S(2)}, u32[]{:S(2)}) collective-permute-start(bf16[64,4096]{1,0:T(8,128)(2,1)S(1)} %add_convert_fusion.11), channel_id=1, source_target_pairs={{0,16},{8,24},{16,0},{24,8},{1,17},{9,25},{17,1},{25,9},{2,18},{10... | collective-permute-start | bytes 1572872 | tf_op jit(solution)/shard_map/ppermute | solution.py:525
  308.9 26.2 %collective-permute-start.23 = (bf16[64,4096]{1,0:T(8,128)(2,1)}, bf16[64,4096]{1,0:T(8,128)(2,1)S(1)}, u32[]{:S(2)}, u32[]{:S(2)}) collective-permute-start(bf16[64,4096]{1,0:T(8,128)(2,1)} %add_convert_fusion.12), channel_id=1, source_target_pairs={{0,8},{8,0},{16,24},{24,16},{1,9},{9,1},{17,25},{25,17},{2,10},{10... | collective-permute-start | bytes 1572872 | tf_op jit(solution)/shard_map/ppermute | solution.py:525
  326.8 34.4 %collective-permute-start.22 = (bf16[512,2432]{1,0:T(8,128)(2,1)}, bf16[512,2432]{1,0:T(8,128)(2,1)S(1)}, u32[]{:S(2)}, u32[]{:S(2)}) collective-permute-start(bf16[512,2432]{1,0:T(8,128)(2,1)} %get-tuple-element.132), channel_id=1, source_target_pairs={{0,4},{4,0},{1,5},{5,1},{2,6},{6,2},{3,7},{7,3},{8,12},{12,8},{9,1... | collective-permute-start | bytes 7471112 | tf_op jit(solution)/shard_map/ppermute | solution.py:525
  337.8 13.7 %collective-permute-start.27 = (bf16[32,4096]{1,0:T(8,128)(2,1)S(1)}, bf16[32,4096]{1,0:T(8,128)(2,1)S(1)}, u32[]{:S(2)}, u32[]{:S(2)}) collective-permute-start(bf16[32,4096]{1,0:T(8,128)(2,1)S(1)} %slice.615), channel_id=1, source_target_pairs={{0,1},{1,0},{2,3},{3,2},{4,5},{5,4},{6,7},{7,6},{8,9},{9,8},{10,11... | collective-permute-start | bytes 786440 | tf_op jit(solution)/shard_map/ppermute | solution.py:525
  338.9 21.4 %collective-permute-start.28 = (bf16[32,4096]{1,0:T(8,128)(2,1)S(1)}, bf16[32,4096]{1,0:T(8,128)(2,1)S(1)}, u32[]{:S(2)}, u32[]{:S(2)}) collective-permute-start(bf16[32,4096]{1,0:T(8,128)(2,1)S(1)} %get-tuple-element.187), channel_id=1, source_target_pairs={{0,2},{1,3},{2,0},{3,1},{4,6},{5,7},{6,4},{7,5},{8,10},{9,11},{10,... | collective-permute-start | bytes 786440 | tf_op jit(solution)/shard_map/ppermute | solution.py:525
  341.7 18.5 %collective-permute-start.29 = (bf16[32,4096]{1,0:T(8,128)(2,1)S(1)}, bf16[32,4096]{1,0:T(8,128)(2,1)S(1)}, u32[]{:S(2)}, u32[]{:S(2)}) collective-permute-start(bf16[32,4096]{1,0:T(8,128)(2,1)S(1)} %get-tuple-element.188), channel_id=1, source_target_pairs={{0,3},{1,2},{2,1},{3,0},{4,7},{5,6},{6,5},{7,4},{8,11},{9,10},{10,... | collective-permute-start | bytes 786440 | tf_op jit(solution)/shard_map/ppermute | solution.py:525
  363.1 14.7 %collective-permute-start.26 = (bf16[128,2432]{1,0:T(8,128)(2,1)S(1)}, bf16[128,2432]{1,0:T(8,128)(2,1)S(1)}, u32[]{:S(2)}, u32[]{:S(2)}) collective-permute-start(bf16[128,2432]{1,0:T(8,128)(2,1)S(1)} %get-tuple-element.175), channel_id=1, source_target_pairs={{0,8},{8,0},{16,24},{24,16},{1,9},{9,1},{17,25},{25,17},{2,10},{10... | collective-permute-start | bytes 1867784 | tf_op jit(solution)/shard_map/ppermute | solution.py:525
  364.8 14.5 %collective-permute-start.25 = (bf16[128,2432]{1,0:T(8,128)(2,1)S(1)}, bf16[128,2432]{1,0:T(8,128)(2,1)S(1)}, u32[]{:S(2)}, u32[]{:S(2)}) collective-permute-start(bf16[128,2432]{1,0:T(8,128)(2,1)S(1)} %get-tuple-element.176), channel_id=1, source_target_pairs={{0,16},{8,24},{16,0},{24,8},{1,17},{9,25},{17,1},{25,9},{2,18},{10... | collective-permute-start | bytes 1867784 | tf_op jit(solution)/shard_map/ppermute | solution.py:525
  380.3 8.8 %collective-permute-start.35 = (f32[32,552]{1,0:T(8,128)S(1)}, f32[32,552]{1,0:T(8,128)S(1)}, u32[]{:S(2)}, u32[]{:S(2)}) collective-permute-start(f32[32,552]{1,0:T(8,128)S(1)} %maximum_maximum_fusion.2), channel_id=1, source_target_pairs={{0,1},{1,0},{2,3},{3,2},{4,5},{5,4},{6,7},{7,6},{8,9},{9,8},{10,11... | collective-permute-start | bytes 211976 | tf_op jit(solution)/shard_map/ppermute | solution.py:525
  395.8 10.2 %collective-permute-start.32 = (bf16[64,2432]{1,0:T(8,128)(2,1)S(1)}, bf16[64,2432]{1,0:T(8,128)(2,1)S(1)}, u32[]{:S(2)}, u32[]{:S(2)}) collective-permute-start(bf16[64,2432]{1,0:T(8,128)(2,1)S(1)} %add_convert_fusion.14), channel_id=1, source_target_pairs={{0,16},{8,24},{16,0},{24,8},{1,17},{9,25},{17,1},{25,9},{2,18},{10... | collective-permute-start | bytes 933896 | tf_op jit(solution)/shard_map/ppermute | solution.py:525
  398.2 9.4 %collective-permute-start.30 = (bf16[64,2432]{1,0:T(8,128)(2,1)S(1)}, bf16[64,2432]{1,0:T(8,128)(2,1)S(1)}, u32[]{:S(2)}, u32[]{:S(2)}) collective-permute-start(bf16[64,2432]{1,0:T(8,128)(2,1)S(1)} %add_convert_fusion.16), channel_id=1, source_target_pairs={{0,8},{8,0},{16,24},{24,16},{1,9},{9,1},{17,25},{25,17},{2,10},{10... | collective-permute-start | bytes 933896 | tf_op jit(solution)/shard_map/ppermute | solution.py:525
  400.9 11.4 %collective-permute-start.39 = (f32[32,552]{1,0:T(8,128)S(1)}, f32[32,552]{1,0:T(8,128)S(1)}, u32[]{:S(2)}, u32[]{:S(2)}) collective-permute-start(f32[32,552]{1,0:T(8,128)S(1)} %add.248), channel_id=1, source_target_pairs={{0,16},{8,24},{16,0},{24,8},{1,17},{9,25},{17,1},{25,9},{2,18},{10... | collective-permute-start | bytes 211976 | tf_op jit(solution)/shard_map/ppermute | solution.py:525
  407.8 14.4 %collective-permute-start.33 = (bf16[32,2432]{1,0:T(8,128)(2,1)S(1)}, bf16[32,2432]{1,0:T(8,128)(2,1)S(1)}, u32[]{:S(2)}, u32[]{:S(2)}) collective-permute-start(bf16[32,2432]{1,0:T(8,128)(2,1)S(1)} %get-tuple-element.189), channel_id=1, source_target_pairs={{0,2},{1,3},{2,0},{3,1},{4,6},{5,7},{6,4},{7,5},{8,10},{9,11},{10,... | collective-permute-start | bytes 466952 | tf_op jit(solution)/shard_map/ppermute | solution.py:525
  410.8 11.4 %collective-permute-start.34 = (bf16[32,2432]{1,0:T(8,128)(2,1)S(1)}, bf16[32,2432]{1,0:T(8,128)(2,1)S(1)}, u32[]{:S(2)}, u32[]{:S(2)}) collective-permute-start(bf16[32,2432]{1,0:T(8,128)(2,1)S(1)} %get-tuple-element.190), channel_id=1, source_target_pairs={{0,3},{1,2},{2,1},{3,0},{4,7},{5,6},{6,5},{7,4},{8,11},{9,10},{10,... | collective-permute-start | bytes 466952 | tf_op jit(solution)/shard_map/ppermute | solution.py:525
  412.3 10.0 %collective-permute-start.31 = (bf16[32,2432]{1,0:T(8,128)(2,1)S(1)}, bf16[32,2432]{1,0:T(8,128)(2,1)S(1)}, u32[]{:S(2)}, u32[]{:S(2)}) collective-permute-start(bf16[32,2432]{1,0:T(8,128)(2,1)S(1)} %slice.616), channel_id=1, source_target_pairs={{0,1},{1,0},{2,3},{3,2},{4,5},{5,4},{6,7},{7,6},{8,9},{9,8},{10,11... | collective-permute-start | bytes 466952 | tf_op jit(solution)/shard_map/ppermute | solution.py:525
  (43 other events, 544.7 us)
Sparse Core Ops, SparseCore 0:
  38.1 77.9 all-gather.1

commit v6 on v5

--- a/solution.py
+++ b/solution.py
@@ -717,7 +717,8 @@
 
 def sum_small(block, pairs, fsdp):
     for axis, mask in links(pairs, fsdp):
-        block = block + swap(block, axis, mask)
+        (other,) = yield [swap(block, axis, mask)]
+        block = block + other
     return block
 
 
@@ -936,6 +937,7 @@
         mix, conv_full, rate, sbias, skip_wide, expand,
     )
 
+    grad_mix, dhalo = gate_steps.beside(grad_mix, dhalo)
     edge = shift(dhalo, 2 * pairs, -1)
     edge = jnp.pad(edge, ((0, 0), (0, MIX_WIDE - CHANNELS)))
     fixed = (grad_mix[count - 8 :].astype(F32) + edge).astype(BF)
@@ -945,7 +947,6 @@
     (grad_mix,) = mix_steps.beside(grad_mix)
     grad_hidden = lax.dot_general(dgate, w_gate, NT, preferred_element_type=F32)
     grad_hidden = grad_hidden + lax.dot_general(grad_mix, w_mix, NT, preferred_element_type=F32)
-    (grad_hidden,) = gate_steps.beside(grad_hidden)
     (grad_hidden,) = mix_steps.beside(grad_hidden)
 
     x = tokens.astype(F32)
@@ -955,7 +956,6 @@
     mean = jnp.mean(scaled * unit, axis=-1, keepdims=True)
     grad_tokens = upstream.astype(F32) + inv * (scaled - unit * mean)
     grad_norm = jnp.sum(grad_hidden * unit, axis=0)
-    grad_tokens, grad_norm = mix_steps.beside(grad_tokens, grad_norm)
 
     conv_sums = conv_sums.reshape(taps + 1, 8, CHANNELS).sum(axis=1)
     gate_sums = gate_sums.reshape(2, 8, DI).sum(axis=1)
@@ -974,9 +974,16 @@
         ],
         axis=1,
     )
-    mine = lax.dynamic_slice(
-        sum_small(parts, pairs, fsdp), (device, 0), (1, parts.shape[1])
-    )[0]
+    small_steps = Steps(sum_small(parts, pairs, fsdp))
+    small_steps.beside()
+    if mix_steps.flight is not None:
+        grad_tokens, small_steps.flight, gate_steps.flight = mix_steps.beside(
+            grad_tokens, small_steps.flight, gate_steps.flight
+        )
+    small_steps.beside()
+    if mix_steps.flight is not None:
+        (small_steps.flight,) = mix_steps.beside(small_steps.flight)
+    mine = lax.dynamic_slice(small_steps.finish(), (device, 0), (1, parts.shape[1]))[0]
     ends = np.cumsum([own[0], own[1], own[2], own[3], HEADS, HEADS, HEADS]).tolist()
     conv_shard, bias_shard, norm_shard, gain_shard, *heads = [
         mine[a:b] for a, b in zip([0] + ends[:-1], ends)

time: 435 us -> 417 us (0.959)
  waiting for transfers between devices: 81.5 us -> 63.4 us
  starting transfers between devices: 50.4 us -> 44.7 us
    ppermute x38, waiting for transfers between devices: 81.4 us -> 62.7 us  [swap(): return lax.ppermute(block, axis, [(i, i ^ mask) for i in range(count)])]
    ppermute x38, starting transfers between devices: 47.8 us -> 42.1 us  [swap(): return lax.ppermute(block, axis, [(i, i ^ mask) for i in range(count)])]
  transfers between devices with their start and end apart: 41 -> 41, of which waited for: 20 -> 19; matrix products, arithmetic and copies ran while one was open for 29% -> 29% of each run, Pallas kernels for 17% -> 25%
where the time goes in v6:
time: 417 us; the launch traced here: 412 us
  Pallas kernels  144 us (35%)
  matrix products  77.3 us (19%)
  waiting for transfers between devices  63.4 us (15%)
  starting transfers between devices  44.7 us (11%)
  other arithmetic  43.8 us (11%)
  local copies, waits for them, and re-layouts  24.4 us (6%)
  between operations  15 us (4%)
    ppermute x38, waiting for transfers between devices, swap(): return lax.ppermute(block, axis, [(i, i ^ mask) for i in range(count)])  62.7 us
    ppermute x38, starting transfers between devices, swap(): return lax.ppermute(block, axis, [(i, i ^ mask) for i in range(count)])  42.1 us
    pallas_call x1, Pallas kernels, on_device(): pl.pallas_call(back_kernel, name='states_conv_back', grid=(chunks,), in_s...  35.2 us
    pallas_call x1, Pallas kernels, on_device(): pl.pallas_call(gate_kernel, name='gate_norm', grid=(chunks,), in_specs=[r...  28.4 us
    pallas_call x1, Pallas kernels, on_device(): pl.pallas_call(intra_back_kernel, name='intra_back', grid=(chunks,), in_s...  26.5 us
    pallas_call x1, Pallas kernels, on_device(): pl.pallas_call(prep_kernel, name='conv_states', grid=(chunks,), in_specs=...  17.8 us
    pallas_call x2, Pallas kernels, pick_rows(): pl.pallas_call(body, name='pick_rows', in_specs=[pl.BlockSpec(memory_spac...  12.3 us
    pallas_call x1, Pallas kernels, on_device(): pl.pallas_call(intra_kernel, name='intra', grid=(chunks,), in_specs=[rows...  11.5 us
  transfers between devices with their start and end apart: 41, of which 19 were waited for; matrix products, arithmetic and copies ran while one was open for 29% of the time, Pallas kernels for 25%

profile of v6, /device:TPU:0, one launch (start us, length us, event | category | flops | bytes accessed | tf_op | source)
XLA Modules:
  0.0 412.4 jit_solution(5959456912846329006)
XLA Ops:
  9.9 5.1 %collective-permute-start.4 = (bf16[32,2432]{1,0:T(8,128)(2,1)S(1)}, bf16[32,2432]{1,0:T(8,128)(2,1)S(1)}, u32[]{:S(2)}, u32[]{:S(2)}) collective-permute-start(bf16[32,2432]{1,0:T(8,128)(2,1)S(1)} %pad_maximum_fusion.12), channel_id=1, source_target_pairs={{0,3},{1,2},{2,1},{3,0},{4,7},{5,6},{6,5},{7,4},{8,11},{9,10},{10,... | collective-permute-start | bytes 466952 | tf_op jit(solution)/shard_map/ppermute | solution.py:525
  17.4 2.5 collective-permute-done.4
  19.9 8.2 %collective-permute-done.3 = bf16[32,2432]{1,0:T(8,128)(2,1)S(1)} collective-permute-done((bf16[32,2432]{1,0:T(8,128)(2,1)S(1)}, bf16[32,2432]{1,0:T(8,128)(2,1)S(1)}, u32[]{:S(2)}, u32[]{:S(2)}) %collective-permute-start.3) | collective-permute-done | bytes 155680 | tf_op jit(solution)/shard_map/ppermute | solution.py:525
  32.0 4.6 %collective-permute-done.5 = bf16[64,2432]{1,0:T(8,128)(2,1)S(1)} collective-permute-done((bf16[64,2432]{1,0:T(8,128)(2,1)S(1)}, bf16[64,2432]{1,0:T(8,128)(2,1)S(1)}, u32[]{:S(2)}, u32[]{:S(2)}) %collective-permute-start.5) | collective-permute-done | bytes 311328 | tf_op jit(solution)/shard_map/ppermute | solution.py:525
  49.9 12.9 %collective-permute-done.7 = bf16[128,2432]{1,0:T(8,128)(2,1)S(1)} collective-permute-done((bf16[128,2432]{1,0:T(8,128)(2,1)S(1)}, bf16[128,2432]{1,0:T(8,128)(2,1)S(1)}, u32[]{:S(2)}, u32[]{:S(2)}) %collective-permute-start.7) | collective-permute-done | bytes 622624 | tf_op jit(solution)/shard_map/ppermute | solution.py:525
  70.2 5.1 %place_rows.1 = bf16[1024,2432]{1,0:T(8,128)(2,1)} custom-call(s32[3]{0:T(128)} %pad_add_fusion.place_ref, bf16[256,2432]{1,0:T(8,128)(2,1)} %copy-done.3, bf16[256,2432]{1,0:T(8,128)(2,1)} %constant_dynamic-update-slice_fusion.refs_1_, bf16[256,2432]{1,0:T(8,128)(2,1)} %collective-permute-done.8.refs_2_, bf16[256,2432]{1,0:T(8,128)(2,1)} %collective-permute-done.9.refs_3_), custom_call_target="tpu_custom_call" | custom-call | bytes 9961472 | tf_op jit(solution)/shard_map/place_rows/pallas_call | solution.py:558
  78.3 10.9 %convolution_convert_fusion.x_ref.raw_ref.halo_ref = bf16[1040,2432]{1,0:T(8,128)(2,1)} fusion(bf16[1024,2432]{1,0:T(8,128)(2,1)} %place_rows.1, f32[1024]{0:T(1024)S(1)} %reshape.210, f32[1040]{0:T(1024)S(1)} %add_rsqrt_fusion, bf16[8,1024]{1,0:T(8,128)(2,1)S(1)} %collective-permute-done, bf16[1024,1024]{1,0:T(8,128)(2,1)S(1)} %bitcast.91, ...), kind=kOutput, calls=%fused_computation | convolution fusion | flops 5192079360 | bytes 12163168 | tf_op jit(solution)/shard_map/dot_general | solution.py:794
  89.1 17.8 %conv_states.1 = (bf16[1024,2304]{1,0:T(8,128)(2,1)}, bf16[1024,2048]{1,0:T(8,128)(2,1)}, f32[1024,128]{1,0:T(8,128)}, f32[1024,128]{1,0:T(8,128)}, f32[1024,32]...) custom-call(bf16[1040,2432]{1,0:T(8,128)(2,1)} %convolution_convert_fusion.x_ref.raw_ref.halo_ref, ...), custom_call_target="tpu_custom_call" | custom-call | flops 1000000000 | bytes 30000000 | tf_op jit(solution)/shard_map/conv_states/pallas_call | solution.py:799
  114.0 11.5 %intra.1.y_ref = f32[1024,2048]{1,0:T(8,128)} custom-call(f32[1024,128]{1,0:T(8,128)} %get-tuple-element.92.q_ref, f32[1024,128]{1,0:T(8,128)} %get-tuple-element.93.k_ref, bf16[1024,2048]{1,0:T(8,128)(2,1)} %get-tuple-element.94.v_ref, f32[1024,32]{1,0:T(8,128)} %get-tuple-element.95.rc_ref, f32[256,128]{1,0:T(8,128)} %get-tuple-element.96.rs_ref, ...), custom_call_target="tpu_custom_call" | custom-call | flops 1000000000 | bytes 30000000 | tf_op jit(solution)/shard_map/intra/pallas_call | solution.py:826
  128.9 7.1 %unpack_weights.1 = (bf16[1024,2048]{1,0:T(8,128)(2,1)}, bf16[2048,1024]{1,0:T(8,128)(2,1)}) custom-call(bf16[1024,4096]{1,0:T(8,128)(2,1)} %all-gather.2.cloned.1.call-done.src), custom_call_target="tpu_custom_call" | custom-call | bytes 16777216 | tf_op jit(solution)/shard_map/unpack_weights/pallas_call | solution.py:619
  136.0 8.6 %convolution_convert_fusion.4.gate_ref = bf16[1024,2048]{1,0:T(8,128)(2,1)} fusion(bf16[1024,2048]{1,0:T(8,128)(2,1)} %get-tuple-element.100, f32[1024]{0:T(1024)S(1)} %reshape.210, f32[1024]{0:T(1024)S(1)} %add_rsqrt_fusion.1, bf16[1,1024,1024]{2,1,0:T(8,128)(2,1)S(1)} %copy-done), kind=kOutput, calls=%fused_computation.25 | convolution fusion | flops 4301258752 | bytes 10493952 | tf_op jit(solution)/shard_map/dot_general | solution.py:841
  144.7 6.8 %convolution_bitcast_fusion.dn_ref = f32[1024,2048]{1,0:T(8,128)} fusion(bf16[2048,1024]{1,0:T(8,128)(2,1)S(1)} %copy-done.29, bf16[1,1024,1024]{2,1,0:T(8,128)(2,1)S(1)} %copy-done.11), kind=kOutput, calls=%fused_computation.11 | convolution fusion | flops 4294967296 | bytes 14680064 | tf_op jit(solution)/shard_map/dot_general | solution.py:842
  156.7 28.4 %gate_norm.1 = (bf16[1024,2048]{1,0:T(8,128)(2,1)}, bf16[1024,2048]{1,0:T(8,128)(2,1)}, bf16[1024,2048]{1,0:T(8,128)(2,1)}, bf16[1024,2048]{1,0:T(8,128)(2,1)}, ...) custom-call(f32[1024,2048]{1,0:T(8,128)} %intra.1.y_ref, ...), custom_call_target="tpu_custom_call" | custom-call | flops 1000000000 | bytes 50000000 | tf_op jit(solution)/shard_map/gate_norm/pallas_call | solution.py:846
  186.4 8.8 %convolution_convert_fusion.3.refs_0_ = bf16[1024,2048]{1,0:T(8,128)(2,1)} fusion(bf16[1024,2048]{1,0:T(8,128)(2,1)} %get-tuple-element.106, f32[1024]{0:T(1024)S(1)} %reshape.210, f32[1024]{0:T(1024)S(1)} %add_rsqrt_fusion.1, bf16[1,1024,1024]{2,1,0:T(8,128)(2,1)S(1)} %copy-done), kind=kOutput, calls=%fused_computation.24 | convolution fusion | flops 4301258752 | bytes 10493952 | tf_op jit(solution)/shard_map/dot_general | solution.py:877
  196.0 6.7 %convolution_convert_fusion.2.refs_1_ = bf16[2048,1024]{1,0:T(8,128)(2,1)} fusion(bf16[1024,2048]{1,0:T(8,128)(2,1)S(1)} %copy-done.31, bf16[1,1024,1024]{2,1,0:T(8,128)(2,1)S(1)} %copy-done.12), kind=kOutput, calls=%fused_computation.23 | convolution fusion | flops 4297064448 | bytes 10485760 | tf_op jit(solution)/shard_map/dot_general | solution.py:879
  204.5 7.3 %pick_rows.2 = (bf16[128,4096]{1,0:T(8,128)(2,1)}, bf16[128,4096]{1,0:T(8,128)(2,1)}, bf16[128,4096]{1,0:T(8,128)(2,1)}, bf16[128,4096]{1,0:T(8,128)(2,1)}, bf16[512,4096]{1,0:T(8,128)(2,1)}) custom-call(s32[3]{0:T(128)} %pad_add_fusion.place_ref, bf16[1024,2048]{1,0:T(8,128)(2,1)} %convolution_convert_fusion.3.refs_0_, ...), custom_call_target="tpu_custom_call" | custom-call | bytes 16777216 | tf_op jit(solution)/shard_map/pick_rows/pallas_call | solution.py:592
  212.8 9.6 %fusion.14 = bf16[1024,1024]{1,0:T(8,128)(2,1)} fusion(bf16[1024,2048]{1,0:T(8,128)(2,1)} %get-tuple-element.114, bf16[2048,1024]{1,0:T(8,128)(2,1)} %get-tuple-element.101, bf16[1,1024,1024]{2,1,0:T(8,128)(2,1)S(1)} %copy-done), kind=kOutput, calls=%fused_computation.22 | convolution fusion | flops 4298113024 | bytes 12582912 | tf_op jit(solution)/shard_map/dot_general | solution.py:884
  222.4 5.4 %add_convert_fusion = (bf16[128,4096]{1,0:T(8,128)(2,1)}, bf16[128,4096]{1,0:T(8,128)(2,1)}, bf16[128,4096]{1,0:T(8,128)(2,1)}, bf16[128,4096]{1,0:T(8,128)(2,1)}) fusion(bf16[128,4096]{1,0:T(8,128)(2,1)S(1)} %copy-done.21, bf16[512,4096]{1,0:T(8,128)(2,1)} %collective-permute-done.17, bf16[128,4096]{1,0:T(8,128)(2,1)S(1)} %copy-done.22, ...), kind=kLoop, calls=%fused_computation.31 | loop fusion | flops 8388608 | bytes 12582912 | tf_op jit(solution)/shard_map/convert_element_type | solution.py:664
  229.6 6.1 %fusion.49 = f32[1024,1024]{1,0:T(8,128)} fusion(bf16[1024,2048]{1,0:T(8,128)(2,1)S(1)} %copy-done.30, bf16[1024,2048]{1,0:T(8,128)(2,1)S(1)} %copy-done.28), kind=kOutput, calls=%fused_computation.171 | convolution fusion | flops 4294967296 | bytes 12582912 | tf_op jit(solution)/shard_map/dot_general | solution.py:948
  237.1 26.5 %intra_back.1 = (bf16[1024,2048]{1,0:T(8,128)(2,1)}, f32[1024,32]{1,0:T(8,128)}, f32[1024,128]{1,0:T(8,128)}, f32[1024,128]{1,0:T(8,128)}) custom-call(f32[1024,128]{1,0:T(8,128)} %get-tuple-element.92.q_ref, f32[1024,128]{1,0:T(8,128)} %get-tuple-element.93.k_ref, bf16[1024,2048]{1,0:T(8,128)(2,1)} %get-tuple-element.94.v_ref, ...), custom_call_target="tpu_custom_call" | custom-call | flops 2000000000 | bytes 40000000 | tf_op jit(solution)/shard_map/intra_back/pallas_call | solution.py:889
  272.1 35.2 %states_conv_back.1 = (bf16[1024,2432]{1,0:T(8,128)(2,1)}, f32[8,2304]{1,0:T(8,128)}, f32[40,2304]{1,0:T(8,128)}, f32[16,32]{1,0:T(8,128)}) custom-call(bf16[1040,2432]{1,0:T(8,128)(2,1)} %convolution_convert_fusion.x_ref.raw_ref.halo_ref, bf16[1040,2432]{1,0:T(8,128)(2,1)} %convolution_convert_fusion.x_ref.raw_ref.halo_ref, ...), custom_call_target="tpu_custom_call" | custom-call | flops 2000000000 | bytes 60000000 | tf_op jit(solution)/shard_map/states_conv_back/pallas_call | solution.py:910
  314.2 10.1 %convolution_convert_fusion.1.refs_0_ = bf16[1024,2432]{1,0:T(8,128)(2,1)} fusion(bf16[1024,2432]{1,0:T(8,128)(2,1)} %fusion.29, f32[1024]{0:T(1024)S(1)} %reshape.210, f32[1024]{0:T(1024)S(1)} %add_rsqrt_fusion.1, bf16[1,1024,1024]{2,1,0:T(8,128)(2,1)S(1)} %copy-done), kind=kOutput, calls=%fused_computation.8 | convolution fusion | flops 5106958336 | bytes 12066816 | tf_op jit(solution)/shard_map/dot_general | solution.py:945
  324.3 5.1 %pick_rows.3 = (bf16[128,2432]{1,0:T(8,128)(2,1)}, bf16[128,2432]{1,0:T(8,128)(2,1)}, bf16[128,2432]{1,0:T(8,128)(2,1)}, bf16[128,2432]{1,0:T(8,128)(2,1)}, bf16[512,2432]{1,0:T(8,128)(2,1)}) custom-call(s32[3]{0:T(128)} %pad_add_fusion.place_ref, bf16[1024,2432]{1,0:T(8,128)(2,1)} %convolution_convert_fusion.1.refs_0_), custom_call_target="tpu_custom_call" | custom-call | bytes 9961472 | tf_op jit(solution)/shard_map/pick_rows/pallas_call | solution.py:592
  329.3 2.4 collective-permute-start.24
  338.5 9.6 %convolution_add_fusion = f32[1024,1024]{1,0:T(8,128)S(1)} fusion(f32[1024,1024]{1,0:T(8,128)} %fusion.49, bf16[1024,2432]{1,0:T(8,128)(2,1)} %fusion.29, bf16[1024,2432]{1,0:T(8,128)(2,1)} %place_rows.1), kind=kOutput, calls=%fused_computation.35 | convolution fusion | flops 5101322240 | bytes 18350080 | tf_op jit(solution)/shard_map/dot_general | solution.py:949
  353.4 2.7 add_convert_fusion.4
  360.5 2.7 fusion.11
  365.3 6.2 %collective-permute-done.26 = bf16[128,2432]{1,0:T(8,128)(2,1)S(1)} collective-permute-done((bf16[128,2432]{1,0:T(8,128)(2,1)S(1)}, bf16[128,2432]{1,0:T(8,128)(2,1)S(1)}, u32[]{:S(2)}, u32[]{:S(2)}) %collective-permute-start.26) | collective-permute-done | bytes 622624 | tf_op jit(solution)/shard_map/ppermute | solution.py:525
  376.4 7.8 %collective-permute-done.33 = bf16[64,2432]{1,0:T(8,128)(2,1)S(1)} collective-permute-done((bf16[64,2432]{1,0:T(8,128)(2,1)S(1)}, bf16[64,2432]{1,0:T(8,128)(2,1)S(1)}, u32[]{:S(2)}, u32[]{:S(2)}) %collective-permute-start.33) | collective-permute-done | bytes 311328 | tf_op jit(solution)/shard_map/ppermute | solution.py:525
  385.5 3.5 collective-permute-done.38
  391.5 2.5 collective-permute-start.36
  397.8 6.6 %collective-permute-done.36 = bf16[32,2432]{1,0:T(8,128)(2,1)S(1)} collective-permute-done((bf16[32,2432]{1,0:T(8,128)(2,1)S(1)}, bf16[32,2432]{1,0:T(8,128)(2,1)S(1)}, u32[]{:S(2)}, u32[]{:S(2)}) %collective-permute-start.36) | collective-permute-done | bytes 155680 | tf_op jit(solution)/shard_map/ppermute | solution.py:525
  (263 shorter events, 103.2 us)
Async XLA Ops:
  7.2 121.7 %all-gather.2.cloned.1.call-start = ((), (), s32[]{:S(2)}) async-start(), calls=%async_computation | async-start | bytes 8650752 | tf_op jit(solution)/shard_map/all_gather | solution.py:753
  9.9 10.0 %collective-permute-start.4 = (bf16[32,2432]{1,0:T(8,128)(2,1)S(1)}, bf16[32,2432]{1,0:T(8,128)(2,1)S(1)}, u32[]{:S(2)}, u32[]{:S(2)}) collective-permute-start(bf16[32,2432]{1,0:T(8,128)(2,1)S(1)} %pad_maximum_fusion.12), channel_id=1, source_target_pairs={{0,3},{1,2},{2,1},{3,0},{4,7},{5,6},{6,5},{7,4},{8,11},{9,10},{10,... | collective-permute-start | bytes 466952 | tf_op jit(solution)/shard_map/ppermute | solution.py:525
  14.9 13.2 %collective-permute-start.3 = (bf16[32,2432]{1,0:T(8,128)(2,1)S(1)}, bf16[32,2432]{1,0:T(8,128)(2,1)S(1)}, u32[]{:S(2)}, u32[]{:S(2)}) collective-permute-start(bf16[32,2432]{1,0:T(8,128)(2,1)S(1)} %pad_maximum_fusion.12), channel_id=1, source_target_pairs={{0,2},{1,3},{2,0},{3,1},{4,6},{5,7},{6,4},{7,5},{8,10},{9,11},{10,... | collective-permute-start | bytes 466952 | tf_op jit(solution)/shard_map/ppermute | solution.py:525
  14.9 14.8 %collective-permute-start.1 = (bf16[32,2432]{1,0:T(8,128)(2,1)S(1)}, bf16[32,2432]{1,0:T(8,128)(2,1)S(1)}, u32[]{:S(2)}, u32[]{:S(2)}) collective-permute-start(bf16[32,2432]{1,0:T(8,128)(2,1)S(1)} %pad_maximum_fusion.12), channel_id=1, source_target_pairs={{0,1},{1,0},{2,3},{3,2},{4,5},{5,4},{6,7},{7,6},{8,9},{9,8},{10,11... | collective-permute-start | bytes 466952 | tf_op jit(solution)/shard_map/ppermute | solution.py:525
  28.1 8.5 %collective-permute-start.5 = (bf16[64,2432]{1,0:T(8,128)(2,1)S(1)}, bf16[64,2432]{1,0:T(8,128)(2,1)S(1)}, u32[]{:S(2)}, u32[]{:S(2)}) collective-permute-start(bf16[64,2432]{1,0:T(8,128)(2,1)S(1)} %pad_maximum_fusion.7), channel_id=1, source_target_pairs={{0,16},{8,24},{16,0},{24,8},{1,17},{9,25},{17,1},{25,9},{2,18},{10... | collective-permute-start | bytes 933896 | tf_op jit(solution)/shard_map/ppermute | solution.py:525
  29.8 8.2 %collective-permute-start.2 = (bf16[64,2432]{1,0:T(8,128)(2,1)S(1)}, bf16[64,2432]{1,0:T(8,128)(2,1)S(1)}, u32[]{:S(2)}, u32[]{:S(2)}) collective-permute-start(bf16[64,2432]{1,0:T(8,128)(2,1)S(1)} %pad_maximum_fusion.6), channel_id=1, source_target_pairs={{0,8},{8,0},{16,24},{24,16},{1,9},{9,1},{17,25},{25,17},{2,10},{10... | collective-permute-start | bytes 933896 | tf_op jit(solution)/shard_map/ppermute | solution.py:525
  38.9 30.5 %collective-permute-start = (bf16[8,1024]{1,0:T(8,128)(2,1)S(1)}, bf16[8,1024]{1,0:T(8,128)(2,1)S(1)}, u32[]{:S(2)}, u32[]{:S(2)}) collective-permute-start(bf16[8,1024]{1,0:T(8,128)(2,1)S(1)} %slice_bitcast_fusion), channel_id=1, source_target_pairs={{0,4},{4,8},{8,12},{12,16},{16,20},{20,24},{24,28},{1,5},{5,9},{9,... | collective-permute-start | bytes 49160 | tf_op jit(solution)/shard_map/ppermute | solution.py:520
  46.3 16.4 %collective-permute-start.7 = (bf16[128,2432]{1,0:T(8,128)(2,1)S(1)}, bf16[128,2432]{1,0:T(8,128)(2,1)S(1)}, u32[]{:S(2)}, u32[]{:S(2)}) collective-permute-start(bf16[128,2432]{1,0:T(8,128)(2,1)S(1)} %pad_maximum_fusion.2), channel_id=1, source_target_pairs={{0,8},{8,0},{16,24},{24,16},{1,9},{9,1},{17,25},{25,17},{2,10},{10... | collective-permute-start | bytes 1867784 | tf_op jit(solution)/shard_map/ppermute | solution.py:525
  48.6 16.3 %collective-permute-start.6 = (bf16[128,2432]{1,0:T(8,128)(2,1)S(1)}, bf16[128,2432]{1,0:T(8,128)(2,1)S(1)}, u32[]{:S(2)}, u32[]{:S(2)}) collective-permute-start(bf16[128,2432]{1,0:T(8,128)(2,1)S(1)} %pad_maximum_fusion.1), channel_id=1, source_target_pairs={{0,16},{8,24},{16,0},{24,8},{1,17},{9,25},{17,1},{25,9},{2,18},{10... | collective-permute-start | bytes 1867784 | tf_op jit(solution)/shard_map/ppermute | solution.py:525
  111.9 14.8 %collective-permute-start.11 = (f32[130,1024]{1,0:T(8,128)S(1)}, f32[130,1024]{1,0:T(8,128)S(1)}, u32[]{:S(2)}, u32[]{:S(2)}) collective-permute-start(f32[130,1024]{1,0:T(8,128)S(1)} %pad_maximum_fusion.4), channel_id=1, source_target_pairs={{0,8},{8,0},{16,24},{24,16},{1,9},{9,1},{17,25},{25,17},{2,10},{10... | collective-permute-start | bytes 1597448 | tf_op jit(solution)/shard_map/ppermute | solution.py:525
  127.5 24.0 %collective-permute-start.12 = (f32[130,1024]{1,0:T(8,128)S(1)}, f32[130,1024]{1,0:T(8,128)}, u32[]{:S(2)}, u32[]{:S(2)}) collective-permute-start(f32[130,1024]{1,0:T(8,128)S(1)} %pad_maximum_fusion.5), channel_id=1, source_target_pairs={{0,16},{8,24},{16,0},{24,8},{1,17},{9,25},{17,1},{25,9},{2,18},{10... | collective-permute-start | bytes 1597448 | tf_op jit(solution)/shard_map/ppermute | solution.py:525
  186.2 9.0 %collective-permute-start.14 = (bf16[130,1024]{1,0:T(8,128)(2,1)S(1)}, bf16[130,1024]{1,0:T(8,128)(2,1)S(1)}, u32[]{:S(2)}, u32[]{:S(2)}) collective-permute-start(bf16[130,1024]{1,0:T(8,128)(2,1)S(1)} %broadcast_select_fusion.1), channel_id=1, source_target_pairs={{0,4},{4,0},{1,5},{5,1},{2,6},{6,2},{3,7},{7,3},{8,12},{12,8},{9,1... | collective-permute-start | bytes 798728 | tf_op jit(solution)/shard_map/ppermute | solution.py:525
  195.4 9.0 %collective-permute-start.15 = (bf16[130,1024]{1,0:T(8,128)(2,1)S(1)}, bf16[130,1024]{1,0:T(8,128)(2,1)S(1)}, u32[]{:S(2)}, u32[]{:S(2)}) collective-permute-start(bf16[130,1024]{1,0:T(8,128)(2,1)S(1)} %pad_maximum_fusion.8), channel_id=1, source_target_pairs={{0,8},{8,0},{16,24},{24,16},{1,9},{9,1},{17,25},{25,17},{2,10},{10... | collective-permute-start | bytes 798728 | tf_op jit(solution)/shard_map/ppermute | solution.py:525
  211.7 10.6 %collective-permute-start.17 = (bf16[512,4096]{1,0:T(8,128)(2,1)}, bf16[512,4096]{1,0:T(8,128)(2,1)}, u32[]{:S(2)}, u32[]{:S(2)}) collective-permute-start(bf16[512,4096]{1,0:T(8,128)(2,1)} %get-tuple-element.113), channel_id=1, source_target_pairs={{0,4},{4,0},{1,5},{5,1},{2,6},{6,2},{3,7},{7,3},{8,12},{12,8},{9,1... | collective-permute-start | bytes 12582920 | tf_op jit(solution)/shard_map/ppermute | solution.py:525
  212.1 23.7 %collective-permute-start.16 = (bf16[130,1024]{1,0:T(8,128)(2,1)S(1)}, bf16[130,1024]{1,0:T(8,128)(2,1)S(1)}, u32[]{:S(2)}, u32[]{:S(2)}) collective-permute-start(bf16[130,1024]{1,0:T(8,128)(2,1)S(1)} %pad_maximum_fusion.9), channel_id=1, source_target_pairs={{0,16},{8,24},{16,0},{24,8},{1,17},{9,25},{17,1},{25,9},{2,18},{10... | collective-permute-start | bytes 798728 | tf_op jit(solution)/shard_map/ppermute | solution.py:525
  227.8 35.8 %collective-permute-start.19 = (bf16[128,4096]{1,0:T(8,128)(2,1)}, bf16[128,4096]{1,0:T(8,128)(2,1)}, u32[]{:S(2)}, u32[]{:S(2)}) collective-permute-start(bf16[128,4096]{1,0:T(8,128)(2,1)} %get-tuple-element.184), channel_id=1, source_target_pairs={{0,8},{8,0},{16,24},{24,16},{1,9},{9,1},{17,25},{25,17},{2,10},{10... | collective-permute-start | bytes 3145736 | tf_op jit(solution)/shard_map/ppermute | solution.py:525
  228.8 34.8 %collective-permute-start.18 = (bf16[128,4096]{1,0:T(8,128)(2,1)}, bf16[128,4096]{1,0:T(8,128)(2,1)}, u32[]{:S(2)}, u32[]{:S(2)}) collective-permute-start(bf16[128,4096]{1,0:T(8,128)(2,1)} %get-tuple-element.185), channel_id=1, source_target_pairs={{0,16},{8,24},{16,0},{24,8},{1,17},{9,25},{17,1},{25,9},{2,18},{10... | collective-permute-start | bytes 3145736 | tf_op jit(solution)/shard_map/ppermute | solution.py:525
  236.8 26.8 %collective-permute-start.22 = (bf16[128,1024]{1,0:T(8,128)(2,1)S(1)}, bf16[128,1024]{1,0:T(8,128)(2,1)}, u32[]{:S(2)}, u32[]{:S(2)}) collective-permute-start(bf16[128,1024]{1,0:T(8,128)(2,1)S(1)} %get-tuple-element.196), channel_id=1, source_target_pairs={{0,4},{4,0},{1,5},{5,1},{2,6},{6,2},{3,7},{7,3},{8,12},{12,8},{9,1... | collective-permute-start | bytes 786440 | tf_op jit(solution)/shard_map/ppermute | solution.py:525
  266.7 42.7 %collective-permute-start.21 = (bf16[64,4096]{1,0:T(8,128)(2,1)}, bf16[64,4096]{1,0:T(8,128)(2,1)}, u32[]{:S(2)}, u32[]{:S(2)}) collective-permute-start(bf16[64,4096]{1,0:T(8,128)(2,1)} %add_convert_fusion.11), channel_id=1, source_target_pairs={{0,16},{8,24},{16,0},{24,8},{1,17},{9,25},{17,1},{25,9},{2,18},{10... | collective-permute-start | bytes 1572872 | tf_op jit(solution)/shard_map/ppermute | solution.py:525
  269.9 39.5 %collective-permute-start.20 = (bf16[64,4096]{1,0:T(8,128)(2,1)}, bf16[64,4096]{1,0:T(8,128)(2,1)}, u32[]{:S(2)}, u32[]{:S(2)}) collective-permute-start(bf16[64,4096]{1,0:T(8,128)(2,1)} %add_convert_fusion.12), channel_id=1, source_target_pairs={{0,8},{8,0},{16,24},{24,16},{1,9},{9,1},{17,25},{25,17},{2,10},{10... | collective-permute-start | bytes 1572872 | tf_op jit(solution)/shard_map/ppermute | solution.py:525
  329.3 18.9 %collective-permute-start.24 = (bf16[512,2432]{1,0:T(8,128)(2,1)}, bf16[512,2432]{1,0:T(8,128)(2,1)S(1)}, u32[]{:S(2)}, u32[]{:S(2)}) collective-permute-start(bf16[512,2432]{1,0:T(8,128)(2,1)} %get-tuple-element.145), channel_id=1, source_target_pairs={{0,4},{4,0},{1,5},{5,1},{2,6},{6,2},{3,7},{7,3},{8,12},{12,8},{9,1... | collective-permute-start | bytes 7471112 | tf_op jit(solution)/shard_map/ppermute | solution.py:525
  333.9 24.6 %collective-permute-start.29 = (bf16[32,4096]{1,0:T(8,128)(2,1)}, bf16[32,4096]{1,0:T(8,128)(2,1)}, u32[]{:S(2)}, u32[]{:S(2)}) collective-permute-start(bf16[32,4096]{1,0:T(8,128)(2,1)} %slice.615), channel_id=1, source_target_pairs={{0,1},{1,0},{2,3},{3,2},{4,5},{5,4},{6,7},{7,6},{8,9},{9,8},{10,11... | collective-permute-start | bytes 786440 | tf_op jit(solution)/shard_map/ppermute | solution.py:525
  335.6 27.6 %collective-permute-start.31 = (bf16[32,4096]{1,0:T(8,128)(2,1)}, bf16[32,4096]{1,0:T(8,128)(2,1)}, u32[]{:S(2)}, u32[]{:S(2)}) collective-permute-start(bf16[32,4096]{1,0:T(8,128)(2,1)} %get-tuple-element.201), channel_id=1, source_target_pairs={{0,3},{1,2},{2,1},{3,0},{4,7},{5,6},{6,5},{7,4},{8,11},{9,10},{10,... | collective-permute-start | bytes 786440 | tf_op jit(solution)/shard_map/ppermute | solution.py:525
  337.9 26.6 %collective-permute-start.30 = (bf16[32,4096]{1,0:T(8,128)(2,1)}, bf16[32,4096]{1,0:T(8,128)(2,1)}, u32[]{:S(2)}, u32[]{:S(2)}) collective-permute-start(bf16[32,4096]{1,0:T(8,128)(2,1)} %get-tuple-element.202), channel_id=1, source_target_pairs={{0,2},{1,3},{2,0},{3,1},{4,6},{5,7},{6,4},{7,5},{8,10},{9,11},{10,... | collective-permute-start | bytes 786440 | tf_op jit(solution)/shard_map/ppermute | solution.py:525
  356.1 15.3 %collective-permute-start.26 = (bf16[128,2432]{1,0:T(8,128)(2,1)S(1)}, bf16[128,2432]{1,0:T(8,128)(2,1)S(1)}, u32[]{:S(2)}, u32[]{:S(2)}) collective-permute-start(bf16[128,2432]{1,0:T(8,128)(2,1)S(1)} %get-tuple-element.189), channel_id=1, source_target_pairs={{0,8},{8,0},{16,24},{24,16},{1,9},{9,1},{17,25},{25,17},{2,10},{10... | collective-permute-start | bytes 1867784 | tf_op jit(solution)/shard_map/ppermute | solution.py:525
  358.0 14.9 %collective-permute-start.25 = (bf16[128,2432]{1,0:T(8,128)(2,1)S(1)}, bf16[128,2432]{1,0:T(8,128)(2,1)S(1)}, u32[]{:S(2)}, u32[]{:S(2)}) collective-permute-start(bf16[128,2432]{1,0:T(8,128)(2,1)S(1)} %get-tuple-element.190), channel_id=1, source_target_pairs={{0,16},{8,24},{16,0},{24,8},{1,17},{9,25},{17,1},{25,9},{2,18},{10... | collective-permute-start | bytes 1867784 | tf_op jit(solution)/shard_map/ppermute | solution.py:525
  358.5 6.8 %collective-permute-start.28 = (f32[32,552]{1,0:T(8,128)S(1)}, f32[32,552]{1,0:T(8,128)S(1)}, u32[]{:S(2)}, u32[]{:S(2)}) collective-permute-start(f32[32,552]{1,0:T(8,128)S(1)} %fusion.62), channel_id=1, source_target_pairs={{0,2},{1,3},{2,0},{3,1},{4,6},{5,7},{6,4},{7,5},{8,10},{9,11},{10,... | collective-permute-start | bytes 211976 | tf_op jit(solution)/shard_map/ppermute | solution.py:525
  374.4 9.8 %collective-permute-start.33 = (bf16[64,2432]{1,0:T(8,128)(2,1)S(1)}, bf16[64,2432]{1,0:T(8,128)(2,1)S(1)}, u32[]{:S(2)}, u32[]{:S(2)}) collective-permute-start(bf16[64,2432]{1,0:T(8,128)(2,1)S(1)} %add_convert_fusion.15), channel_id=1, source_target_pairs={{0,16},{8,24},{16,0},{24,8},{1,17},{9,25},{17,1},{25,9},{2,18},{10... | collective-permute-start | bytes 933896 | tf_op jit(solution)/shard_map/ppermute | solution.py:525
  374.8 9.5 %collective-permute-start.32 = (bf16[64,2432]{1,0:T(8,128)(2,1)S(1)}, bf16[64,2432]{1,0:T(8,128)(2,1)S(1)}, u32[]{:S(2)}, u32[]{:S(2)}) collective-permute-start(bf16[64,2432]{1,0:T(8,128)(2,1)S(1)} %add_convert_fusion.16), channel_id=1, source_target_pairs={{0,8},{8,0},{16,24},{24,16},{1,9},{9,1},{17,25},{25,17},{2,10},{10... | collective-permute-start | bytes 933896 | tf_op jit(solution)/shard_map/ppermute | solution.py:525
  390.9 6.9 %collective-permute-start.35 = (bf16[32,2432]{1,0:T(8,128)(2,1)S(1)}, bf16[32,2432]{1,0:T(8,128)(2,1)S(1)}, u32[]{:S(2)}, u32[]{:S(2)}) collective-permute-start(bf16[32,2432]{1,0:T(8,128)(2,1)S(1)} %slice.616), channel_id=1, source_target_pairs={{0,1},{1,0},{2,3},{3,2},{4,5},{5,4},{6,7},{7,6},{8,9},{9,8},{10,11... | collective-permute-start | bytes 466952 | tf_op jit(solution)/shard_map/ppermute | solution.py:525
  391.5 12.9 %collective-permute-start.36 = (bf16[32,2432]{1,0:T(8,128)(2,1)S(1)}, bf16[32,2432]{1,0:T(8,128)(2,1)S(1)}, u32[]{:S(2)}, u32[]{:S(2)}) collective-permute-start(bf16[32,2432]{1,0:T(8,128)(2,1)S(1)} %get-tuple-element.203), channel_id=1, source_target_pairs={{0,2},{1,3},{2,0},{3,1},{4,6},{5,7},{6,4},{7,5},{8,10},{9,11},{10,... | collective-permute-start | bytes 466952 | tf_op jit(solution)/shard_map/ppermute | solution.py:525
  394.1 10.4 %collective-permute-start.37 = (bf16[32,2432]{1,0:T(8,128)(2,1)S(1)}, bf16[32,2432]{1,0:T(8,128)(2,1)S(1)}, u32[]{:S(2)}, u32[]{:S(2)}) collective-permute-start(bf16[32,2432]{1,0:T(8,128)(2,1)S(1)} %get-tuple-element.204), channel_id=1, source_target_pairs={{0,3},{1,2},{2,1},{3,0},{4,7},{5,6},{6,5},{7,4},{8,11},{9,10},{10,... | collective-permute-start | bytes 466952 | tf_op jit(solution)/shard_map/ppermute | solution.py:525
  (41 other events, 437.2 us)
Sparse Core Ops, SparseCore 0:
  38.1 77.9 all-gather.1
